TPU v7x, 32 devices: a whole 2x2x4 slice. The times are simulated.
32 devices in a mesh: groups: 2 (over x), row: 16 (over z, y, core).
Axes of the slice: x: 2, y: 2, z: 4, core: 2. Of those that a mesh axis runs over, the one named last changes fastest.
Arguments:
- basis: float32 [8192, 128], P(('groups', 'row')), parts along dimension 0, may hold values from -6 to 6
- springs: float32 [8192], P(('groups', 'row')), parts along dimension 0, may hold values from 0.25 to 8
- tangent_blocks: float32 [4096, 4096], P(('groups', 'row')), parts along dimension 0, may hold values from -0.375 to 0.375
- tile_rows: int32 [4096], P(('groups', 'row')), parts along dimension 0, may hold values from 0 to 3
- tile_owner: int32 [4096, 1], P(('groups', 'row')), parts along dimension 0, may hold values from 0 to 15, as said below
- tile_offset: int32 [4096], P(('groups', 'row')), parts along dimension 0, may hold values from 0 to 3
- tile_count: int32 [32], P(('groups', 'row')), parts along dimension 0, may hold values from 32 to 128, as said below
Outputs:
- stiff_image: float32 [8192, 128], P(('groups', 'row')), parts along dimension 0
- reduced: float32 [256, 128], P('groups'), parts along dimension 0
There are 2 independent parts, one for each index of `groups`. A program takes and returns all parts, laid end to end along the dimension named above; each array names one. Nothing has to cross between parts.
Inputs may be any that keep to these rules, and one draw needn't show every extreme that they name: The first tile_count[d] slots of device d are live; some device has exactly 128. `tile_owner`: the slab is closed into a shell: every slot of device d names owner (d + o) mod 16 with o one of 0, 1, -1, 4, -4, 5, -5, 8. Among the slots of one device no owner appears more than 32 times, and owner d itself appears exactly 32 times in every device.
All inputs are finite; a program needn't handle non-finite values.
Results may differ from a plain program's by a relative error of at most 0.0003.
Values sent between devices are 32-bit elements; how exact they have to be, the bound alone decides.
No kernel may reach another device: no remote copies, remote signals or barrier semaphores. Data moves between devices by JAX's collectives and lax.ppermute only.
A program may use at most 128 MiB of HBM per device.

v0:
```python
import functools

import jax
import jax.numpy as jnp
from jax import lax
from jax.experimental import pallas as pl
from jax.experimental.pallas import tpu as pltpu
from jax.sharding import PartitionSpec as P

B = 64
MODES = 128
BR_DEV = 4
CAP = 128
LINKS = 8
LATE = 3
HALF = B // 2
ROWS = BR_DEV * B


def split(x):
    high = x.astype(jnp.bfloat16)
    return high, (x - high.astype(jnp.float32)).astype(jnp.bfloat16)


def dot3(a_high, a_low, b_high, b_low):
    dot = functools.partial(jnp.dot, preferred_element_type=jnp.float32)
    return dot(a_high, b_high) + (dot(a_low, b_high) + dot(a_high, b_low))


def halves():
    for r in range(BR_DEV):
        for h in range(2):
            yield pl.ds(r * B + h, HALF, stride=2), slice(r * B + h * HALF, r * B + (h + 1) * HALF)


def assemble(place_ref, count_ref, blocks_ref, basis_ref, high_ref, low_ref, turned_high_ref, turned_low_ref, weight_high_ref, weight_low_ref, slots, dense, sorted_basis):
    dense[...] = jnp.zeros_like(dense)
    for rows, target in halves():
        sorted_basis[target, :] = basis_ref[rows, :]
    turned_high, turned_low = split(sorted_basis[...].T)
    turned_high_ref[...] = turned_high
    turned_low_ref[...] = turned_low

    @pl.loop(0, CAP // 8)
    def _(group):
        eight = blocks_ref[pl.ds(pl.multiple_of(group * 8, 8), 8), :]
        for t in range(HALF):
            slots[pl.ds(group * (8 * HALF) + t, 8, stride=HALF), :] = eight[:, t * 128:(t + 1) * 128]

    @pl.loop(0, count_ref[0])
    def _(s):
        target = pl.ds(pl.multiple_of(place_ref[s] * HALF, HALF), HALF)
        dense[target, :] += slots[pl.ds(pl.multiple_of(s * HALF, HALF), HALF), :]

    left = lax.broadcasted_iota(jnp.int32, (HALF, 128), 1) < B

    @pl.loop(0, LINKS)
    def _(link):
        for r in range(BR_DEV):
            for pair in range(BR_DEV // 2):
                start = ((link * BR_DEV + r) * BR_DEV + 2 * pair) * HALF
                first = dense[pl.ds(pl.multiple_of(start, HALF), HALF), :]
                second = dense[pl.ds(pl.multiple_of(start + HALF, HALF), HALF), :]
                even = jnp.where(left, first, pltpu.roll(second, B, 1))
                odd = jnp.where(left, pltpu.roll(first, B, 1), second)
                for h, part in enumerate((even, odd)):
                    high, low = split(part)
                    rows = slice(r * B + h * HALF, r * B + (h + 1) * HALF)
                    high_ref[link, rows, pair * 128:(pair + 1) * 128] = high
                    low_ref[link, rows, pair * 128:(pair + 1) * 128] = low

    for k in range(LATE):
        link = LINKS - LATE + k
        high, low = split(dot3(turned_high, turned_low, high_ref[link], low_ref[link]))
        weight_high_ref[k] = high
        weight_low_ref[k] = low


def project_early(high_ref, low_ref, turned_high_ref, turned_low_ref, springs_ref, own_ref, *refs):
    basis_refs, (total_ref, partial_ref) = refs[:-2], refs[-2:]
    total = jnp.zeros((ROWS, MODES), jnp.float32)
    for link, ref in enumerate((own_ref,) + basis_refs):
        b_high, b_low = split(ref[...])
        total += dot3(high_ref[link], low_ref[link], b_high, b_low)
    for part in range(ROWS // MODES):
        rows = slice(part * MODES, (part + 1) * MODES)
        column = jnp.broadcast_to(springs_ref[:, rows], (MODES, MODES)).T
        total_ref[rows, :] = column * own_ref[rows, :]
    for rows, target in halves():
        total_ref[rows, :] += total[target, :]
    sorted_total = jnp.concatenate([total_ref[rows, :] for rows, _ in halves()], axis=0)
    partial_ref[...] = dot3(turned_high_ref[...], turned_low_ref[...], *split(sorted_total))


def reduce_late(scale, core_ref, weight_high_ref, weight_low_ref, early_ref, *refs):
    basis_refs, (kept_ref, sent_ref, partial) = refs[:LATE], refs[LATE:]
    total = early_ref[...]
    for k, ref in enumerate(basis_refs):
        total += dot3(weight_high_ref[k], weight_low_ref[k], *split(ref[...]))
    partial[...] = total * scale
    half = MODES // 2
    kept_ref[...] = partial[pl.ds(pl.multiple_of(core_ref[0] * half, half), half), :]
    sent_ref[...] = partial[pl.ds(pl.multiple_of((1 - core_ref[0]) * half, half), half), :]


def join(core_ref, mine_ref, other_ref, whole_ref):
    half = MODES // 2
    whole_ref[pl.ds(pl.multiple_of(core_ref[0] * half, half), half), :] = mine_ref[...]
    whole_ref[pl.ds(pl.multiple_of((1 - core_ref[0]) * half, half), half), :] = other_ref[...]


def project_late(high_ref, low_ref, total_ref, *refs):
    basis_refs, stiff_ref = refs[:LATE], refs[LATE]
    total = jnp.zeros((ROWS, MODES), jnp.float32)
    for k, ref in enumerate(basis_refs):
        b_high, b_low = split(ref[...])
        total += dot3(high_ref[LINKS - LATE + k], low_ref[LINKS - LATE + k], b_high, b_low)
    for rows, target in halves():
        stiff_ref[rows, :] = total_ref[rows, :] + total[target, :]


def shards(basis, springs, tangent_blocks, tile_rows, tile_owner, tile_offset, tile_count):
    n = lax.axis_size("row")
    me = lax.axis_index("row")
    steps = (0, 1, n - 1, 4, n - 4, n // 2, 5, n - 5)

    def fetch(block, step):
        return lax.ppermute(block, "row", [((d + step) % n, d) for d in range(n)])

    above, below = fetch(basis, 4), fetch(basis, n - 4)
    across = fetch(basis, n // 2)
    after, before = fetch(basis, 1), fetch(basis, n - 1)
    far_above, far_below = fetch(above, 1), fetch(below, n - 1)

    away = (tile_owner[:, 0] - me + n) % n
    link = jnp.zeros_like(away)
    for k, step in enumerate(steps):
        link = jnp.where(away == step, k, link)
    place = (link * BR_DEV + tile_rows) * BR_DEV + tile_offset

    smem = pl.BlockSpec(memory_space=pltpu.SMEM)
    vmem = pl.BlockSpec(memory_space=pltpu.VMEM)
    half, full = jnp.bfloat16, jnp.float32
    params = pltpu.CompilerParams(vmem_limit_bytes=32 * 2**20)

    high, low, turned_high, turned_low, weight_high, weight_low = pl.pallas_call(
        assemble,
        out_shape=(
            jax.ShapeDtypeStruct((LINKS, ROWS, ROWS), half),
            jax.ShapeDtypeStruct((LINKS, ROWS, ROWS), half),
            jax.ShapeDtypeStruct((MODES, ROWS), half),
            jax.ShapeDtypeStruct((MODES, ROWS), half),
            jax.ShapeDtypeStruct((LATE, MODES, ROWS), half),
            jax.ShapeDtypeStruct((LATE, MODES, ROWS), half),
        ),
        in_specs=[smem, smem, vmem, vmem],
        out_specs=(vmem,) * 6,
        scratch_shapes=[
            pltpu.VMEM((CAP * HALF, 128), full),
            pltpu.VMEM((CAP * HALF, 128), full),
            pltpu.VMEM((ROWS, MODES), full),
        ],
        compiler_params=params,
        cost_estimate=pl.CostEstimate(flops=10_000_000, bytes_accessed=12_000_000, transcendentals=0),
        name="assemble",
    )(place, tile_count, tangent_blocks, basis)

    total, early = pl.pallas_call(
        project_early,
        out_shape=(jax.ShapeDtypeStruct((ROWS, MODES), full), jax.ShapeDtypeStruct((MODES, MODES), full)),
        in_specs=[vmem] * (5 + LINKS - LATE),
        out_specs=(vmem,) * 2,
        compiler_params=params,
        cost_estimate=pl.CostEstimate(flops=300_000_000, bytes_accessed=2_500_000, transcendentals=0),
        name="project_early",
    )(high, low, turned_high, turned_low, springs.reshape(1, ROWS), basis, after, before, above, below)

    core = (me % 2).reshape(1)
    piece = jax.ShapeDtypeStruct((MODES // 2, MODES), full)
    kept, sent = pl.pallas_call(
        functools.partial(reduce_late, 1.0 / (basis.shape[0] * n)),
        out_shape=(piece, piece),
        in_specs=[smem] + [vmem] * (3 + LATE),
        out_specs=(vmem,) * 2,
        scratch_shapes=[pltpu.VMEM((MODES, MODES), full)],
        compiler_params=params,
        cost_estimate=pl.CostEstimate(flops=80_000_000, bytes_accessed=700_000, transcendentals=0),
        name="reduce_late",
    )(core, weight_high, weight_low, early, across, far_above, far_below)

    stiff_image = pl.pallas_call(
        project_late,
        out_shape=jax.ShapeDtypeStruct((ROWS, MODES), full),
        in_specs=[vmem] * (3 + LATE),
        out_specs=vmem,
        compiler_params=params,
        cost_estimate=pl.CostEstimate(flops=160_000_000, bytes_accessed=1_500_000, transcendentals=0),
        name="project_late",
    )(high, low, total, across, far_above, far_below)

    def swap(block, apart):
        return lax.ppermute(block, "row", [(d, d ^ apart) for d in range(n)])

    mine = kept + swap(sent, 1)
    apart = 2
    while apart < n:
        mine += swap(mine, apart)
        apart *= 2
    reduced = pl.pallas_call(
        join,
        out_shape=jax.ShapeDtypeStruct((MODES, MODES), full),
        in_specs=[smem, vmem, vmem],
        out_specs=vmem,
        compiler_params=params,
        cost_estimate=pl.CostEstimate(flops=0, bytes_accessed=130_000, transcendentals=0),
        name="join",
    )(core, mine, swap(mine, 1))
    return (stiff_image, reduced)


def solution(mesh):
    in_specs = (
        P(("groups", "row"), None),
        P(("groups", "row")),
        P(("groups", "row"), None),
        P(("groups", "row")),
        P(("groups", "row"), None),
        P(("groups", "row")),
        P(("groups", "row")),
    )
    out_specs = (P(("groups", "row"), None), P("groups", None))
    return jax.shard_map(shards, mesh=mesh, in_specs=in_specs, out_specs=out_specs, check_vma=False)
```

profile of v0, /device:TPU:0, one launch (start us, length us, event | category | flops | bytes accessed | tf_op | source)
XLA Modules:
  0.0 39.6 jit_solution(2669787571435718504)
XLA Ops:
  0.6 5.1 %collective-permute-start.2 = (f32[256,128]{1,0:T(8,128)}, f32[256,128]{1,0:T(8,128)S(1)}, u32[]{:S(2)}, u32[]{:S(2)}) collective-permute-start(f32[256,128]{1,0:T(8,128)} %own_ref.1), channel_id=1, source_target_pairs={{4,0},{5,1},{6,2},{7,3},{8,4},{9,5},{10,6},{11,7},{12,8},{13,9},{1... | collective-permute-start | bytes 393224 | tf_op jit(solution)/shard_map/ppermute | solution.py:128
  5.7 0.0 collective-permute-start.3
  5.7 3.7 %collective-permute-start = (f32[256,128]{1,0:T(8,128)}, f32[256,128]{1,0:T(8,128)S(1)}, u32[]{:S(2)}, u32[]{:S(2)}) collective-permute-start(f32[256,128]{1,0:T(8,128)} %own_ref.1), channel_id=1, source_target_pairs={{1,0},{2,1},{3,2},{4,3},{5,4},{6,5},{7,6},{8,7},{9,8},{10,9},{11,1... | collective-permute-start | bytes 393224 | tf_op jit(solution)/shard_map/ppermute | solution.py:128
  9.4 0.0 collective-permute-start.1
  9.4 0.0 collective-permute-start.4
  9.4 0.6 %collective-permute-done.2.refs_2_ = f32[256,128]{1,0:T(8,128)S(1)} collective-permute-done((f32[256,128]{1,0:T(8,128)}, f32[256,128]{1,0:T(8,128)S(1)}, u32[]{:S(2)}, u32[]{:S(2)}) %collective-permute-start.2) | collective-permute-done | bytes 131104 | tf_op jit(solution)/shard_map/ppermute | solution.py:128
  10.0 3.9 %collective-permute-start.5 = (f32[256,128]{1,0:T(8,128)S(1)}, f32[256,128]{1,0:T(8,128)S(1)}, u32[]{:S(2)}, u32[]{:S(2)}) collective-permute-start(f32[256,128]{1,0:T(8,128)S(1)} %collective-permute-done.2.refs_2_), channel_id=1, source_target_pairs={{1,0},{2,1},{3,2},{4,3},{5,4},{6,5},{7,6},{8,7},{9,8},{10,9},{11,1... | collective-permute-start | bytes 393224 | tf_op jit(solution)/shard_map/ppermute | solution.py:128
  13.9 0.0 collective-permute-done.3.refs_3_
  13.9 0.0 collective-permute-start.6
  13.9 0.7 %multiply_add_fusion.place_ref = s32[128]{0:T(128)S(1)} fusion(s32[128]{0:T(128)} %param.12, s32[128]{0:T(128)} %param.10, s32[128,1]{0,1:T(1,128)} %param.11, s32[]{:T(128)S(6)} %axis_index.12), kind=kLoop, calls=%fused_computation.13 | loop fusion | flops 3968 | bytes 2052 | tf_op jit(solution)/shard_map/add | solution.py:139
  15.2 0.0 copy-start
  15.2 1.6 %copy-done = f32[128,4096]{1,0:T(8,128)S(1)} copy-done((f32[128,4096]{1,0:T(8,128)S(1)}, f32[128,4096]{1,0:T(8,128)}, u32[]{:S(2)}) %copy-start) | copy-done | bytes 2097176
  16.8 0.9 %copy-done.1 = f32[256,128]{1,0:T(8,128)S(1)} copy-done((f32[256,128]{1,0:T(8,128)S(1)}, f32[256,128]{1,0:T(8,128)}, u32[]{:S(2)}) %copy-start.1) | copy-done | bytes 131096
  17.7 4.1 %assemble.1 = (bf16[8,256,256]{2,1,0:T(8,128)(2,1)S(1)}, bf16[8,256,256]{2,1,0:T(8,128)(2,1)S(1)}, bf16[128,256]{1,0:T(8,128)(2,1)S(1)}, bf16[128,256]{1,0:T(8,1...) custom-call(s32[128]{0:T(128)S(1)} %multiply_add_fusion.place_ref, s32[1]{0:T(128)S(6)} %copy.9.count_ref, ...), custom_call_target="tpu_custom_call" | custom-call | flops 10000000 | bytes 12000000 | tf_op jit(solution)/shard_map/assemble/pallas_call | solution.py:146
  21.8 0.0 collective-permute-done.refs_0_
  21.8 0.0 collective-permute-done.1.refs_1_
  21.8 0.9 %project_early.1 = (f32[256,128]{1,0:T(8,128)S(1)}, f32[128,128]{1,0:T(8,128)S(1)}) custom-call(bf16[8,256,256]{2,1,0:T(8,128)(2,1)S(1)} %get-tuple-element.12.high_ref, bf16[8,256,256]{2,1,0:T(8,128)(2,1)S(1)} %get-tuple-element.13.low_ref, bf16[128,256]{1,0:T(8,128)(2,1)S(1)} %get-tuple-element.14.turned_high_ref, ...), custom_call_target="tpu_custom_call" | custom-call | flops 300000000 | bytes 2500000 | tf_op jit(solution)/shard_map/project_early/pallas_call | solution.py:168
  22.8 0.0 collective-permute-done.4.refs_0_
  22.8 0.0 collective-permute-done.5.refs_1_
  22.8 0.0 collective-permute-done.6.refs_2_
  22.8 0.3 reduce_late.1
  23.1 0.6 %collective-permute-start.7 = (f32[64,128]{1,0:T(8,128)S(1)}, f32[64,128]{1,0:T(8,128)S(1)}, u32[]{:S(2)}, u32[]{:S(2)}) collective-permute-start(f32[64,128]{1,0:T(8,128)S(1)} %get-tuple-element.21), channel_id=1, source_target_pairs={{0,1},{1,0},{2,3},{3,2},{4,5},{5,4},{6,7},{7,6},{8,9},{9,8},{10,11... | collective-permute-start | bytes 98312 | tf_op jit(solution)/shard_map/ppermute | solution.py:202
  23.7 0.9 %collective-permute-done.7 = f32[64,128]{1,0:T(8,128)S(1)} collective-permute-done((f32[64,128]{1,0:T(8,128)S(1)}, f32[64,128]{1,0:T(8,128)S(1)}, u32[]{:S(2)}, u32[]{:S(2)}) %collective-permute-start.7) | collective-permute-done | bytes 32800 | tf_op jit(solution)/shard_map/ppermute | solution.py:202
  24.6 1.9 %collective-permute-start.8 = (f32[64,128]{1,0:T(8,128)S(1)}, f32[64,128]{1,0:T(8,128)S(1)}, u32[]{:S(2)}, u32[]{:S(2)}) collective-permute-start(f32[64,128]{1,0:T(8,128)S(1)} %add.47), channel_id=1, source_target_pairs={{0,2},{1,3},{2,0},{3,1},{4,6},{5,7},{6,4},{7,5},{8,10},{9,11},{10,... | collective-permute-start | bytes 98312 | tf_op jit(solution)/shard_map/ppermute | solution.py:202
  26.5 2.0 %collective-permute-done.8 = f32[64,128]{1,0:T(8,128)S(1)} collective-permute-done((f32[64,128]{1,0:T(8,128)S(1)}, f32[64,128]{1,0:T(8,128)S(1)}, u32[]{:S(2)}, u32[]{:S(2)}) %collective-permute-start.8) | collective-permute-done | bytes 32800 | tf_op jit(solution)/shard_map/ppermute | solution.py:202
  28.5 2.5 %collective-permute-start.9 = (f32[64,128]{1,0:T(8,128)S(1)}, f32[64,128]{1,0:T(8,128)S(1)}, u32[]{:S(2)}, u32[]{:S(2)}) collective-permute-start(f32[64,128]{1,0:T(8,128)S(1)} %add.48), channel_id=1, source_target_pairs={{0,4},{1,5},{2,6},{3,7},{4,0},{5,1},{6,2},{7,3},{8,12},{9,13},{10,... | collective-permute-start | bytes 98312 | tf_op jit(solution)/shard_map/ppermute | solution.py:202
  31.0 1.9 %collective-permute-done.9 = f32[64,128]{1,0:T(8,128)S(1)} collective-permute-done((f32[64,128]{1,0:T(8,128)S(1)}, f32[64,128]{1,0:T(8,128)S(1)}, u32[]{:S(2)}, u32[]{:S(2)}) %collective-permute-start.9) | collective-permute-done | bytes 32800 | tf_op jit(solution)/shard_map/ppermute | solution.py:202
  32.9 1.1 %collective-permute-start.10 = (f32[64,128]{1,0:T(8,128)S(1)}, f32[64,128]{1,0:T(8,128)S(1)}, u32[]{:S(2)}, u32[]{:S(2)}) collective-permute-start(f32[64,128]{1,0:T(8,128)S(1)} %add.49), channel_id=1, source_target_pairs={{0,8},{1,9},{2,10},{3,11},{4,12},{5,13},{6,14},{7,15},{8,0},{9,1},... | collective-permute-start | bytes 98312 | tf_op jit(solution)/shard_map/ppermute | solution.py:202
  34.0 3.7 %collective-permute-done.10 = f32[64,128]{1,0:T(8,128)S(1)} collective-permute-done((f32[64,128]{1,0:T(8,128)S(1)}, f32[64,128]{1,0:T(8,128)S(1)}, u32[]{:S(2)}, u32[]{:S(2)}) %collective-permute-start.10) | collective-permute-done | bytes 32800 | tf_op jit(solution)/shard_map/ppermute | solution.py:202
  37.7 1.1 %project_late.1 = f32[256,128]{1,0:T(8,128)} custom-call(bf16[8,256,256]{2,1,0:T(8,128)(2,1)S(1)} %get-tuple-element.12.high_ref, bf16[8,256,256]{2,1,0:T(8,128)(2,1)S(1)} %get-tuple-element.13.low_ref, f32[256,128]{1,0:T(8,128)S(1)} %get-tuple-element.16.total_ref, f32[256,128]{1,0:T(8,128)S(1)} %collective-permute-done.4.refs_0_, ...), custom_call_target="tpu_custom_call" | custom-call | flops 160000000 | bytes 1500000 | tf_op jit(solution)/shard_map/project_late/pallas_call | solution.py:191
  38.9 0.1 collective-permute-done.11.other_ref
  38.9 0.6 %join.1 = f32[128,128]{1,0:T(8,128)} custom-call(s32[1]{0:T(128)} %bitcast.2.core_ref, f32[64,128]{1,0:T(8,128)S(1)} %add.50.mine_ref, f32[64,128]{1,0:T(8,128)S(1)} %collective-permute-done.11.other_ref), custom_call_target="tpu_custom_call" | custom-call | bytes 130000 | tf_op jit(solution)/shard_map/join/pallas_call | solution.py:209
  (8 shorter events, 0.0 us)
Async XLA Ops:
  0.6 21.2 %copy-start.2 = (f32[256]{0:T(256)S(1)}, f32[256]{0:T(256)}, u32[]{:S(2)}) copy-start(f32[256]{0:T(256)} %param.8) | copy-start | bytes 3076
  0.6 9.3 %collective-permute-start.2 = (f32[256,128]{1,0:T(8,128)}, f32[256,128]{1,0:T(8,128)S(1)}, u32[]{:S(2)}, u32[]{:S(2)}) collective-permute-start(f32[256,128]{1,0:T(8,128)} %own_ref.1), channel_id=1, source_target_pairs={{4,0},{5,1},{6,2},{7,3},{8,4},{9,5},{10,6},{11,7},{12,8},{13,9},{1... | collective-permute-start | bytes 393224 | tf_op jit(solution)/shard_map/ppermute | solution.py:128
  5.7 8.1 %collective-permute-start.3 = (f32[256,128]{1,0:T(8,128)}, f32[256,128]{1,0:T(8,128)S(1)}, u32[]{:S(2)}, u32[]{:S(2)}) collective-permute-start(f32[256,128]{1,0:T(8,128)} %own_ref.1), channel_id=1, source_target_pairs={{12,0},{13,1},{14,2},{15,3},{0,4},{1,5},{2,6},{3,7},{4,8},{5,9},{6... | collective-permute-start | bytes 393224 | tf_op jit(solution)/shard_map/ppermute | solution.py:128
  5.7 16.1 %collective-permute-start = (f32[256,128]{1,0:T(8,128)}, f32[256,128]{1,0:T(8,128)S(1)}, u32[]{:S(2)}, u32[]{:S(2)}) collective-permute-start(f32[256,128]{1,0:T(8,128)} %own_ref.1), channel_id=1, source_target_pairs={{1,0},{2,1},{3,2},{4,3},{5,4},{6,5},{7,6},{8,7},{9,8},{10,9},{11,1... | collective-permute-start | bytes 393224 | tf_op jit(solution)/shard_map/ppermute | solution.py:128
  9.4 12.4 %collective-permute-start.1 = (f32[256,128]{1,0:T(8,128)}, f32[256,128]{1,0:T(8,128)S(1)}, u32[]{:S(2)}, u32[]{:S(2)}) collective-permute-start(f32[256,128]{1,0:T(8,128)} %own_ref.1), channel_id=1, source_target_pairs={{15,0},{0,1},{1,2},{2,3},{3,4},{4,5},{5,6},{6,7},{7,8},{8,9},{9,10... | collective-permute-start | bytes 393224 | tf_op jit(solution)/shard_map/ppermute | solution.py:128
  9.4 13.3 %collective-permute-start.4 = (f32[256,128]{1,0:T(8,128)}, f32[256,128]{1,0:T(8,128)S(1)}, u32[]{:S(2)}, u32[]{:S(2)}) collective-permute-start(f32[256,128]{1,0:T(8,128)} %own_ref.1), channel_id=1, source_target_pairs={{8,0},{9,1},{10,2},{11,3},{12,4},{13,5},{14,6},{15,7},{0,8},{1,9},... | collective-permute-start | bytes 393224 | tf_op jit(solution)/shard_map/ppermute | solution.py:128
  10.0 12.8 %collective-permute-start.5 = (f32[256,128]{1,0:T(8,128)S(1)}, f32[256,128]{1,0:T(8,128)S(1)}, u32[]{:S(2)}, u32[]{:S(2)}) collective-permute-start(f32[256,128]{1,0:T(8,128)S(1)} %collective-permute-done.2.refs_2_), channel_id=1, source_target_pairs={{1,0},{2,1},{3,2},{4,3},{5,4},{6,5},{7,6},{8,7},{9,8},{10,9},{11,1... | collective-permute-start | bytes 393224 | tf_op jit(solution)/shard_map/ppermute | solution.py:128
  13.9 8.9 %collective-permute-start.6 = (f32[256,128]{1,0:T(8,128)S(1)}, f32[256,128]{1,0:T(8,128)S(1)}, u32[]{:S(2)}, u32[]{:S(2)}) collective-permute-start(f32[256,128]{1,0:T(8,128)S(1)} %collective-permute-done.3.refs_3_), channel_id=1, source_target_pairs={{15,0},{0,1},{1,2},{2,3},{3,4},{4,5},{5,6},{6,7},{7,8},{8,9},{9,10... | collective-permute-start | bytes 393224 | tf_op jit(solution)/shard_map/ppermute | solution.py:128
  15.2 1.6 %copy-start = (f32[128,4096]{1,0:T(8,128)S(1)}, f32[128,4096]{1,0:T(8,128)}, u32[]{:S(2)}) copy-start(f32[128,4096]{1,0:T(8,128)} %blocks_ref.1) | copy-start | bytes 6291460
  16.8 0.9 %copy-start.1 = (f32[256,128]{1,0:T(8,128)S(1)}, f32[256,128]{1,0:T(8,128)}, u32[]{:S(2)}) copy-start(f32[256,128]{1,0:T(8,128)} %own_ref.1) | copy-start | bytes 393220
  23.1 1.5 %collective-permute-start.7 = (f32[64,128]{1,0:T(8,128)S(1)}, f32[64,128]{1,0:T(8,128)S(1)}, u32[]{:S(2)}, u32[]{:S(2)}) collective-permute-start(f32[64,128]{1,0:T(8,128)S(1)} %get-tuple-element.21), channel_id=1, source_target_pairs={{0,1},{1,0},{2,3},{3,2},{4,5},{5,4},{6,7},{7,6},{8,9},{9,8},{10,11... | collective-permute-start | bytes 98312 | tf_op jit(solution)/shard_map/ppermute | solution.py:202
  24.6 3.9 %collective-permute-start.8 = (f32[64,128]{1,0:T(8,128)S(1)}, f32[64,128]{1,0:T(8,128)S(1)}, u32[]{:S(2)}, u32[]{:S(2)}) collective-permute-start(f32[64,128]{1,0:T(8,128)S(1)} %add.47), channel_id=1, source_target_pairs={{0,2},{1,3},{2,0},{3,1},{4,6},{5,7},{6,4},{7,5},{8,10},{9,11},{10,... | collective-permute-start | bytes 98312 | tf_op jit(solution)/shard_map/ppermute | solution.py:202
  28.5 4.4 %collective-permute-start.9 = (f32[64,128]{1,0:T(8,128)S(1)}, f32[64,128]{1,0:T(8,128)S(1)}, u32[]{:S(2)}, u32[]{:S(2)}) collective-permute-start(f32[64,128]{1,0:T(8,128)S(1)} %add.48), channel_id=1, source_target_pairs={{0,4},{1,5},{2,6},{3,7},{4,0},{5,1},{6,2},{7,3},{8,12},{9,13},{10,... | collective-permute-start | bytes 98312 | tf_op jit(solution)/shard_map/ppermute | solution.py:202
  32.9 4.8 %collective-permute-start.10 = (f32[64,128]{1,0:T(8,128)S(1)}, f32[64,128]{1,0:T(8,128)S(1)}, u32[]{:S(2)}, u32[]{:S(2)}) collective-permute-start(f32[64,128]{1,0:T(8,128)S(1)} %add.49), channel_id=1, source_target_pairs={{0,8},{1,9},{2,10},{3,11},{4,12},{5,13},{6,14},{7,15},{8,0},{9,1},... | collective-permute-start | bytes 98312 | tf_op jit(solution)/shard_map/ppermute | solution.py:202
  37.7 1.2 %collective-permute-start.11 = (f32[64,128]{1,0:T(8,128)S(1)}, f32[64,128]{1,0:T(8,128)S(1)}, u32[]{:S(2)}, u32[]{:S(2)}) collective-permute-start(f32[64,128]{1,0:T(8,128)S(1)} %add.50.mine_ref), channel_id=1, source_target_pairs={{0,1},{1,0},{2,3},{3,2},{4,5},{5,4},{6,7},{7,6},{8,9},{9,8},{10,11... | collective-permute-start | bytes 98312 | tf_op jit(solution)/shard_map/ppermute | solution.py:202
where the time goes:
time: 39.6 us
  starting transfers between devices  18.8 us (47%)
  waiting for transfers between devices  9.11 us (23%)
  Pallas kernels  7.07 us (18%)
  local copies, waits for them, and re-layouts  2.49 us (6%)
  between operations  1.39 us (4%)
  other arithmetic  0.73 us (2%)
    ppermute x7, starting transfers between devices, fetch(): return lax.ppermute(block, 'row', [((d + step) % n, d) for d in range(n)])  12.7 us
    ppermute x5, waiting for transfers between devices, swap(): return lax.ppermute(block, 'row', [(d, d ^ apart) for d in range(n)])  8.54 us
    ppermute x5, starting transfers between devices, swap(): return lax.ppermute(block, 'row', [(d, d ^ apart) for d in range(n)])  6.11 us
    pallas_call x1, Pallas kernels, shards(): pl.pallas_call(assemble, out_shape=(jax.ShapeDtypeStruct((LINKS, ROWS, RO...  4.07 us
    unnamed x6, local copies, waits for them, and re-layouts  2.49 us
    pallas_call x1, Pallas kernels, shards(): pl.pallas_call(project_late, out_shape=jax.ShapeDtypeStruct((ROWS, MODES)...  1.13 us
    pallas_call x1, Pallas kernels, shards(): pl.pallas_call(project_early, out_shape=(jax.ShapeDtypeStruct((ROWS, MODE...  0.91 us
  transfers between devices with their start and end apart: 12, of which 6 were waited for; matrix products, arithmetic and copies ran while one was open for 2% of the time, Pallas kernels for 15%

commit v1 on v0

--- a/solution.py
+++ b/solution.py
@@ -92,31 +92,36 @@
     partial_ref[...] = dot3(turned_high_ref[...], turned_low_ref[...], *split(sorted_total))
 
 
-def reduce_late(scale, core_ref, weight_high_ref, weight_low_ref, early_ref, *refs):
+def reduce_late(scale, side_ref, weight_high_ref, weight_low_ref, early_ref, *refs):
     basis_refs, (kept_ref, sent_ref, partial) = refs[:LATE], refs[LATE:]
     total = early_ref[...]
     for k, ref in enumerate(basis_refs):
         total += dot3(weight_high_ref[k], weight_low_ref[k], *split(ref[...]))
     partial[...] = total * scale
     half = MODES // 2
-    kept_ref[...] = partial[pl.ds(pl.multiple_of(core_ref[0] * half, half), half), :]
-    sent_ref[...] = partial[pl.ds(pl.multiple_of((1 - core_ref[0]) * half, half), half), :]
-
-
-def join(core_ref, mine_ref, other_ref, whole_ref):
+    kept_ref[...] = partial[pl.ds(pl.multiple_of(side_ref[0] * half, half), half), :]
+    sent_ref[...] = partial[pl.ds(pl.multiple_of((1 - side_ref[0]) * half, half), half), :]
+
+
+def add_after(first_ref, second_ref, done_ref, sum_ref):
+    sum_ref[...] = first_ref[...] + second_ref[...]
+
+
+def join(side_ref, mine_ref, other_ref, whole_ref):
     half = MODES // 2
-    whole_ref[pl.ds(pl.multiple_of(core_ref[0] * half, half), half), :] = mine_ref[...]
-    whole_ref[pl.ds(pl.multiple_of((1 - core_ref[0]) * half, half), half), :] = other_ref[...]
+    whole_ref[pl.ds(pl.multiple_of(side_ref[0] * half, half), half), :] = mine_ref[...]
+    whole_ref[pl.ds(pl.multiple_of((1 - side_ref[0]) * half, half), half), :] = other_ref[...]
 
 
 def project_late(high_ref, low_ref, total_ref, *refs):
-    basis_refs, stiff_ref = refs[:LATE], refs[LATE]
+    basis_refs, (stiff_ref, done_ref) = refs[:LATE], refs[LATE:]
     total = jnp.zeros((ROWS, MODES), jnp.float32)
     for k, ref in enumerate(basis_refs):
         b_high, b_low = split(ref[...])
         total += dot3(high_ref[LINKS - LATE + k], low_ref[LINKS - LATE + k], b_high, b_low)
     for rows, target in halves():
         stiff_ref[rows, :] = total_ref[rows, :] + total[target, :]
+    done_ref[...] = jnp.zeros_like(done_ref)
 
 
 def shards(basis, springs, tangent_blocks, tile_rows, tile_owner, tile_offset, tile_count):
@@ -175,7 +180,10 @@
         name="project_early",
     )(high, low, turned_high, turned_low, springs.reshape(1, ROWS), basis, after, before, above, below)
 
-    core = (me % 2).reshape(1)
+    side = me
+    for shift in (8, 4, 2, 1):
+        side = side ^ (side >> shift)
+    side = (side & 1).reshape(1)
     piece = jax.ShapeDtypeStruct((MODES // 2, MODES), full)
     kept, sent = pl.pallas_call(
         functools.partial(reduce_late, 1.0 / (basis.shape[0] * n)),
@@ -186,13 +194,13 @@
         compiler_params=params,
         cost_estimate=pl.CostEstimate(flops=80_000_000, bytes_accessed=700_000, transcendentals=0),
         name="reduce_late",
-    )(core, weight_high, weight_low, early, across, far_above, far_below)
-
-    stiff_image = pl.pallas_call(
+    )(side, weight_high, weight_low, early, across, far_above, far_below)
+
+    stiff_image, done = pl.pallas_call(
         project_late,
-        out_shape=jax.ShapeDtypeStruct((ROWS, MODES), full),
+        out_shape=(jax.ShapeDtypeStruct((ROWS, MODES), full), jax.ShapeDtypeStruct((8, 128), full)),
         in_specs=[vmem] * (3 + LATE),
-        out_specs=vmem,
+        out_specs=(vmem,) * 2,
         compiler_params=params,
         cost_estimate=pl.CostEstimate(flops=160_000_000, bytes_accessed=1_500_000, transcendentals=0),
         name="project_late",
@@ -202,9 +210,17 @@
         return lax.ppermute(block, "row", [(d, d ^ apart) for d in range(n)])
 
     mine = kept + swap(sent, 1)
-    apart = 2
+    mine = pl.pallas_call(
+        add_after,
+        out_shape=piece,
+        in_specs=[vmem] * 3,
+        out_specs=vmem,
+        compiler_params=params,
+        name="add_after",
+    )(mine, swap(mine, 3), done)
+    apart = 4
     while apart < n:
-        mine += swap(mine, apart)
+        mine += swap(mine, apart + 1)
         apart *= 2
     reduced = pl.pallas_call(
         join,
@@ -214,7 +230,7 @@
         compiler_params=params,
         cost_estimate=pl.CostEstimate(flops=0, bytes_accessed=130_000, transcendentals=0),
         name="join",
-    )(core, mine, swap(mine, 1))
+    )(side, mine, swap(mine, 1))
     return (stiff_image, reduced)
 
 

time: 39.6 us -> 38.3 us (0.967)
  waiting for transfers between devices: 9.11 us -> 8.23 us
  starting transfers between devices: 18.8 us -> 18.1 us
    ppermute x5, waiting for transfers between devices: 8.54 us -> 7.66 us  [swap(): return lax.ppermute(block, 'row', [(d, d ^ apart) for d in range(n)])]
    ppermute x5, starting transfers between devices: 6.11 us -> 5.39 us  [swap(): return lax.ppermute(block, 'row', [(d, d ^ apart) for d in range(n)])]
    pallas_call x1 -> x2, Pallas kernels: 1.13 us -> 1.13 us  [the longest x1 1.13 us: shards(): pl.pallas_call(project_late, out_shape=(jax.ShapeDtypeStruct((ROWS, MODES...]
  transfers between devices with their start and end apart: 12 -> 12, of which waited for: 6 -> 6; matrix products, arithmetic and copies ran while one was open for 2% -> 2% of each run, Pallas kernels for 15% -> 16%
where the time goes in v1:
time: 38.3 us; the launch traced here: 38.1 us
  starting transfers between devices  18.1 us (47%)
  waiting for transfers between devices  8.23 us (21%)
  Pallas kernels  7.21 us (19%)
  local copies, waits for them, and re-layouts  2.49 us (7%)
  between operations  1.38 us (4%)
  other arithmetic  0.72 us (2%)
    ppermute x7, starting transfers between devices, fetch(): return lax.ppermute(block, 'row', [((d + step) % n, d) for d in range(n)])  12.7 us
    ppermute x5, waiting for transfers between devices, swap(): return lax.ppermute(block, 'row', [(d, d ^ apart) for d in range(n)])  7.66 us
    ppermute x5, starting transfers between devices, swap(): return lax.ppermute(block, 'row', [(d, d ^ apart) for d in range(n)])  5.39 us
    pallas_call x1, Pallas kernels, shards(): pl.pallas_call(assemble, out_shape=(jax.ShapeDtypeStruct((LINKS, ROWS, RO...  4.21 us
    unnamed x6, local copies, waits for them, and re-layouts  2.49 us
    pallas_call x1, Pallas kernels, shards(): pl.pallas_call(project_late, out_shape=(jax.ShapeDtypeStruct((ROWS, MODES...  1.13 us
    pallas_call x1, Pallas kernels, shards(): pl.pallas_call(project_early, out_shape=(jax.ShapeDtypeStruct((ROWS, MODE...  0.91 us
  transfers between devices with their start and end apart: 12, of which 6 were waited for; matrix products, arithmetic and copies ran while one was open for 2% of the time, Pallas kernels for 16%

profile of v1, /device:TPU:0, one launch (start us, length us, event | category | flops | bytes accessed | tf_op | source)
XLA Modules:
  0.0 38.1 jit_solution(12608376230459820983)
XLA Ops:
  0.6 5.1 %collective-permute-start.2 = (f32[256,128]{1,0:T(8,128)}, f32[256,128]{1,0:T(8,128)S(1)}, u32[]{:S(2)}, u32[]{:S(2)}) collective-permute-start(f32[256,128]{1,0:T(8,128)} %own_ref.1), channel_id=1, source_target_pairs={{4,0},{5,1},{6,2},{7,3},{8,4},{9,5},{10,6},{11,7},{12,8},{13,9},{1... | collective-permute-start | bytes 393224 | tf_op jit(solution)/shard_map/ppermute | solution.py:133
  5.7 0.0 collective-permute-start.3
  5.7 3.7 %collective-permute-start = (f32[256,128]{1,0:T(8,128)}, f32[256,128]{1,0:T(8,128)S(1)}, u32[]{:S(2)}, u32[]{:S(2)}) collective-permute-start(f32[256,128]{1,0:T(8,128)} %own_ref.1), channel_id=1, source_target_pairs={{1,0},{2,1},{3,2},{4,3},{5,4},{6,5},{7,6},{8,7},{9,8},{10,9},{11,1... | collective-permute-start | bytes 393224 | tf_op jit(solution)/shard_map/ppermute | solution.py:133
  9.4 0.0 collective-permute-start.1
  9.4 0.0 collective-permute-start.4
  9.4 0.6 %collective-permute-done.2.refs_2_ = f32[256,128]{1,0:T(8,128)S(1)} collective-permute-done((f32[256,128]{1,0:T(8,128)}, f32[256,128]{1,0:T(8,128)S(1)}, u32[]{:S(2)}, u32[]{:S(2)}) %collective-permute-start.2) | collective-permute-done | bytes 131104 | tf_op jit(solution)/shard_map/ppermute | solution.py:133
  10.0 3.9 %collective-permute-start.5 = (f32[256,128]{1,0:T(8,128)S(1)}, f32[256,128]{1,0:T(8,128)S(1)}, u32[]{:S(2)}, u32[]{:S(2)}) collective-permute-start(f32[256,128]{1,0:T(8,128)S(1)} %collective-permute-done.2.refs_2_), channel_id=1, source_target_pairs={{1,0},{2,1},{3,2},{4,3},{5,4},{6,5},{7,6},{8,7},{9,8},{10,9},{11,1... | collective-permute-start | bytes 393224 | tf_op jit(solution)/shard_map/ppermute | solution.py:133
  13.9 0.0 collective-permute-done.3.refs_3_
  13.9 0.0 collective-permute-start.6
  13.9 0.7 %multiply_add_fusion.place_ref = s32[128]{0:T(128)S(1)} fusion(s32[128]{0:T(128)} %param.12, s32[128]{0:T(128)} %param.10, s32[128,1]{0,1:T(1,128)} %param.11, s32[]{:T(128)S(6)} %axis_index.12), kind=kLoop, calls=%fused_computation.13 | loop fusion | flops 3968 | bytes 2052 | tf_op jit(solution)/shard_map/add | solution.py:144
  15.2 0.0 copy-start
  15.2 1.6 %copy-done = f32[128,4096]{1,0:T(8,128)S(1)} copy-done((f32[128,4096]{1,0:T(8,128)S(1)}, f32[128,4096]{1,0:T(8,128)}, u32[]{:S(2)}) %copy-start) | copy-done | bytes 2097176
  16.8 0.9 %copy-done.1 = f32[256,128]{1,0:T(8,128)S(1)} copy-done((f32[256,128]{1,0:T(8,128)S(1)}, f32[256,128]{1,0:T(8,128)}, u32[]{:S(2)}) %copy-start.1) | copy-done | bytes 131096
  17.7 4.2 %assemble.1 = (bf16[8,256,256]{2,1,0:T(8,128)(2,1)S(1)}, bf16[8,256,256]{2,1,0:T(8,128)(2,1)S(1)}, bf16[128,256]{1,0:T(8,128)(2,1)S(1)}, bf16[128,256]{1,0:T(8,1...) custom-call(s32[128]{0:T(128)S(1)} %multiply_add_fusion.place_ref, s32[1]{0:T(128)S(6)} %copy.9.count_ref, ...), custom_call_target="tpu_custom_call" | custom-call | flops 10000000 | bytes 12000000 | tf_op jit(solution)/shard_map/assemble/pallas_call | solution.py:151
  21.9 0.0 collective-permute-done.refs_0_
  22.0 0.0 collective-permute-done.1.refs_1_
  22.0 0.9 %project_early.1 = (f32[256,128]{1,0:T(8,128)S(1)}, f32[128,128]{1,0:T(8,128)S(1)}) custom-call(bf16[8,256,256]{2,1,0:T(8,128)(2,1)S(1)} %get-tuple-element.14.high_ref, bf16[8,256,256]{2,1,0:T(8,128)(2,1)S(1)} %get-tuple-element.15.low_ref, bf16[128,256]{1,0:T(8,128)(2,1)S(1)} %get-tuple-element.16.turned_high_ref, ...), custom_call_target="tpu_custom_call" | custom-call | flops 300000000 | bytes 2500000 | tf_op jit(solution)/shard_map/project_early/pallas_call | solution.py:173
  22.9 0.0 collective-permute-done.4.refs_0_
  22.9 0.0 collective-permute-done.5.refs_1_
  22.9 0.3 reduce_late.1
  23.2 0.6 %collective-permute-start.7 = (f32[64,128]{1,0:T(8,128)S(1)}, f32[64,128]{1,0:T(8,128)S(1)}, u32[]{:S(2)}, u32[]{:S(2)}) collective-permute-start(f32[64,128]{1,0:T(8,128)S(1)} %get-tuple-element.24), channel_id=1, source_target_pairs={{0,1},{1,0},{2,3},{3,2},{4,5},{5,4},{6,7},{7,6},{8,9},{9,8},{10,11... | collective-permute-start | bytes 98312 | tf_op jit(solution)/shard_map/ppermute | solution.py:210
  23.9 0.9 %collective-permute-done.7 = f32[64,128]{1,0:T(8,128)S(1)} collective-permute-done((f32[64,128]{1,0:T(8,128)S(1)}, f32[64,128]{1,0:T(8,128)S(1)}, u32[]{:S(2)}, u32[]{:S(2)}) %collective-permute-start.7) | collective-permute-done | bytes 32800 | tf_op jit(solution)/shard_map/ppermute | solution.py:210
  24.7 2.3 %collective-permute-start.8 = (f32[64,128]{1,0:T(8,128)S(1)}, f32[64,128]{1,0:T(8,128)S(1)}, u32[]{:S(2)}, u32[]{:S(2)}) collective-permute-start(f32[64,128]{1,0:T(8,128)S(1)} %add.39.first_ref), channel_id=1, source_target_pairs={{0,3},{1,2},{2,1},{3,0},{4,7},{5,6},{6,5},{7,4},{8,11},{9,10},{10,... | collective-permute-start | bytes 98312 | tf_op jit(solution)/shard_map/ppermute | solution.py:210
  27.0 1.1 %project_late.1 = (f32[256,128]{1,0:T(8,128)}, f32[8,128]{1,0:T(8,128)S(1)}) custom-call(bf16[8,256,256]{2,1,0:T(8,128)(2,1)S(1)} %get-tuple-element.14.high_ref, bf16[8,256,256]{2,1,0:T(8,128)(2,1)S(1)} %get-tuple-element.15.low_ref, f32[256,128]{1,0:T(8,128)S(1)} %get-tuple-element.18.total_ref, f32[256,128]{1,0:T(8,128)S(1)} %collective-permute-done.4.refs_0_, ...), custom_call_target="tpu_custom_call" | custom-call | flops 160000000 | bytes 1500000 | tf_op jit(solution)/shard_map/project_late/pallas_call | solution.py:199
  28.2 0.5 %collective-permute-done.8.second_ref = f32[64,128]{1,0:T(8,128)S(1)} collective-permute-done((f32[64,128]{1,0:T(8,128)S(1)}, f32[64,128]{1,0:T(8,128)S(1)}, u32[]{:S(2)}, u32[]{:S(2)}) %collective-permute-start.8) | collective-permute-done | bytes 32800 | tf_op jit(solution)/shard_map/ppermute | solution.py:210
  28.7 1.4 %collective-permute-start.9 = (f32[64,128]{1,0:T(8,128)S(1)}, f32[64,128]{1,0:T(8,128)S(1)}, u32[]{:S(2)}, u32[]{:S(2)}) collective-permute-start(f32[64,128]{1,0:T(8,128)S(1)} %add_after.1), channel_id=1, source_target_pairs={{0,5},{1,4},{2,7},{3,6},{4,1},{5,0},{6,3},{7,2},{8,13},{9,12},{10,... | collective-permute-start | bytes 98312 | tf_op jit(solution)/shard_map/ppermute | solution.py:210
  30.0 2.0 %collective-permute-done.9 = f32[64,128]{1,0:T(8,128)S(1)} collective-permute-done((f32[64,128]{1,0:T(8,128)S(1)}, f32[64,128]{1,0:T(8,128)S(1)}, u32[]{:S(2)}, u32[]{:S(2)}) %collective-permute-start.9) | collective-permute-done | bytes 32800 | tf_op jit(solution)/shard_map/ppermute | solution.py:210
  32.0 0.9 %collective-permute-start.10 = (f32[64,128]{1,0:T(8,128)S(1)}, f32[64,128]{1,0:T(8,128)S(1)}, u32[]{:S(2)}, u32[]{:S(2)}) collective-permute-start(f32[64,128]{1,0:T(8,128)S(1)} %add.40), channel_id=1, source_target_pairs={{0,9},{1,8},{2,11},{3,10},{4,13},{5,12},{6,15},{7,14},{8,1},{9,0},... | collective-permute-start | bytes 98312 | tf_op jit(solution)/shard_map/ppermute | solution.py:210
  32.9 3.3 %collective-permute-done.10 = f32[64,128]{1,0:T(8,128)S(1)} collective-permute-done((f32[64,128]{1,0:T(8,128)S(1)}, f32[64,128]{1,0:T(8,128)S(1)}, u32[]{:S(2)}, u32[]{:S(2)}) %collective-permute-start.10) | collective-permute-done | bytes 32800 | tf_op jit(solution)/shard_map/ppermute | solution.py:210
  36.2 0.2 collective-permute-start.11
  36.4 1.0 %collective-permute-done.11.other_ref = f32[64,128]{1,0:T(8,128)S(1)} collective-permute-done((f32[64,128]{1,0:T(8,128)S(1)}, f32[64,128]{1,0:T(8,128)S(1)}, u32[]{:S(2)}, u32[]{:S(2)}) %collective-permute-start.11) | collective-permute-done | bytes 32800 | tf_op jit(solution)/shard_map/ppermute | solution.py:210
  37.5 0.6 %join.1 = f32[128,128]{1,0:T(8,128)} custom-call(s32[1]{0:T(128)} %bitcast.2.side_ref, f32[64,128]{1,0:T(8,128)S(1)} %add.41.mine_ref, f32[64,128]{1,0:T(8,128)S(1)} %collective-permute-done.11.other_ref), custom_call_target="tpu_custom_call" | custom-call | bytes 130000 | tf_op jit(solution)/shard_map/join/pallas_call | solution.py:225
  (8 shorter events, 0.0 us)
Async XLA Ops:
  0.6 21.3 %copy-start.2 = (f32[256]{0:T(256)S(1)}, f32[256]{0:T(256)}, u32[]{:S(2)}) copy-start(f32[256]{0:T(256)} %param.8) | copy-start | bytes 3076
  0.6 9.3 %collective-permute-start.2 = (f32[256,128]{1,0:T(8,128)}, f32[256,128]{1,0:T(8,128)S(1)}, u32[]{:S(2)}, u32[]{:S(2)}) collective-permute-start(f32[256,128]{1,0:T(8,128)} %own_ref.1), channel_id=1, source_target_pairs={{4,0},{5,1},{6,2},{7,3},{8,4},{9,5},{10,6},{11,7},{12,8},{13,9},{1... | collective-permute-start | bytes 393224 | tf_op jit(solution)/shard_map/ppermute | solution.py:133
  5.7 8.1 %collective-permute-start.3 = (f32[256,128]{1,0:T(8,128)}, f32[256,128]{1,0:T(8,128)S(1)}, u32[]{:S(2)}, u32[]{:S(2)}) collective-permute-start(f32[256,128]{1,0:T(8,128)} %own_ref.1), channel_id=1, source_target_pairs={{12,0},{13,1},{14,2},{15,3},{0,4},{1,5},{2,6},{3,7},{4,8},{5,9},{6... | collective-permute-start | bytes 393224 | tf_op jit(solution)/shard_map/ppermute | solution.py:133
  5.7 16.2 %collective-permute-start = (f32[256,128]{1,0:T(8,128)}, f32[256,128]{1,0:T(8,128)S(1)}, u32[]{:S(2)}, u32[]{:S(2)}) collective-permute-start(f32[256,128]{1,0:T(8,128)} %own_ref.1), channel_id=1, source_target_pairs={{1,0},{2,1},{3,2},{4,3},{5,4},{6,5},{7,6},{8,7},{9,8},{10,9},{11,1... | collective-permute-start | bytes 393224 | tf_op jit(solution)/shard_map/ppermute | solution.py:133
  9.4 12.6 %collective-permute-start.1 = (f32[256,128]{1,0:T(8,128)}, f32[256,128]{1,0:T(8,128)S(1)}, u32[]{:S(2)}, u32[]{:S(2)}) collective-permute-start(f32[256,128]{1,0:T(8,128)} %own_ref.1), channel_id=1, source_target_pairs={{15,0},{0,1},{1,2},{2,3},{3,4},{4,5},{5,6},{6,7},{7,8},{8,9},{9,10... | collective-permute-start | bytes 393224 | tf_op jit(solution)/shard_map/ppermute | solution.py:133
  9.4 13.5 %collective-permute-start.4 = (f32[256,128]{1,0:T(8,128)}, f32[256,128]{1,0:T(8,128)S(1)}, u32[]{:S(2)}, u32[]{:S(2)}) collective-permute-start(f32[256,128]{1,0:T(8,128)} %own_ref.1), channel_id=1, source_target_pairs={{8,0},{9,1},{10,2},{11,3},{12,4},{13,5},{14,6},{15,7},{0,8},{1,9},... | collective-permute-start | bytes 393224 | tf_op jit(solution)/shard_map/ppermute | solution.py:133
  10.0 12.9 %collective-permute-start.5 = (f32[256,128]{1,0:T(8,128)S(1)}, f32[256,128]{1,0:T(8,128)S(1)}, u32[]{:S(2)}, u32[]{:S(2)}) collective-permute-start(f32[256,128]{1,0:T(8,128)S(1)} %collective-permute-done.2.refs_2_), channel_id=1, source_target_pairs={{1,0},{2,1},{3,2},{4,3},{5,4},{6,5},{7,6},{8,7},{9,8},{10,9},{11,1... | collective-permute-start | bytes 393224 | tf_op jit(solution)/shard_map/ppermute | solution.py:133
  13.9 9.1 %collective-permute-start.6 = (f32[256,128]{1,0:T(8,128)S(1)}, f32[256,128]{1,0:T(8,128)S(1)}, u32[]{:S(2)}, u32[]{:S(2)}) collective-permute-start(f32[256,128]{1,0:T(8,128)S(1)} %collective-permute-done.3.refs_3_), channel_id=1, source_target_pairs={{15,0},{0,1},{1,2},{2,3},{3,4},{4,5},{5,6},{6,7},{7,8},{8,9},{9,10... | collective-permute-start | bytes 393224 | tf_op jit(solution)/shard_map/ppermute | solution.py:133
  15.2 1.6 %copy-start = (f32[128,4096]{1,0:T(8,128)S(1)}, f32[128,4096]{1,0:T(8,128)}, u32[]{:S(2)}) copy-start(f32[128,4096]{1,0:T(8,128)} %blocks_ref.1) | copy-start | bytes 6291460
  16.8 0.9 %copy-start.1 = (f32[256,128]{1,0:T(8,128)S(1)}, f32[256,128]{1,0:T(8,128)}, u32[]{:S(2)}) copy-start(f32[256,128]{1,0:T(8,128)} %own_ref.1) | copy-start | bytes 393220
  23.2 1.5 %collective-permute-start.7 = (f32[64,128]{1,0:T(8,128)S(1)}, f32[64,128]{1,0:T(8,128)S(1)}, u32[]{:S(2)}, u32[]{:S(2)}) collective-permute-start(f32[64,128]{1,0:T(8,128)S(1)} %get-tuple-element.24), channel_id=1, source_target_pairs={{0,1},{1,0},{2,3},{3,2},{4,5},{5,4},{6,7},{7,6},{8,9},{9,8},{10,11... | collective-permute-start | bytes 98312 | tf_op jit(solution)/shard_map/ppermute | solution.py:210
  24.7 3.9 %collective-permute-start.8 = (f32[64,128]{1,0:T(8,128)S(1)}, f32[64,128]{1,0:T(8,128)S(1)}, u32[]{:S(2)}, u32[]{:S(2)}) collective-permute-start(f32[64,128]{1,0:T(8,128)S(1)} %add.39.first_ref), channel_id=1, source_target_pairs={{0,3},{1,2},{2,1},{3,0},{4,7},{5,6},{6,5},{7,4},{8,11},{9,10},{10,... | collective-permute-start | bytes 98312 | tf_op jit(solution)/shard_map/ppermute | solution.py:210
  28.7 3.3 %collective-permute-start.9 = (f32[64,128]{1,0:T(8,128)S(1)}, f32[64,128]{1,0:T(8,128)S(1)}, u32[]{:S(2)}, u32[]{:S(2)}) collective-permute-start(f32[64,128]{1,0:T(8,128)S(1)} %add_after.1), channel_id=1, source_target_pairs={{0,5},{1,4},{2,7},{3,6},{4,1},{5,0},{6,3},{7,2},{8,13},{9,12},{10,... | collective-permute-start | bytes 98312 | tf_op jit(solution)/shard_map/ppermute | solution.py:210
  32.0 4.2 %collective-permute-start.10 = (f32[64,128]{1,0:T(8,128)S(1)}, f32[64,128]{1,0:T(8,128)S(1)}, u32[]{:S(2)}, u32[]{:S(2)}) collective-permute-start(f32[64,128]{1,0:T(8,128)S(1)} %add.40), channel_id=1, source_target_pairs={{0,9},{1,8},{2,11},{3,10},{4,13},{5,12},{6,15},{7,14},{8,1},{9,0},... | collective-permute-start | bytes 98312 | tf_op jit(solution)/shard_map/ppermute | solution.py:210
  36.2 1.2 %collective-permute-start.11 = (f32[64,128]{1,0:T(8,128)S(1)}, f32[64,128]{1,0:T(8,128)S(1)}, u32[]{:S(2)}, u32[]{:S(2)}) collective-permute-start(f32[64,128]{1,0:T(8,128)S(1)} %add.41.mine_ref), channel_id=1, source_target_pairs={{0,1},{1,0},{2,3},{3,2},{4,5},{5,4},{6,7},{7,6},{8,9},{9,8},{10,11... | collective-permute-start | bytes 98312 | tf_op jit(solution)/shard_map/ppermute | solution.py:210

commit v2 on v1

--- a/solution.py
+++ b/solution.py
@@ -33,25 +33,24 @@
             yield pl.ds(r * B + h, HALF, stride=2), slice(r * B + h * HALF, r * B + (h + 1) * HALF)
 
 
-def assemble(place_ref, count_ref, blocks_ref, basis_ref, high_ref, low_ref, turned_high_ref, turned_low_ref, weight_high_ref, weight_low_ref, slots, dense, sorted_basis):
-    dense[...] = jnp.zeros_like(dense)
+def sum_slots(place_ref, blocks_ref, basis_ref, dense_ref, turned_high_ref, turned_low_ref, sorted_basis):
+    dense_ref[...] = jnp.zeros_like(dense_ref)
+
+    @pl.loop(0, CAP // 8)
+    def _(group):
+        for k in range(8):
+            block = blocks_ref[pl.ds(group * (8 * HALF) + k, HALF, stride=8), :]
+            target = pl.ds(pl.multiple_of(place_ref[group * 8 + k] * HALF, HALF), HALF)
+            dense_ref[target, :] += block
+
     for rows, target in halves():
         sorted_basis[target, :] = basis_ref[rows, :]
     turned_high, turned_low = split(sorted_basis[...].T)
     turned_high_ref[...] = turned_high
     turned_low_ref[...] = turned_low
 
-    @pl.loop(0, CAP // 8)
-    def _(group):
-        eight = blocks_ref[pl.ds(pl.multiple_of(group * 8, 8), 8), :]
-        for t in range(HALF):
-            slots[pl.ds(group * (8 * HALF) + t, 8, stride=HALF), :] = eight[:, t * 128:(t + 1) * 128]
-
-    @pl.loop(0, count_ref[0])
-    def _(s):
-        target = pl.ds(pl.multiple_of(place_ref[s] * HALF, HALF), HALF)
-        dense[target, :] += slots[pl.ds(pl.multiple_of(s * HALF, HALF), HALF), :]
-
+
+def pack(dense_ref, turned_high_ref, turned_low_ref, high_ref, low_ref, weight_high_ref, weight_low_ref):
     left = lax.broadcasted_iota(jnp.int32, (HALF, 128), 1) < B
 
     @pl.loop(0, LINKS)
@@ -59,8 +58,8 @@
         for r in range(BR_DEV):
             for pair in range(BR_DEV // 2):
                 start = ((link * BR_DEV + r) * BR_DEV + 2 * pair) * HALF
-                first = dense[pl.ds(pl.multiple_of(start, HALF), HALF), :]
-                second = dense[pl.ds(pl.multiple_of(start + HALF, HALF), HALF), :]
+                first = dense_ref[pl.ds(pl.multiple_of(start, HALF), HALF), :]
+                second = dense_ref[pl.ds(pl.multiple_of(start + HALF, HALF), HALF), :]
                 even = jnp.where(left, first, pltpu.roll(second, B, 1))
                 odd = jnp.where(left, pltpu.roll(first, B, 1), second)
                 for h, part in enumerate((even, odd)):
@@ -71,21 +70,21 @@
 
     for k in range(LATE):
         link = LINKS - LATE + k
-        high, low = split(dot3(turned_high, turned_low, high_ref[link], low_ref[link]))
+        high, low = split(dot3(turned_high_ref[...], turned_low_ref[...], high_ref[link], low_ref[link]))
         weight_high_ref[k] = high
         weight_low_ref[k] = low
 
 
-def project_early(high_ref, low_ref, turned_high_ref, turned_low_ref, springs_ref, own_ref, *refs):
+def project_early(high_ref, low_ref, turned_high_ref, turned_low_ref, springs_ref, *refs):
     basis_refs, (total_ref, partial_ref) = refs[:-2], refs[-2:]
     total = jnp.zeros((ROWS, MODES), jnp.float32)
-    for link, ref in enumerate((own_ref,) + basis_refs):
+    for link, ref in enumerate(basis_refs):
         b_high, b_low = split(ref[...])
         total += dot3(high_ref[link], low_ref[link], b_high, b_low)
     for part in range(ROWS // MODES):
         rows = slice(part * MODES, (part + 1) * MODES)
         column = jnp.broadcast_to(springs_ref[:, rows], (MODES, MODES)).T
-        total_ref[rows, :] = column * own_ref[rows, :]
+        total_ref[rows, :] = column * basis_refs[0][rows, :]
     for rows, target in halves():
         total_ref[rows, :] += total[target, :]
     sorted_total = jnp.concatenate([total_ref[rows, :] for rows, _ in halves()], axis=0)
@@ -142,33 +141,43 @@
     for k, step in enumerate(steps):
         link = jnp.where(away == step, k, link)
     place = (link * BR_DEV + tile_rows) * BR_DEV + tile_offset
+    place = jnp.where(jnp.arange(CAP, dtype=jnp.int32) < tile_count[0], place, CAP)
+    blocks = tangent_blocks.reshape(CAP // 8, 8, HALF, 128).transpose(0, 2, 1, 3).reshape(CAP * HALF, 128)
 
     smem = pl.BlockSpec(memory_space=pltpu.SMEM)
     vmem = pl.BlockSpec(memory_space=pltpu.VMEM)
     half, full = jnp.bfloat16, jnp.float32
     params = pltpu.CompilerParams(vmem_limit_bytes=32 * 2**20)
 
-    high, low, turned_high, turned_low, weight_high, weight_low = pl.pallas_call(
-        assemble,
+    dense, turned_high, turned_low = pl.pallas_call(
+        sum_slots,
+        out_shape=(
+            jax.ShapeDtypeStruct(((CAP + 1) * HALF, 128), full),
+            jax.ShapeDtypeStruct((MODES, ROWS), half),
+            jax.ShapeDtypeStruct((MODES, ROWS), half),
+        ),
+        in_specs=[smem] + [vmem] * 2,
+        out_specs=(vmem,) * 3,
+        scratch_shapes=[pltpu.VMEM((ROWS, MODES), full)],
+        compiler_params=params,
+        cost_estimate=pl.CostEstimate(flops=500_000, bytes_accessed=4_000_000, transcendentals=0),
+        name="sum_slots",
+    )(place, blocks, basis)
+
+    high, low, weight_high, weight_low = pl.pallas_call(
+        pack,
         out_shape=(
             jax.ShapeDtypeStruct((LINKS, ROWS, ROWS), half),
             jax.ShapeDtypeStruct((LINKS, ROWS, ROWS), half),
-            jax.ShapeDtypeStruct((MODES, ROWS), half),
-            jax.ShapeDtypeStruct((MODES, ROWS), half),
             jax.ShapeDtypeStruct((LATE, MODES, ROWS), half),
             jax.ShapeDtypeStruct((LATE, MODES, ROWS), half),
         ),
-        in_specs=[smem, smem, vmem, vmem],
-        out_specs=(vmem,) * 6,
-        scratch_shapes=[
-            pltpu.VMEM((CAP * HALF, 128), full),
-            pltpu.VMEM((CAP * HALF, 128), full),
-            pltpu.VMEM((ROWS, MODES), full),
-        ],
-        compiler_params=params,
-        cost_estimate=pl.CostEstimate(flops=10_000_000, bytes_accessed=12_000_000, transcendentals=0),
-        name="assemble",
-    )(place, tile_count, tangent_blocks, basis)
+        in_specs=[vmem] * 3,
+        out_specs=(vmem,) * 4,
+        compiler_params=params,
+        cost_estimate=pl.CostEstimate(flops=10_000_000_000, bytes_accessed=4_000_000, transcendentals=0),
+        name="pack",
+    )(dense, turned_high, turned_low)
 
     total, early = pl.pallas_call(
         project_early,

time: 38.3 us -> 41.7 us (1.089)
  waiting for transfers between devices: 8.23 us -> 14.3 us
  starting transfers between devices: 18.1 us -> 13.6 us
  local copies, waits for them, and re-layouts: 2.49 us -> 5.43 us
  Pallas kernels: 7.21 us -> 5.96 us
    ppermute x5, starting transfers between devices: 5.39 us -> 0.28 us  [swap(): return lax.ppermute(block, 'row', [(d, d ^ apart) for d in range(n)])]
    ppermute x5, waiting for transfers between devices: 7.66 us -> 12.6 us  [swap(): return lax.ppermute(block, 'row', [(d, d ^ apart) for d in range(n)])]
    unnamed x6 -> x16, local copies, waits for them, and re-layouts: 2.49 us -> 5.43 us
    pallas_call x1 -> x2, Pallas kernels: 4.21 us -> 2.97 us  [the longest x1 1.53 us: shards(): pl.pallas_call(sum_slots, out_shape=(jax.ShapeDtypeStruct(((CAP + 1) * HA...]
    ppermute x7, waiting for transfers between devices: 0.57 us -> 1.74 us  [fetch(): return lax.ppermute(block, 'row', [((d + step) % n, d) for d in range(n)])]
    select_n x0 -> x1, other arithmetic: none -> 0.71 us  [shards(): jnp.where(jnp.arange(CAP, dtype=jnp.int32) < tile_count[0], place, CAP)]
    add x1 -> x0, other arithmetic: 0.71 us -> none  [shards(): place = (link * BR_DEV + tile_rows) * BR_DEV + tile_offset]
    ppermute x7, starting transfers between devices: 12.7 us -> 13.4 us  [fetch(): return lax.ppermute(block, 'row', [((d + step) % n, d) for d in range(n)])]
  transfers between devices with their start and end apart: 12 -> 12, of which waited for: 6 -> 6; matrix products, arithmetic and copies ran while one was open for 2% -> 2% of each run, Pallas kernels for 16% -> 12%
where the time goes in v2:
time: 41.7 us; the launch traced here: 41.5 us
  waiting for transfers between devices  14.3 us (34%)
  starting transfers between devices  13.6 us (33%)
  Pallas kernels  5.96 us (14%)
  local copies, waits for them, and re-layouts  5.43 us (13%)
  between operations  1.42 us (3%)
  other arithmetic  0.72 us (2%)
    ppermute x7, starting transfers between devices, fetch(): return lax.ppermute(block, 'row', [((d + step) % n, d) for d in range(n)])  13.4 us
    ppermute x5, waiting for transfers between devices, swap(): return lax.ppermute(block, 'row', [(d, d ^ apart) for d in range(n)])  12.6 us
    unnamed x16, local copies, waits for them, and re-layouts  5.43 us
    ppermute x7, waiting for transfers between devices, fetch(): return lax.ppermute(block, 'row', [((d + step) % n, d) for d in range(n)])  1.74 us
    pallas_call x1, Pallas kernels, shards(): pl.pallas_call(sum_slots, out_shape=(jax.ShapeDtypeStruct(((CAP + 1) * HA...  1.53 us
    pallas_call x1, Pallas kernels, shards(): pl.pallas_call(pack, out_shape=(jax.ShapeDtypeStruct((LINKS, ROWS, ROWS),...  1.44 us
    pallas_call x1, Pallas kernels, shards(): pl.pallas_call(project_late, out_shape=(jax.ShapeDtypeStruct((ROWS, MODES...  1.12 us
    pallas_call x1, Pallas kernels, shards(): pl.pallas_call(project_early, out_shape=(jax.ShapeDtypeStruct((ROWS, MODE...  0.91 us
  transfers between devices with their start and end apart: 12, of which 6 were waited for; matrix products, arithmetic and copies ran while one was open for 2% of the time, Pallas kernels for 12%

profile of v2, /device:TPU:0, one launch (start us, length us, event | category | flops | bytes accessed | tf_op | source)
XLA Modules:
  0.0 41.5 jit_solution(8200861782042788607)
XLA Ops:
  0.6 5.1 %collective-permute-start.2 = (f32[256,128]{1,0:T(8,128)}, f32[256,128]{1,0:T(8,128)S(1)}, u32[]{:S(2)}, u32[]{:S(2)}) collective-permute-start(f32[256,128]{1,0:T(8,128)} %refs_0_.1), channel_id=1, source_target_pairs={{4,0},{5,1},{6,2},{7,3},{8,4},{9,5},{10,6},{11,7},{12,8},{13,9},{1... | collective-permute-start | bytes 393224 | tf_op jit(solution)/shard_map/ppermute | solution.py:132
  5.7 0.0 collective-permute-start.3
  5.7 3.7 %collective-permute-start = (f32[256,128]{1,0:T(8,128)}, f32[256,128]{1,0:T(8,128)S(1)}, u32[]{:S(2)}, u32[]{:S(2)}) collective-permute-start(f32[256,128]{1,0:T(8,128)} %refs_0_.1), channel_id=1, source_target_pairs={{1,0},{2,1},{3,2},{4,3},{5,4},{6,5},{7,6},{8,7},{9,8},{10,9},{11,1... | collective-permute-start | bytes 393224 | tf_op jit(solution)/shard_map/ppermute | solution.py:132
  9.4 0.0 collective-permute-start.1
  9.4 0.0 collective-permute-start.4
  10.1 0.7 %compare_select_fusion.9.place_ref = s32[128]{0:T(128)S(1)} fusion(s32[128]{0:T(128)} %param.12, s32[128]{0:T(128)} %param.10, s32[128,1]{0,1:T(1,128)} %param.11, s32[]{:T(128)S(6)} %axis_index.12, s32[]{:T(128)} %bitcast.12), kind=kLoop, calls=%fused_computation.10 | loop fusion | flops 4224 | bytes 2056 | tf_op jit(solution)/shard_map/jit(_where)/select_n | solution.py:144
  10.8 0.0 copy-start
  10.8 1.6 %copy-done = f32[128,4096]{1,0:T(8,128)S(1)} copy-done((f32[128,4096]{1,0:T(8,128)S(1)}, f32[128,4096]{1,0:T(8,128)}, u32[]{:S(2)}) %copy-start) | copy-done | bytes 2097176
  12.4 0.9 %copy-done.1 = f32[256,128]{1,0:T(8,128)S(1)} copy-done((f32[256,128]{1,0:T(8,128)S(1)}, f32[256,128]{1,0:T(8,128)}, u32[]{:S(2)}) %copy-start.1) | copy-done | bytes 131096
  13.3 1.5 %sum_slots.1 = (f32[4128,128]{1,0:T(8,128)S(1)}, bf16[128,256]{1,0:T(8,128)(2,1)S(1)}, bf16[128,256]{1,0:T(8,128)(2,1)S(1)}) custom-call(s32[128]{0:T(128)S(1)} %compare_select_fusion.9.place_ref, f32[4096,128]{1,0:T(8,128)S(1)} %bitcast.13, f32[256,128]{1,0:T(8,128)S(1)} %copy-done.1), custom_call_target="tpu_custom_call" | custom-call | flops 500000 | bytes 4000000 | tf_op jit(solution)/shard_map/sum_slots/pallas_call | solution.py:152
  14.8 4.6 %collective-permute-start.5 = (f32[256,128]{1,0:T(8,128)S(1)}, f32[256,128]{1,0:T(8,128)S(1)}, u32[]{:S(2)}, u32[]{:S(2)}) collective-permute-start(f32[256,128]{1,0:T(8,128)S(1)} %collective-permute-done.2.refs_3_), channel_id=1, source_target_pairs={{1,0},{2,1},{3,2},{4,3},{5,4},{6,5},{7,6},{8,7},{9,8},{10,9},{11,1... | collective-permute-start | bytes 393224 | tf_op jit(solution)/shard_map/ppermute | solution.py:132
  19.4 0.0 copy-start.7
  19.4 1.4 %pack.1 = (bf16[8,256,256]{2,1,0:T(8,128)(2,1)S(1)}, bf16[8,256,256]{2,1,0:T(8,128)(2,1)S(1)}, bf16[3,128,256]{2,1,0:T(8,128)(2,1)S(1)}, bf16[3,128,256]{2,1,0:T(8,128)(2,1)S(1)}) custom-call(f32[4128,128]{1,0:T(8,128)S(1)} %get-tuple-element.15.dense_ref, bf16[128,256]{1,0:T(8,128)(2,1)S(1)} %get-tuple-element.16.turned_high_ref, ...), custom_call_target="tpu_custom_call" | custom-call | flops 10000000000 | bytes 4000000 | tf_op jit(solution)/shard_map/pack/pallas_call | solution.py:167
  20.9 0.0 copy-start.3
  20.9 0.6 %copy-done.3 = bf16[128,256]{1,0:T(8,128)(2,1)} copy-done((bf16[128,256]{1,0:T(8,128)(2,1)}, bf16[128,256]{1,0:T(8,128)(2,1)S(1)}, u32[]{:S(2)}) %copy-start.3) | copy-done | bytes 65560
  21.5 0.6 %copy-done.5 = bf16[128,256]{1,0:T(8,128)(2,1)} copy-done((bf16[128,256]{1,0:T(8,128)(2,1)}, bf16[128,256]{1,0:T(8,128)(2,1)S(1)}, u32[]{:S(2)}) %copy-start.5) | copy-done | bytes 65560
  22.1 0.0 copy-start.4
  22.2 0.8 %copy-done.4 = bf16[128,256]{1,0:T(8,128)(2,1)S(1)} copy-done((bf16[128,256]{1,0:T(8,128)(2,1)S(1)}, bf16[128,256]{1,0:T(8,128)(2,1)}, u32[]{:S(2)}) %copy-start.4) | copy-done | bytes 65560
  23.0 0.8 %copy-done.6 = bf16[128,256]{1,0:T(8,128)(2,1)S(1)} copy-done((bf16[128,256]{1,0:T(8,128)(2,1)S(1)}, bf16[128,256]{1,0:T(8,128)(2,1)}, u32[]{:S(2)}) %copy-start.6) | copy-done | bytes 65560
  23.8 0.9 %project_early.1 = (f32[256,128]{1,0:T(8,128)S(1)}, f32[128,128]{1,0:T(8,128)S(1)}) custom-call(bf16[8,256,256]{2,1,0:T(8,128)(2,1)S(1)} %get-tuple-element.18.high_ref, bf16[8,256,256]{2,1,0:T(8,128)(2,1)S(1)} %get-tuple-element.19.low_ref, bf16[128,256]{1,0:T(8,128)(2,1)S(1)} %copy-done.4, bf16[128,256]{1,0:T(8,128)(2,1)S(1)} %copy-done.6, ...), custom_call_target="tpu_custom_call" | custom-call | flops 300000000 | bytes 2500000 | tf_op jit(solution)/shard_map/project_early/pallas_call | solution.py:182
  24.8 1.7 %collective-permute-done.6.refs_2_ = f32[256,128]{1,0:T(8,128)S(1)} collective-permute-done((f32[256,128]{1,0:T(8,128)S(1)}, f32[256,128]{1,0:T(8,128)S(1)}, u32[]{:S(2)}, u32[]{:S(2)}) %collective-permute-start.6) | collective-permute-done | bytes 131104 | tf_op jit(solution)/shard_map/ppermute | solution.py:132
  26.5 0.3 reduce_late.1
  26.8 0.1 collective-permute-start.7
  26.9 1.2 %collective-permute-done.7 = f32[64,128]{1,0:T(8,128)S(1)} collective-permute-done((f32[64,128]{1,0:T(8,128)S(1)}, f32[64,128]{1,0:T(8,128)S(1)}, u32[]{:S(2)}, u32[]{:S(2)}) %collective-permute-start.7) | collective-permute-done | bytes 32800 | tf_op jit(solution)/shard_map/ppermute | solution.py:219
  28.1 1.1 %project_late.1 = (f32[256,128]{1,0:T(8,128)}, f32[8,128]{1,0:T(8,128)S(1)}) custom-call(bf16[8,256,256]{2,1,0:T(8,128)(2,1)S(1)} %get-tuple-element.18.high_ref, bf16[8,256,256]{2,1,0:T(8,128)(2,1)S(1)} %get-tuple-element.19.low_ref, f32[256,128]{1,0:T(8,128)S(1)} %get-tuple-element.20.total_ref, f32[256,128]{1,0:T(8,128)S(1)} %collective-permute-done.4.refs_0_, ...), custom_call_target="tpu_custom_call" | custom-call | flops 160000000 | bytes 1500000 | tf_op jit(solution)/shard_map/project_late/pallas_call | solution.py:208
  29.2 2.2 %collective-permute-done.8.second_ref = f32[64,128]{1,0:T(8,128)S(1)} collective-permute-done((f32[64,128]{1,0:T(8,128)S(1)}, f32[64,128]{1,0:T(8,128)S(1)}, u32[]{:S(2)}, u32[]{:S(2)}) %collective-permute-start.8) | collective-permute-done | bytes 32800 | tf_op jit(solution)/shard_map/ppermute | solution.py:219
  31.5 3.3 %collective-permute-done.9 = f32[64,128]{1,0:T(8,128)S(1)} collective-permute-done((f32[64,128]{1,0:T(8,128)S(1)}, f32[64,128]{1,0:T(8,128)S(1)}, u32[]{:S(2)}, u32[]{:S(2)}) %collective-permute-start.9) | collective-permute-done | bytes 32800 | tf_op jit(solution)/shard_map/ppermute | solution.py:219
  34.8 0.1 collective-permute-start.10
  34.9 4.7 %collective-permute-done.10 = f32[64,128]{1,0:T(8,128)S(1)} collective-permute-done((f32[64,128]{1,0:T(8,128)S(1)}, f32[64,128]{1,0:T(8,128)S(1)}, u32[]{:S(2)}, u32[]{:S(2)}) %collective-permute-start.10) | collective-permute-done | bytes 32800 | tf_op jit(solution)/shard_map/ppermute | solution.py:219
  39.6 0.1 collective-permute-start.11
  39.7 1.1 %collective-permute-done.11.other_ref = f32[64,128]{1,0:T(8,128)S(1)} collective-permute-done((f32[64,128]{1,0:T(8,128)S(1)}, f32[64,128]{1,0:T(8,128)S(1)}, u32[]{:S(2)}, u32[]{:S(2)}) %collective-permute-start.11) | collective-permute-done | bytes 32800 | tf_op jit(solution)/shard_map/ppermute | solution.py:219
  40.8 0.6 %join.1 = f32[128,128]{1,0:T(8,128)} custom-call(s32[1]{0:T(128)} %bitcast.6.side_ref, f32[64,128]{1,0:T(8,128)S(1)} %add.41.mine_ref, f32[64,128]{1,0:T(8,128)S(1)} %collective-permute-done.11.other_ref), custom_call_target="tpu_custom_call" | custom-call | bytes 130000 | tf_op jit(solution)/shard_map/join/pallas_call | solution.py:234
  (19 shorter events, 0.1 us)
Async XLA Ops:
  0.6 14.2 %collective-permute-start.2 = (f32[256,128]{1,0:T(8,128)}, f32[256,128]{1,0:T(8,128)S(1)}, u32[]{:S(2)}, u32[]{:S(2)}) collective-permute-start(f32[256,128]{1,0:T(8,128)} %refs_0_.1), channel_id=1, source_target_pairs={{4,0},{5,1},{6,2},{7,3},{8,4},{9,5},{10,6},{11,7},{12,8},{13,9},{1... | collective-permute-start | bytes 393224 | tf_op jit(solution)/shard_map/ppermute | solution.py:132
  5.7 13.7 %collective-permute-start.3 = (f32[256,128]{1,0:T(8,128)}, f32[256,128]{1,0:T(8,128)S(1)}, u32[]{:S(2)}, u32[]{:S(2)}) collective-permute-start(f32[256,128]{1,0:T(8,128)} %refs_0_.1), channel_id=1, source_target_pairs={{12,0},{13,1},{14,2},{15,3},{0,4},{1,5},{2,6},{3,7},{4,8},{5,9},{6... | collective-permute-start | bytes 393224 | tf_op jit(solution)/shard_map/ppermute | solution.py:132
  5.7 16.4 %collective-permute-start = (f32[256,128]{1,0:T(8,128)}, f32[256,128]{1,0:T(8,128)S(1)}, u32[]{:S(2)}, u32[]{:S(2)}) collective-permute-start(f32[256,128]{1,0:T(8,128)} %refs_0_.1), channel_id=1, source_target_pairs={{1,0},{2,1},{3,2},{4,3},{5,4},{6,5},{7,6},{8,7},{9,8},{10,9},{11,1... | collective-permute-start | bytes 393224 | tf_op jit(solution)/shard_map/ppermute | solution.py:132
  9.4 12.7 %collective-permute-start.1 = (f32[256,128]{1,0:T(8,128)}, f32[256,128]{1,0:T(8,128)S(1)}, u32[]{:S(2)}, u32[]{:S(2)}) collective-permute-start(f32[256,128]{1,0:T(8,128)} %refs_0_.1), channel_id=1, source_target_pairs={{15,0},{0,1},{1,2},{2,3},{3,4},{4,5},{5,6},{6,7},{7,8},{8,9},{9,10... | collective-permute-start | bytes 393224 | tf_op jit(solution)/shard_map/ppermute | solution.py:132
  9.4 15.3 %collective-permute-start.4 = (f32[256,128]{1,0:T(8,128)}, f32[256,128]{1,0:T(8,128)S(1)}, u32[]{:S(2)}, u32[]{:S(2)}) collective-permute-start(f32[256,128]{1,0:T(8,128)} %refs_0_.1), channel_id=1, source_target_pairs={{8,0},{9,1},{10,2},{11,3},{12,4},{13,5},{14,6},{15,7},{0,8},{1,9},... | collective-permute-start | bytes 393224 | tf_op jit(solution)/shard_map/ppermute | solution.py:132
  10.8 1.6 %copy-start = (f32[128,4096]{1,0:T(8,128)S(1)}, f32[128,4096]{1,0:T(8,128)}, u32[]{:S(2)}) copy-start(f32[128,4096]{1,0:T(8,128)} %param.9) | copy-start | bytes 6291460
  12.4 0.9 %copy-start.1 = (f32[256,128]{1,0:T(8,128)S(1)}, f32[256,128]{1,0:T(8,128)}, u32[]{:S(2)}) copy-start(f32[256,128]{1,0:T(8,128)} %refs_0_.1) | copy-start | bytes 393220
  14.8 9.9 %collective-permute-start.5 = (f32[256,128]{1,0:T(8,128)S(1)}, f32[256,128]{1,0:T(8,128)S(1)}, u32[]{:S(2)}, u32[]{:S(2)}) collective-permute-start(f32[256,128]{1,0:T(8,128)S(1)} %collective-permute-done.2.refs_3_), channel_id=1, source_target_pairs={{1,0},{2,1},{3,2},{4,3},{5,4},{6,5},{7,6},{8,7},{9,8},{10,9},{11,1... | collective-permute-start | bytes 393224 | tf_op jit(solution)/shard_map/ppermute | solution.py:132
  19.4 7.1 %collective-permute-start.6 = (f32[256,128]{1,0:T(8,128)S(1)}, f32[256,128]{1,0:T(8,128)S(1)}, u32[]{:S(2)}, u32[]{:S(2)}) collective-permute-start(f32[256,128]{1,0:T(8,128)S(1)} %collective-permute-done.3.refs_4_), channel_id=1, source_target_pairs={{15,0},{0,1},{1,2},{2,3},{3,4},{4,5},{5,6},{6,7},{7,8},{8,9},{9,10... | collective-permute-start | bytes 393224 | tf_op jit(solution)/shard_map/ppermute | solution.py:132
  19.4 2.7 %copy-start.2 = (f32[256,128]{1,0:T(8,128)S(1)}, f32[256,128]{1,0:T(8,128)}, u32[]{:S(2)}) copy-start(f32[256,128]{1,0:T(8,128)} %refs_0_.1) | copy-start | bytes 393220
  19.4 2.7 %copy-start.7 = (f32[256]{0:T(256)S(1)}, f32[256]{0:T(256)}, u32[]{:S(2)}) copy-start(f32[256]{0:T(256)} %param.8) | copy-start | bytes 3076
  20.9 0.6 %copy-start.3 = (bf16[128,256]{1,0:T(8,128)(2,1)}, bf16[128,256]{1,0:T(8,128)(2,1)S(1)}, u32[]{:S(2)}) copy-start(bf16[128,256]{1,0:T(8,128)(2,1)S(1)} %get-tuple-element.16.turned_high_ref) | copy-start | bytes 196612
  21.5 0.6 %copy-start.5 = (bf16[128,256]{1,0:T(8,128)(2,1)}, bf16[128,256]{1,0:T(8,128)(2,1)S(1)}, u32[]{:S(2)}) copy-start(bf16[128,256]{1,0:T(8,128)(2,1)S(1)} %get-tuple-element.17.turned_low_ref) | copy-start | bytes 196612
  22.1 0.8 %copy-start.4 = (bf16[128,256]{1,0:T(8,128)(2,1)S(1)}, bf16[128,256]{1,0:T(8,128)(2,1)}, u32[]{:S(2)}) copy-start(bf16[128,256]{1,0:T(8,128)(2,1)} %copy-done.3) | copy-start | bytes 196612
  23.0 0.8 %copy-start.6 = (bf16[128,256]{1,0:T(8,128)(2,1)S(1)}, bf16[128,256]{1,0:T(8,128)(2,1)}, u32[]{:S(2)}) copy-start(bf16[128,256]{1,0:T(8,128)(2,1)} %copy-done.5) | copy-start | bytes 196612
  26.8 1.3 %collective-permute-start.7 = (f32[64,128]{1,0:T(8,128)S(1)}, f32[64,128]{1,0:T(8,128)S(1)}, u32[]{:S(2)}, u32[]{:S(2)}) collective-permute-start(f32[64,128]{1,0:T(8,128)S(1)} %get-tuple-element.26), channel_id=1, source_target_pairs={{0,1},{1,0},{2,3},{3,2},{4,5},{5,4},{6,7},{7,6},{8,9},{9,8},{10,11... | collective-permute-start | bytes 98312 | tf_op jit(solution)/shard_map/ppermute | solution.py:219
  28.1 3.3 %collective-permute-start.8 = (f32[64,128]{1,0:T(8,128)S(1)}, f32[64,128]{1,0:T(8,128)S(1)}, u32[]{:S(2)}, u32[]{:S(2)}) collective-permute-start(f32[64,128]{1,0:T(8,128)S(1)} %add.39.first_ref), channel_id=1, source_target_pairs={{0,3},{1,2},{2,1},{3,0},{4,7},{5,6},{6,5},{7,4},{8,11},{9,10},{10,... | collective-permute-start | bytes 98312 | tf_op jit(solution)/shard_map/ppermute | solution.py:219
  31.4 3.3 %collective-permute-start.9 = (f32[64,128]{1,0:T(8,128)S(1)}, f32[64,128]{1,0:T(8,128)S(1)}, u32[]{:S(2)}, u32[]{:S(2)}) collective-permute-start(f32[64,128]{1,0:T(8,128)S(1)} %add_after.1), channel_id=1, source_target_pairs={{0,5},{1,4},{2,7},{3,6},{4,1},{5,0},{6,3},{7,2},{8,13},{9,12},{10,... | collective-permute-start | bytes 98312 | tf_op jit(solution)/shard_map/ppermute | solution.py:219
  34.8 4.8 %collective-permute-start.10 = (f32[64,128]{1,0:T(8,128)S(1)}, f32[64,128]{1,0:T(8,128)S(1)}, u32[]{:S(2)}, u32[]{:S(2)}) collective-permute-start(f32[64,128]{1,0:T(8,128)S(1)} %add.40), channel_id=1, source_target_pairs={{0,9},{1,8},{2,11},{3,10},{4,13},{5,12},{6,15},{7,14},{8,1},{9,0},... | collective-permute-start | bytes 98312 | tf_op jit(solution)/shard_map/ppermute | solution.py:219
  39.6 1.2 %collective-permute-start.11 = (f32[64,128]{1,0:T(8,128)S(1)}, f32[64,128]{1,0:T(8,128)S(1)}, u32[]{:S(2)}, u32[]{:S(2)}) collective-permute-start(f32[64,128]{1,0:T(8,128)S(1)} %add.41.mine_ref), channel_id=1, source_target_pairs={{0,1},{1,0},{2,3},{3,2},{4,5},{5,4},{6,7},{7,6},{8,9},{9,8},{10,11... | collective-permute-start | bytes 98312 | tf_op jit(solution)/shard_map/ppermute | solution.py:219

commit v3 on v1

--- a/solution.py
+++ b/solution.py
@@ -33,24 +33,30 @@
             yield pl.ds(r * B + h, HALF, stride=2), slice(r * B + h * HALF, r * B + (h + 1) * HALF)
 
 
-def assemble(place_ref, count_ref, blocks_ref, basis_ref, high_ref, low_ref, turned_high_ref, turned_low_ref, weight_high_ref, weight_low_ref, slots, dense, sorted_basis):
+def prepare(basis_ref, held_ref):
+    held_ref[...] = basis_ref[...]
+
+
+def assemble(count_ref, rows_ref, owner_ref, offset_ref, blocks_ref, high_ref, low_ref, dense, placed, place, arrived):
+    n = lax.axis_size("row")
+    away = lax.rem(owner_ref[...].reshape(1, CAP) - lax.axis_index("row") + n, n)
+    link = jnp.zeros_like(away)
+    for k, step in enumerate(steps(n)):
+        link = jnp.where(away == step, k, link)
+    target = (link * BR_DEV + rows_ref[...].reshape(1, CAP)) * BR_DEV + offset_ref[...].reshape(1, CAP)
+    slot = lax.broadcasted_iota(jnp.int32, (1, CAP), 1)
+    placed[...] = jnp.where(slot < count_ref[0], target, CAP)
+    copy = pltpu.make_async_copy(placed, place, arrived)
+    copy.start()
     dense[...] = jnp.zeros_like(dense)
-    for rows, target in halves():
-        sorted_basis[target, :] = basis_ref[rows, :]
-    turned_high, turned_low = split(sorted_basis[...].T)
-    turned_high_ref[...] = turned_high
-    turned_low_ref[...] = turned_low
+    copy.wait()
 
     @pl.loop(0, CAP // 8)
     def _(group):
-        eight = blocks_ref[pl.ds(pl.multiple_of(group * 8, 8), 8), :]
-        for t in range(HALF):
-            slots[pl.ds(group * (8 * HALF) + t, 8, stride=HALF), :] = eight[:, t * 128:(t + 1) * 128]
-
-    @pl.loop(0, count_ref[0])
-    def _(s):
-        target = pl.ds(pl.multiple_of(place_ref[s] * HALF, HALF), HALF)
-        dense[target, :] += slots[pl.ds(pl.multiple_of(s * HALF, HALF), HALF), :]
+        for k in range(8):
+            block = blocks_ref[pl.ds(group * (8 * HALF) + k, HALF, stride=8), :]
+            target = pl.ds(pl.multiple_of(place[0, group * 8 + k] * HALF, HALF), HALF)
+            dense[target, :] += block
 
     left = lax.broadcasted_iota(jnp.int32, (HALF, 128), 1) < B
 
@@ -69,17 +75,20 @@
                     high_ref[link, rows, pair * 128:(pair + 1) * 128] = high
                     low_ref[link, rows, pair * 128:(pair + 1) * 128] = low
 
+
+def project_early(high_ref, low_ref, springs_ref, *refs):
+    basis_refs, (total_ref, partial_ref, weight_high_ref, weight_low_ref, sorted_rows) = refs[:-5], refs[-5:]
+    own_ref = basis_refs[0]
+    for rows, target in halves():
+        sorted_rows[target, :] = own_ref[rows, :]
+    turned_high, turned_low = split(sorted_rows[...].T)
     for k in range(LATE):
         link = LINKS - LATE + k
         high, low = split(dot3(turned_high, turned_low, high_ref[link], low_ref[link]))
         weight_high_ref[k] = high
         weight_low_ref[k] = low
-
-
-def project_early(high_ref, low_ref, turned_high_ref, turned_low_ref, springs_ref, own_ref, *refs):
-    basis_refs, (total_ref, partial_ref) = refs[:-2], refs[-2:]
     total = jnp.zeros((ROWS, MODES), jnp.float32)
-    for link, ref in enumerate((own_ref,) + basis_refs):
+    for link, ref in enumerate(basis_refs):
         b_high, b_low = split(ref[...])
         total += dot3(high_ref[link], low_ref[link], b_high, b_low)
     for part in range(ROWS // MODES):
@@ -88,8 +97,8 @@
         total_ref[rows, :] = column * own_ref[rows, :]
     for rows, target in halves():
         total_ref[rows, :] += total[target, :]
-    sorted_total = jnp.concatenate([total_ref[rows, :] for rows, _ in halves()], axis=0)
-    partial_ref[...] = dot3(turned_high_ref[...], turned_low_ref[...], *split(sorted_total))
+        sorted_rows[target, :] = total_ref[rows, :]
+    partial_ref[...] = dot3(turned_high, turned_low, *split(sorted_rows[...]))
 
 
 def reduce_late(scale, side_ref, weight_high_ref, weight_low_ref, early_ref, *refs):
@@ -124,61 +133,71 @@
     done_ref[...] = jnp.zeros_like(done_ref)
 
 
+def steps(n):
+    return (0, 1, n - 1, 4, n - 4, n // 2, 5, n - 5)
+
+
 def shards(basis, springs, tangent_blocks, tile_rows, tile_owner, tile_offset, tile_count):
     n = lax.axis_size("row")
     me = lax.axis_index("row")
-    steps = (0, 1, n - 1, 4, n - 4, n // 2, 5, n - 5)
-
-    def fetch(block, step):
-        return lax.ppermute(block, "row", [((d + step) % n, d) for d in range(n)])
-
-    above, below = fetch(basis, 4), fetch(basis, n - 4)
-    across = fetch(basis, n // 2)
-    after, before = fetch(basis, 1), fetch(basis, n - 1)
-    far_above, far_below = fetch(above, 1), fetch(below, n - 1)
-
-    away = (tile_owner[:, 0] - me + n) % n
-    link = jnp.zeros_like(away)
-    for k, step in enumerate(steps):
-        link = jnp.where(away == step, k, link)
-    place = (link * BR_DEV + tile_rows) * BR_DEV + tile_offset
-
     smem = pl.BlockSpec(memory_space=pltpu.SMEM)
     vmem = pl.BlockSpec(memory_space=pltpu.VMEM)
     half, full = jnp.bfloat16, jnp.float32
     params = pltpu.CompilerParams(vmem_limit_bytes=32 * 2**20)
 
-    high, low, turned_high, turned_low, weight_high, weight_low = pl.pallas_call(
+    held = pl.pallas_call(
+        prepare,
+        out_shape=jax.ShapeDtypeStruct((ROWS, MODES), full),
+        in_specs=[vmem],
+        out_specs=vmem,
+        compiler_params=params,
+        cost_estimate=pl.CostEstimate(flops=10_000_000_000, bytes_accessed=300_000, transcendentals=0),
+        name="prepare",
+    )(basis)
+
+    def fetch(block, step):
+        return lax.ppermute(block, "row", [((d + step) % n, d) for d in range(n)])
+
+    above, below = fetch(held, 4), fetch(held, n - 4)
+    across = fetch(held, n // 2)
+    after, before = fetch(held, 1), fetch(held, n - 1)
+    far_above, far_below = fetch(above, 1), fetch(below, n - 1)
+
+    blocks = tangent_blocks.reshape(CAP // 8, 8, HALF, 128).transpose(0, 2, 1, 3).reshape(CAP * HALF, 128)
+    high, low = pl.pallas_call(
         assemble,
         out_shape=(
             jax.ShapeDtypeStruct((LINKS, ROWS, ROWS), half),
             jax.ShapeDtypeStruct((LINKS, ROWS, ROWS), half),
-            jax.ShapeDtypeStruct((MODES, ROWS), half),
-            jax.ShapeDtypeStruct((MODES, ROWS), half),
+        ),
+        in_specs=[smem] + [vmem] * 4,
+        out_specs=(vmem,) * 2,
+        scratch_shapes=[
+            pltpu.VMEM(((CAP + 1) * HALF, 128), full),
+            pltpu.VMEM((1, CAP), jnp.int32),
+            pltpu.SMEM((1, CAP), jnp.int32),
+            pltpu.SemaphoreType.DMA(()),
+        ],
+        compiler_params=params,
+        cost_estimate=pl.CostEstimate(flops=10_000_000, bytes_accessed=8_000_000, transcendentals=0),
+        name="assemble",
+    )(tile_count, tile_rows, tile_owner[:, 0], tile_offset, blocks)
+
+    total, early, weight_high, weight_low = pl.pallas_call(
+        project_early,
+        out_shape=(
+            jax.ShapeDtypeStruct((ROWS, MODES), full),
+            jax.ShapeDtypeStruct((MODES, MODES), full),
             jax.ShapeDtypeStruct((LATE, MODES, ROWS), half),
             jax.ShapeDtypeStruct((LATE, MODES, ROWS), half),
         ),
-        in_specs=[smem, smem, vmem, vmem],
-        out_specs=(vmem,) * 6,
-        scratch_shapes=[
-            pltpu.VMEM((CAP * HALF, 128), full),
-            pltpu.VMEM((CAP * HALF, 128), full),
-            pltpu.VMEM((ROWS, MODES), full),
-        ],
-        compiler_params=params,
-        cost_estimate=pl.CostEstimate(flops=10_000_000, bytes_accessed=12_000_000, transcendentals=0),
-        name="assemble",
-    )(place, tile_count, tangent_blocks, basis)
-
-    total, early = pl.pallas_call(
-        project_early,
-        out_shape=(jax.ShapeDtypeStruct((ROWS, MODES), full), jax.ShapeDtypeStruct((MODES, MODES), full)),
-        in_specs=[vmem] * (5 + LINKS - LATE),
-        out_specs=(vmem,) * 2,
+        in_specs=[vmem] * (3 + LINKS - LATE),
+        out_specs=(vmem,) * 4,
+        scratch_shapes=[pltpu.VMEM((ROWS, MODES), full)],
         compiler_params=params,
         cost_estimate=pl.CostEstimate(flops=300_000_000, bytes_accessed=2_500_000, transcendentals=0),
         name="project_early",
-    )(high, low, turned_high, turned_low, springs.reshape(1, ROWS), basis, after, before, above, below)
+    )(high, low, springs.reshape(1, ROWS), held, after, before, above, below)
 
     side = me
     for shift in (8, 4, 2, 1):

time: 38.3 us -> 37.3 us (0.974)
  waiting for transfers between devices: 8.23 us -> 13.4 us
  starting transfers between devices: 18.1 us -> 15.4 us
  Pallas kernels: 7.21 us -> 5.77 us
  local copies, waits for them, and re-layouts: 2.49 us -> 1.07 us
  other arithmetic: 0.72 us -> 0.02 us
    ppermute x5, starting transfers between devices: 5.39 us -> 2.44 us  [swap(): return lax.ppermute(block, 'row', [(d, d ^ apart) for d in range(n)])]
    ppermute x5, waiting for transfers between devices: 7.66 us -> 10.4 us  [swap(): return lax.ppermute(block, 'row', [(d, d ^ apart) for d in range(n)])]
    ppermute x7, waiting for transfers between devices: 0.57 us -> 3.02 us  [fetch(): return lax.ppermute(block, 'row', [((d + step) % n, d) for d in range(n)])]
    pallas_call x1, Pallas kernels: 4.21 us -> 2.54 us  [shards(): pl.pallas_call(assemble, out_shape=(jax.ShapeDtypeStruct((LINKS, ROWS, RO...]
    unnamed x6 -> x12, local copies, waits for them, and re-layouts: 2.49 us -> 1.07 us
    add x1 -> x0, other arithmetic: 0.71 us -> none  [shards(): place = (link * BR_DEV + tile_rows) * BR_DEV + tile_offset]
  transfers between devices with their start and end apart: 12 -> 12, of which waited for: 6 -> 8; matrix products, arithmetic and copies ran while one was open for 2% -> 0% of each run, Pallas kernels for 16% -> 13%
where the time goes in v3:
time: 37.3 us; the launch traced here: 37.1 us
  starting transfers between devices  15.4 us (41%)
  waiting for transfers between devices  13.4 us (36%)
  Pallas kernels  5.77 us (15%)
  between operations  1.44 us (4%)
  local copies, waits for them, and re-layouts  1.07 us (3%)
    ppermute x7, starting transfers between devices, fetch(): return lax.ppermute(block, 'row', [((d + step) % n, d) for d in range(n)])  13 us
    ppermute x5, waiting for transfers between devices, swap(): return lax.ppermute(block, 'row', [(d, d ^ apart) for d in range(n)])  10.4 us
    ppermute x7, waiting for transfers between devices, fetch(): return lax.ppermute(block, 'row', [((d + step) % n, d) for d in range(n)])  3.02 us
    pallas_call x1, Pallas kernels, shards(): pl.pallas_call(assemble, out_shape=(jax.ShapeDtypeStruct((LINKS, ROWS, RO...  2.54 us
    ppermute x5, starting transfers between devices, swap(): return lax.ppermute(block, 'row', [(d, d ^ apart) for d in range(n)])  2.44 us
    pallas_call x1, Pallas kernels, shards(): pl.pallas_call(project_early, out_shape=(jax.ShapeDtypeStruct((ROWS, MODE...  1.13 us
    pallas_call x1, Pallas kernels, shards(): pl.pallas_call(project_late, out_shape=(jax.ShapeDtypeStruct((ROWS, MODES...  1.13 us
    unnamed x12, local copies, waits for them, and re-layouts  1.07 us
  transfers between devices with their start and end apart: 12, of which 8 were waited for; matrix products, arithmetic and copies ran while one was open for 0% of the time, Pallas kernels for 13%

profile of v3, /device:TPU:0, one launch (start us, length us, event | category | flops | bytes accessed | tf_op | source)
XLA Modules:
  0.0 37.1 jit_solution(6757836936936786049)
XLA Ops:
  0.6 0.0 copy-start.3
  0.7 1.0 %copy-done.5 = f32[256,128]{1,0:T(8,128)S(1)} copy-done((f32[256,128]{1,0:T(8,128)S(1)}, f32[256,128]{1,0:T(8,128)}, u32[]{:S(2)}) %copy-start.5) | copy-done | bytes 131096
  1.7 0.0 copy-start.1
  1.7 5.1 %collective-permute-start.2 = (f32[256,128]{1,0:T(8,128)S(1)}, f32[256,128]{1,0:T(8,128)S(1)}, u32[]{:S(2)}, u32[]{:S(2)}) collective-permute-start(f32[256,128]{1,0:T(8,128)S(1)} %prepare.1.refs_0_), channel_id=1, source_target_pairs={{4,0},{5,1},{6,2},{7,3},{8,4},{9,5},{10,6},{11,7},{12,8},{13,9},{1... | collective-permute-start | bytes 393224 | tf_op jit(solution)/shard_map/ppermute | solution.py:159
  6.8 0.0 collective-permute-start.3
  6.9 3.7 %collective-permute-start = (f32[256,128]{1,0:T(8,128)S(1)}, f32[256,128]{1,0:T(8,128)S(1)}, u32[]{:S(2)}, u32[]{:S(2)}) collective-permute-start(f32[256,128]{1,0:T(8,128)S(1)} %prepare.1.refs_0_), channel_id=1, source_target_pairs={{1,0},{2,1},{3,2},{4,3},{5,4},{6,5},{7,6},{8,7},{9,8},{10,9},{11,1... | collective-permute-start | bytes 393224 | tf_op jit(solution)/shard_map/ppermute | solution.py:159
  10.5 0.0 collective-permute-start.1
  10.5 0.0 collective-permute-start.4
  10.5 0.2 collective-permute-done.2.refs_3_
  10.8 4.2 %collective-permute-start.5 = (f32[256,128]{1,0:T(8,128)S(1)}, f32[256,128]{1,0:T(8,128)S(1)}, u32[]{:S(2)}, u32[]{:S(2)}) collective-permute-start(f32[256,128]{1,0:T(8,128)S(1)} %collective-permute-done.2.refs_3_), channel_id=1, source_target_pairs={{1,0},{2,1},{3,2},{4,3},{5,4},{6,5},{7,6},{8,7},{9,8},{10,9},{11,1... | collective-permute-start | bytes 393224 | tf_op jit(solution)/shard_map/ppermute | solution.py:159
  15.0 0.0 collective-permute-done.3.refs_4_
  15.0 0.0 collective-permute-start.6
  15.7 2.5 %assemble.1 = (bf16[8,256,256]{2,1,0:T(8,128)(2,1)S(1)}, bf16[8,256,256]{2,1,0:T(8,128)(2,1)S(1)}) custom-call(s32[1]{0:T(128)S(6)} %copy.9.count_ref, s32[128]{0:T(128)S(1)} %copy-done.2, s32[128]{0:T(128)S(1)} %bitcast.10, s32[128]{0:T(128)S(1)} %copy-done.4, f32[4096,128]{1,0:T(8,128)S(1)} %bitcast.8), custom_call_target="tpu_custom_call" | custom-call | flops 10000000 | bytes 8000000 | tf_op jit(solution)/shard_map/assemble/pallas_call | solution.py:167
  18.2 0.0 collective-permute-done.refs_1_
  18.2 0.0 collective-permute-done.1.refs_2_
  18.2 1.1 %project_early.1 = (f32[256,128]{1,0:T(8,128)S(1)}, f32[128,128]{1,0:T(8,128)S(1)}, bf16[3,128,256]{2,1,0:T(8,128)(2,1)S(1)}, bf16[3,128,256]{2,1,0:T(8,128)(2,1)S(1)}) custom-call(bf16[8,256,256]{2,1,0:T(8,128)(2,1)S(1)} %get-tuple-element.12.high_ref, bf16[8,256,256]{2,1,0:T(8,128)(2,1)S(1)} %get-tuple-element.13.low_ref, f32[1,256]{1,0:T(1,128)S(1)} %bitcast.9, ...), custom_call_target="tpu_custom_call" | custom-call | flops 300000000 | bytes 2500000 | tf_op jit(solution)/shard_map/project_early/pallas_call | solution.py:186
  19.4 0.2 collective-permute-done.4.refs_0_
  19.6 0.0 collective-permute-done.5.refs_1_
  19.6 2.6 %collective-permute-done.6.refs_2_ = f32[256,128]{1,0:T(8,128)S(1)} collective-permute-done((f32[256,128]{1,0:T(8,128)S(1)}, f32[256,128]{1,0:T(8,128)S(1)}, u32[]{:S(2)}, u32[]{:S(2)}) %collective-permute-start.6) | collective-permute-done | bytes 131104 | tf_op jit(solution)/shard_map/ppermute | solution.py:159
  22.2 0.3 reduce_late.1
  22.5 0.1 collective-permute-start.7
  22.6 1.2 %collective-permute-done.7 = f32[64,128]{1,0:T(8,128)S(1)} collective-permute-done((f32[64,128]{1,0:T(8,128)S(1)}, f32[64,128]{1,0:T(8,128)S(1)}, u32[]{:S(2)}, u32[]{:S(2)}) %collective-permute-start.7) | collective-permute-done | bytes 32800 | tf_op jit(solution)/shard_map/ppermute | solution.py:229
  23.8 1.1 %collective-permute-start.8 = (f32[64,128]{1,0:T(8,128)S(1)}, f32[64,128]{1,0:T(8,128)S(1)}, u32[]{:S(2)}, u32[]{:S(2)}) collective-permute-start(f32[64,128]{1,0:T(8,128)S(1)} %add.9.first_ref), channel_id=1, source_target_pairs={{0,3},{1,2},{2,1},{3,0},{4,7},{5,6},{6,5},{7,4},{8,11},{9,10},{10,... | collective-permute-start | bytes 98312 | tf_op jit(solution)/shard_map/ppermute | solution.py:229
  24.9 1.1 %project_late.1 = (f32[256,128]{1,0:T(8,128)}, f32[8,128]{1,0:T(8,128)S(1)}) custom-call(bf16[8,256,256]{2,1,0:T(8,128)(2,1)S(1)} %get-tuple-element.12.high_ref, bf16[8,256,256]{2,1,0:T(8,128)(2,1)S(1)} %get-tuple-element.13.low_ref, f32[256,128]{1,0:T(8,128)S(1)} %get-tuple-element.14.total_ref, f32[256,128]{1,0:T(8,128)S(1)} %collective-permute-done.4.refs_0_, ...), custom_call_target="tpu_custom_call" | custom-call | flops 160000000 | bytes 1500000 | tf_op jit(solution)/shard_map/project_late/pallas_call | solution.py:218
  26.0 1.1 %collective-permute-done.8.second_ref = f32[64,128]{1,0:T(8,128)S(1)} collective-permute-done((f32[64,128]{1,0:T(8,128)S(1)}, f32[64,128]{1,0:T(8,128)S(1)}, u32[]{:S(2)}, u32[]{:S(2)}) %collective-permute-start.8) | collective-permute-done | bytes 32800 | tf_op jit(solution)/shard_map/ppermute | solution.py:229
  27.1 0.0 collective-permute-start.9
  27.1 3.3 %collective-permute-done.9 = f32[64,128]{1,0:T(8,128)S(1)} collective-permute-done((f32[64,128]{1,0:T(8,128)S(1)}, f32[64,128]{1,0:T(8,128)S(1)}, u32[]{:S(2)}, u32[]{:S(2)}) %collective-permute-start.9) | collective-permute-done | bytes 32800 | tf_op jit(solution)/shard_map/ppermute | solution.py:229
  30.5 1.2 %collective-permute-start.10 = (f32[64,128]{1,0:T(8,128)S(1)}, f32[64,128]{1,0:T(8,128)S(1)}, u32[]{:S(2)}, u32[]{:S(2)}) collective-permute-start(f32[64,128]{1,0:T(8,128)S(1)} %add.10), channel_id=1, source_target_pairs={{0,9},{1,8},{2,11},{3,10},{4,13},{5,12},{6,15},{7,14},{8,1},{9,0},... | collective-permute-start | bytes 98312 | tf_op jit(solution)/shard_map/ppermute | solution.py:229
  31.6 3.7 %collective-permute-done.10 = f32[64,128]{1,0:T(8,128)S(1)} collective-permute-done((f32[64,128]{1,0:T(8,128)S(1)}, f32[64,128]{1,0:T(8,128)S(1)}, u32[]{:S(2)}, u32[]{:S(2)}) %collective-permute-start.10) | collective-permute-done | bytes 32800 | tf_op jit(solution)/shard_map/ppermute | solution.py:229
  35.3 0.1 collective-permute-start.11
  35.4 1.1 %collective-permute-done.11.other_ref = f32[64,128]{1,0:T(8,128)S(1)} collective-permute-done((f32[64,128]{1,0:T(8,128)S(1)}, f32[64,128]{1,0:T(8,128)S(1)}, u32[]{:S(2)}, u32[]{:S(2)}) %collective-permute-start.11) | collective-permute-done | bytes 32800 | tf_op jit(solution)/shard_map/ppermute | solution.py:229
  36.5 0.6 %join.1 = f32[128,128]{1,0:T(8,128)} custom-call(s32[1]{0:T(128)} %bitcast.5.side_ref, f32[64,128]{1,0:T(8,128)S(1)} %add.11.mine_ref, f32[64,128]{1,0:T(8,128)S(1)} %collective-permute-done.11.other_ref), custom_call_target="tpu_custom_call" | custom-call | bytes 130000 | tf_op jit(solution)/shard_map/join/pallas_call | solution.py:244
  (14 shorter events, 0.0 us)
Async XLA Ops:
  0.6 15.0 %copy-start.3 = (s32[128,1]{0,1:T(1,128)S(1)}, s32[128,1]{0,1:T(1,128)}, u32[]{:S(2)}) copy-start(s32[128,1]{0,1:T(1,128)} %param.11) | copy-start | bytes 1540
  0.6 15.0 %copy-start = (f32[128,4096]{1,0:T(8,128)S(1)}, f32[128,4096]{1,0:T(8,128)}, u32[]{:S(2)}) copy-start(f32[128,4096]{1,0:T(8,128)} %param.9) | copy-start | bytes 6291460
  0.7 15.0 %copy-start.2 = (s32[128]{0:T(128)S(1)}, s32[128]{0:T(128)}, u32[]{:S(2)}) copy-start(s32[128]{0:T(128)} %rows_ref.1) | copy-start | bytes 1540
  0.7 15.0 %copy-start.4 = (s32[128]{0:T(128)S(1)}, s32[128]{0:T(128)}, u32[]{:S(2)}) copy-start(s32[128]{0:T(128)} %offset_ref.1) | copy-start | bytes 1540
  0.7 1.1 %copy-start.5 = (f32[256,128]{1,0:T(8,128)S(1)}, f32[256,128]{1,0:T(8,128)}, u32[]{:S(2)}) copy-start(f32[256,128]{1,0:T(8,128)} %basis_ref.1) | copy-start | bytes 393220
  1.7 16.5 %copy-start.1 = (f32[256]{0:T(256)S(1)}, f32[256]{0:T(256)}, u32[]{:S(2)}) copy-start(f32[256]{0:T(256)} %param.8) | copy-start | bytes 3076
  1.7 9.0 %collective-permute-start.2 = (f32[256,128]{1,0:T(8,128)S(1)}, f32[256,128]{1,0:T(8,128)S(1)}, u32[]{:S(2)}, u32[]{:S(2)}) collective-permute-start(f32[256,128]{1,0:T(8,128)S(1)} %prepare.1.refs_0_), channel_id=1, source_target_pairs={{4,0},{5,1},{6,2},{7,3},{8,4},{9,5},{10,6},{11,7},{12,8},{13,9},{1... | collective-permute-start | bytes 393224 | tf_op jit(solution)/shard_map/ppermute | solution.py:159
  6.8 8.1 %collective-permute-start.3 = (f32[256,128]{1,0:T(8,128)S(1)}, f32[256,128]{1,0:T(8,128)S(1)}, u32[]{:S(2)}, u32[]{:S(2)}) collective-permute-start(f32[256,128]{1,0:T(8,128)S(1)} %prepare.1.refs_0_), channel_id=1, source_target_pairs={{12,0},{13,1},{14,2},{15,3},{0,4},{1,5},{2,6},{3,7},{4,8},{5,9},{6... | collective-permute-start | bytes 393224 | tf_op jit(solution)/shard_map/ppermute | solution.py:159
  6.9 11.4 %collective-permute-start = (f32[256,128]{1,0:T(8,128)S(1)}, f32[256,128]{1,0:T(8,128)S(1)}, u32[]{:S(2)}, u32[]{:S(2)}) collective-permute-start(f32[256,128]{1,0:T(8,128)S(1)} %prepare.1.refs_0_), channel_id=1, source_target_pairs={{1,0},{2,1},{3,2},{4,3},{5,4},{6,5},{7,6},{8,7},{9,8},{10,9},{11,1... | collective-permute-start | bytes 393224 | tf_op jit(solution)/shard_map/ppermute | solution.py:159
  10.5 7.7 %collective-permute-start.1 = (f32[256,128]{1,0:T(8,128)S(1)}, f32[256,128]{1,0:T(8,128)S(1)}, u32[]{:S(2)}, u32[]{:S(2)}) collective-permute-start(f32[256,128]{1,0:T(8,128)S(1)} %prepare.1.refs_0_), channel_id=1, source_target_pairs={{15,0},{0,1},{1,2},{2,3},{3,4},{4,5},{5,6},{6,7},{7,8},{8,9},{9,10... | collective-permute-start | bytes 393224 | tf_op jit(solution)/shard_map/ppermute | solution.py:159
  10.5 9.0 %collective-permute-start.4 = (f32[256,128]{1,0:T(8,128)S(1)}, f32[256,128]{1,0:T(8,128)S(1)}, u32[]{:S(2)}, u32[]{:S(2)}) collective-permute-start(f32[256,128]{1,0:T(8,128)S(1)} %prepare.1.refs_0_), channel_id=1, source_target_pairs={{8,0},{9,1},{10,2},{11,3},{12,4},{13,5},{14,6},{15,7},{0,8},{1,9},... | collective-permute-start | bytes 393224 | tf_op jit(solution)/shard_map/ppermute | solution.py:159
  10.8 8.8 %collective-permute-start.5 = (f32[256,128]{1,0:T(8,128)S(1)}, f32[256,128]{1,0:T(8,128)S(1)}, u32[]{:S(2)}, u32[]{:S(2)}) collective-permute-start(f32[256,128]{1,0:T(8,128)S(1)} %collective-permute-done.2.refs_3_), channel_id=1, source_target_pairs={{1,0},{2,1},{3,2},{4,3},{5,4},{6,5},{7,6},{8,7},{9,8},{10,9},{11,1... | collective-permute-start | bytes 393224 | tf_op jit(solution)/shard_map/ppermute | solution.py:159
  15.0 7.2 %collective-permute-start.6 = (f32[256,128]{1,0:T(8,128)S(1)}, f32[256,128]{1,0:T(8,128)S(1)}, u32[]{:S(2)}, u32[]{:S(2)}) collective-permute-start(f32[256,128]{1,0:T(8,128)S(1)} %collective-permute-done.3.refs_4_), channel_id=1, source_target_pairs={{15,0},{0,1},{1,2},{2,3},{3,4},{4,5},{5,6},{6,7},{7,8},{8,9},{9,10... | collective-permute-start | bytes 393224 | tf_op jit(solution)/shard_map/ppermute | solution.py:159
  22.5 1.3 %collective-permute-start.7 = (f32[64,128]{1,0:T(8,128)S(1)}, f32[64,128]{1,0:T(8,128)S(1)}, u32[]{:S(2)}, u32[]{:S(2)}) collective-permute-start(f32[64,128]{1,0:T(8,128)S(1)} %get-tuple-element.20), channel_id=1, source_target_pairs={{0,1},{1,0},{2,3},{3,2},{4,5},{5,4},{6,7},{7,6},{8,9},{9,8},{10,11... | collective-permute-start | bytes 98312 | tf_op jit(solution)/shard_map/ppermute | solution.py:229
  23.8 3.3 %collective-permute-start.8 = (f32[64,128]{1,0:T(8,128)S(1)}, f32[64,128]{1,0:T(8,128)S(1)}, u32[]{:S(2)}, u32[]{:S(2)}) collective-permute-start(f32[64,128]{1,0:T(8,128)S(1)} %add.9.first_ref), channel_id=1, source_target_pairs={{0,3},{1,2},{2,1},{3,0},{4,7},{5,6},{6,5},{7,4},{8,11},{9,10},{10,... | collective-permute-start | bytes 98312 | tf_op jit(solution)/shard_map/ppermute | solution.py:229
  27.1 3.3 %collective-permute-start.9 = (f32[64,128]{1,0:T(8,128)S(1)}, f32[64,128]{1,0:T(8,128)S(1)}, u32[]{:S(2)}, u32[]{:S(2)}) collective-permute-start(f32[64,128]{1,0:T(8,128)S(1)} %add_after.1), channel_id=1, source_target_pairs={{0,5},{1,4},{2,7},{3,6},{4,1},{5,0},{6,3},{7,2},{8,13},{9,12},{10,... | collective-permute-start | bytes 98312 | tf_op jit(solution)/shard_map/ppermute | solution.py:229
  30.5 4.8 %collective-permute-start.10 = (f32[64,128]{1,0:T(8,128)S(1)}, f32[64,128]{1,0:T(8,128)S(1)}, u32[]{:S(2)}, u32[]{:S(2)}) collective-permute-start(f32[64,128]{1,0:T(8,128)S(1)} %add.10), channel_id=1, source_target_pairs={{0,9},{1,8},{2,11},{3,10},{4,13},{5,12},{6,15},{7,14},{8,1},{9,0},... | collective-permute-start | bytes 98312 | tf_op jit(solution)/shard_map/ppermute | solution.py:229
  35.3 1.2 %collective-permute-start.11 = (f32[64,128]{1,0:T(8,128)S(1)}, f32[64,128]{1,0:T(8,128)S(1)}, u32[]{:S(2)}, u32[]{:S(2)}) collective-permute-start(f32[64,128]{1,0:T(8,128)S(1)} %add.11.mine_ref), channel_id=1, source_target_pairs={{0,1},{1,0},{2,3},{3,2},{4,5},{5,4},{6,7},{7,6},{8,9},{9,8},{10,11... | collective-permute-start | bytes 98312 | tf_op jit(solution)/shard_map/ppermute | solution.py:229

commit v4 on v3

--- a/solution.py
+++ b/solution.py
@@ -38,10 +38,10 @@
 
 
 def assemble(count_ref, rows_ref, owner_ref, offset_ref, blocks_ref, high_ref, low_ref, dense, placed, place, arrived):
-    n = lax.axis_size("row")
-    away = lax.rem(owner_ref[...].reshape(1, CAP) - lax.axis_index("row") + n, n)
+    n, me = lax.axis_size("row"), lax.axis_index("row")
+    away = lax.rem(owner_ref[...].reshape(1, CAP) - me + n, n)
     link = jnp.zeros_like(away)
-    for k, step in enumerate(steps(n)):
+    for k, step in enumerate(steps(n, me)):
         link = jnp.where(away == step, k, link)
     target = (link * BR_DEV + rows_ref[...].reshape(1, CAP)) * BR_DEV + offset_ref[...].reshape(1, CAP)
     slot = lax.broadcasted_iota(jnp.int32, (1, CAP), 1)
@@ -133,8 +133,37 @@
     done_ref[...] = jnp.zeros_like(done_ref)
 
 
-def steps(n):
-    return (0, 1, n - 1, 4, n - 4, n // 2, 5, n - 5)
+def steps(n, me):
+    even, even_four = me % 2 == 0, (me // 4) % 2 == 0
+
+    def one_of(first, when_first):
+        return jnp.where(when_first, first, n - first)
+
+    return (
+        0,
+        one_of(4, even_four),
+        one_of(n - 4, even_four),
+        one_of(1, even),
+        one_of(n - 1, even),
+        n // 2,
+        one_of(5, even),
+        one_of(n - 5, even),
+    )
+
+
+def pick(first_ref, second_ref, near_ref, next_ref):
+    me = lax.axis_index("row")
+    straight = (me % 2 == 1) == ((me // 4) % 2 == 0)
+
+    @pl.when(straight)
+    def _():
+        near_ref[...] = first_ref[...]
+        next_ref[...] = second_ref[...]
+
+    @pl.when(jnp.logical_not(straight))
+    def _():
+        near_ref[...] = second_ref[...]
+        next_ref[...] = first_ref[...]
 
 
 def shards(basis, springs, tangent_blocks, tile_rows, tile_owner, tile_offset, tile_count):
@@ -155,13 +184,29 @@
         name="prepare",
     )(basis)
 
-    def fetch(block, step):
-        return lax.ppermute(block, "row", [((d + step) % n, d) for d in range(n)])
-
-    above, below = fetch(held, 4), fetch(held, n - 4)
-    across = fetch(held, n // 2)
-    after, before = fetch(held, 1), fetch(held, n - 1)
-    far_above, far_below = fetch(above, 1), fetch(below, n - 1)
+    def trade(block, partner):
+        return lax.ppermute(block, "row", [(d, partner(d) % n) for d in range(n)])
+
+    def near(d):
+        return d ^ 1
+
+    def next_chip(d):
+        return d + 1 if d % 2 else d - 1
+
+    first = trade(basis, lambda d: d - 4 if d // 4 % 2 else d + 4)
+    second = trade(basis, lambda d: d + 4 if d // 4 % 2 else d - 4)
+    across = trade(held, lambda d: d + n // 2)
+    beside, beyond = trade(held, near), trade(held, next_chip)
+    near_sent, next_sent = pl.pallas_call(
+        pick,
+        out_shape=(jax.ShapeDtypeStruct((ROWS, MODES), full),) * 2,
+        in_specs=[vmem] * 2,
+        out_specs=(vmem,) * 2,
+        compiler_params=params,
+        cost_estimate=pl.CostEstimate(flops=0, bytes_accessed=500_000, transcendentals=0),
+        name="pick",
+    )(first, second)
+    far_near, far_next = trade(near_sent, near), trade(next_sent, next_chip)
 
     blocks = tangent_blocks.reshape(CAP // 8, 8, HALF, 128).transpose(0, 2, 1, 3).reshape(CAP * HALF, 128)
     high, low = pl.pallas_call(
@@ -197,7 +242,7 @@
         compiler_params=params,
         cost_estimate=pl.CostEstimate(flops=300_000_000, bytes_accessed=2_500_000, transcendentals=0),
         name="project_early",
-    )(high, low, springs.reshape(1, ROWS), held, after, before, above, below)
+    )(high, low, springs.reshape(1, ROWS), held, first, second, beside, beyond)
 
     side = me
     for shift in (8, 4, 2, 1):
@@ -213,7 +258,7 @@
         compiler_params=params,
         cost_estimate=pl.CostEstimate(flops=80_000_000, bytes_accessed=700_000, transcendentals=0),
         name="reduce_late",
-    )(side, weight_high, weight_low, early, across, far_above, far_below)
+    )(side, weight_high, weight_low, early, across, far_near, far_next)
 
     stiff_image, done = pl.pallas_call(
         project_late,
@@ -223,7 +268,7 @@
         compiler_params=params,
         cost_estimate=pl.CostEstimate(flops=160_000_000, bytes_accessed=1_500_000, transcendentals=0),
         name="project_late",
-    )(high, low, total, across, far_above, far_below)
+    )(high, low, total, across, far_near, far_next)
 
     def swap(block, apart):
         return lax.ppermute(block, "row", [(d, d ^ apart) for d in range(n)])

time: 37.3 us -> 37.6 us (level)
  starting transfers between devices: 15.4 us -> 21.1 us
  waiting for transfers between devices: 13.4 us -> 8.09 us
    ppermute x5, starting transfers between devices: 2.44 us -> 9.04 us  [swap(): return lax.ppermute(block, 'row', [(d, d ^ apart) for d in range(n)])]
    ppermute x5, waiting for transfers between devices: 10.4 us -> 5.91 us  [swap(): return lax.ppermute(block, 'row', [(d, d ^ apart) for d in range(n)])]
    ppermute x7, starting transfers between devices: 13 us -> 12 us  [trade(): return lax.ppermute(block, 'row', [(d, partner(d) % n) for d in range(n)])]
    ppermute x7, waiting for transfers between devices: 3.02 us -> 2.17 us  [trade(): return lax.ppermute(block, 'row', [(d, partner(d) % n) for d in range(n)])]
  transfers between devices with their start and end apart: 12 -> 12, of which waited for: 8 -> 6; matrix products, arithmetic and copies ran while one was open for 0% -> 0% of each run, Pallas kernels for 13% -> 13%
where the time goes in v4:
time: 37.6 us; the launch traced here: 37.4 us
  starting transfers between devices  21.1 us (56%)
  waiting for transfers between devices  8.09 us (22%)
  Pallas kernels  5.82 us (15%)
  between operations  1.47 us (4%)
  local copies, waits for them, and re-layouts  0.96 us (3%)
    ppermute x7, starting transfers between devices, trade(): return lax.ppermute(block, 'row', [(d, partner(d) % n) for d in range(n)])  12 us
    ppermute x5, starting transfers between devices, swap(): return lax.ppermute(block, 'row', [(d, d ^ apart) for d in range(n)])  9.04 us
    ppermute x5, waiting for transfers between devices, swap(): return lax.ppermute(block, 'row', [(d, d ^ apart) for d in range(n)])  5.91 us
    pallas_call x1, Pallas kernels, shards(): pl.pallas_call(assemble, out_shape=(jax.ShapeDtypeStruct((LINKS, ROWS, RO...  2.58 us
    ppermute x7, waiting for transfers between devices, trade(): return lax.ppermute(block, 'row', [(d, partner(d) % n) for d in range(n)])  2.17 us
    pallas_call x1, Pallas kernels, shards(): pl.pallas_call(project_early, out_shape=(jax.ShapeDtypeStruct((ROWS, MODE...  1.13 us
    pallas_call x1, Pallas kernels, shards(): pl.pallas_call(project_late, out_shape=(jax.ShapeDtypeStruct((ROWS, MODES...  1.13 us
    unnamed x12, local copies, waits for them, and re-layouts  0.96 us
  transfers between devices with their start and end apart: 12, of which 6 were waited for; matrix products, arithmetic and copies ran while one was open for 0% of the time, Pallas kernels for 13%

profile of v4, /device:TPU:0, one launch (start us, length us, event | category | flops | bytes accessed | tf_op | source)
XLA Modules:
  0.0 37.4 jit_solution(5145845586427096384)
XLA Ops:
  0.6 0.0 copy-start.2
  0.7 3.1 %collective-permute-start = (f32[256,128]{1,0:T(8,128)}, f32[256,128]{1,0:T(8,128)S(1)}, u32[]{:S(2)}, u32[]{:S(2)}) collective-permute-start(f32[256,128]{1,0:T(8,128)} %basis_ref.1), channel_id=1, source_target_pairs={{0,4},{1,5},{2,6},{3,7},{4,0},{5,1},{6,2},{7,3},{8,12},{9,13},{10,... | collective-permute-start | bytes 393224 | tf_op jit(solution)/shard_map/ppermute | solution.py:188
  3.8 2.5 %collective-permute-start.1 = (f32[256,128]{1,0:T(8,128)}, f32[256,128]{1,0:T(8,128)S(1)}, u32[]{:S(2)}, u32[]{:S(2)}) collective-permute-start(f32[256,128]{1,0:T(8,128)} %basis_ref.1), channel_id=1, source_target_pairs={{0,12},{1,13},{2,14},{3,15},{4,8},{5,9},{6,10},{7,11},{8,4},{9,5},... | collective-permute-start | bytes 393224 | tf_op jit(solution)/shard_map/ppermute | solution.py:188
  6.2 0.9 %copy-done.5 = f32[256,128]{1,0:T(8,128)S(1)} copy-done((f32[256,128]{1,0:T(8,128)S(1)}, f32[256,128]{1,0:T(8,128)}, u32[]{:S(2)}) %copy-start.5) | copy-done | bytes 131096
  7.2 0.0 copy-start.1
  7.2 0.1 collective-permute-start.2
  7.3 2.4 %collective-permute-start.3 = (f32[256,128]{1,0:T(8,128)S(1)}, f32[256,128]{1,0:T(8,128)S(1)}, u32[]{:S(2)}, u32[]{:S(2)}) collective-permute-start(f32[256,128]{1,0:T(8,128)S(1)} %prepare.1.refs_0_), channel_id=1, source_target_pairs={{0,15},{1,2},{2,1},{3,4},{4,3},{5,6},{6,5},{7,8},{8,7},{9,10},{10,... | collective-permute-start | bytes 393224 | tf_op jit(solution)/shard_map/ppermute | solution.py:188
  9.7 0.8 %collective-permute-start.4 = (f32[256,128]{1,0:T(8,128)S(1)}, f32[256,128]{1,0:T(8,128)S(1)}, u32[]{:S(2)}, u32[]{:S(2)}) collective-permute-start(f32[256,128]{1,0:T(8,128)S(1)} %prepare.1.refs_0_), channel_id=1, source_target_pairs={{0,8},{1,9},{2,10},{3,11},{4,12},{5,13},{6,14},{7,15},{8,0},{9,1},... | collective-permute-start | bytes 393224 | tf_op jit(solution)/shard_map/ppermute | solution.py:188
  10.5 0.0 collective-permute-done.refs_1_.first_ref
  10.5 2.2 %collective-permute-done.1.refs_2_.second_ref = f32[256,128]{1,0:T(8,128)S(1)} collective-permute-done((f32[256,128]{1,0:T(8,128)}, f32[256,128]{1,0:T(8,128)S(1)}, u32[]{:S(2)}, u32[]{:S(2)}) %collective-permute-start.1) | collective-permute-done | bytes 131104 | tf_op jit(solution)/shard_map/ppermute | solution.py:188
  12.7 0.1 collective-permute-start.5
  12.7 3.1 %collective-permute-start.6 = (f32[256,128]{1,0:T(8,128)S(1)}, f32[256,128]{1,0:T(8,128)S(1)}, u32[]{:S(2)}, u32[]{:S(2)}) collective-permute-start(f32[256,128]{1,0:T(8,128)S(1)} %get-tuple-element.18), channel_id=1, source_target_pairs={{0,15},{1,2},{2,1},{3,4},{4,3},{5,6},{6,5},{7,8},{8,7},{9,10},{10,... | collective-permute-start | bytes 393224 | tf_op jit(solution)/shard_map/ppermute | solution.py:188
  16.6 2.6 %assemble.1 = (bf16[8,256,256]{2,1,0:T(8,128)(2,1)S(1)}, bf16[8,256,256]{2,1,0:T(8,128)(2,1)S(1)}) custom-call(s32[1]{0:T(128)S(6)} %copy.9.count_ref, s32[128]{0:T(128)S(1)} %copy-done.2, s32[128]{0:T(128)S(1)} %bitcast.10, s32[128]{0:T(128)S(1)} %copy-done.4, f32[4096,128]{1,0:T(8,128)S(1)} %bitcast.8), custom_call_target="tpu_custom_call" | custom-call | flops 10000000 | bytes 8000000 | tf_op jit(solution)/shard_map/assemble/pallas_call | solution.py:212
  19.2 0.0 collective-permute-done.2.refs_3_
  19.2 0.0 collective-permute-done.3.refs_4_
  19.2 1.1 %project_early.1 = (f32[256,128]{1,0:T(8,128)S(1)}, f32[128,128]{1,0:T(8,128)S(1)}, bf16[3,128,256]{2,1,0:T(8,128)(2,1)S(1)}, bf16[3,128,256]{2,1,0:T(8,128)(2,1)S(1)}) custom-call(bf16[8,256,256]{2,1,0:T(8,128)(2,1)S(1)} %get-tuple-element.14.high_ref, bf16[8,256,256]{2,1,0:T(8,128)(2,1)S(1)} %get-tuple-element.15.low_ref, f32[1,256]{1,0:T(1,128)S(1)} %bitcast.9, ...), custom_call_target="tpu_custom_call" | custom-call | flops 300000000 | bytes 2500000 | tf_op jit(solution)/shard_map/project_early/pallas_call | solution.py:231
  20.3 0.0 collective-permute-done.4.refs_0_
  20.3 0.0 collective-permute-done.5.refs_1_
  20.4 0.0 collective-permute-done.6.refs_2_
  20.4 0.3 reduce_late.1
  20.7 0.1 collective-permute-start.7
  20.8 1.2 %collective-permute-done.7 = f32[64,128]{1,0:T(8,128)S(1)} collective-permute-done((f32[64,128]{1,0:T(8,128)S(1)}, f32[64,128]{1,0:T(8,128)S(1)}, u32[]{:S(2)}, u32[]{:S(2)}) %collective-permute-start.7) | collective-permute-done | bytes 32800 | tf_op jit(solution)/shard_map/ppermute | solution.py:274
  22.0 3.2 %collective-permute-start.8 = (f32[64,128]{1,0:T(8,128)S(1)}, f32[64,128]{1,0:T(8,128)S(1)}, u32[]{:S(2)}, u32[]{:S(2)}) collective-permute-start(f32[64,128]{1,0:T(8,128)S(1)} %add.9.first_ref), channel_id=1, source_target_pairs={{0,3},{1,2},{2,1},{3,0},{4,7},{5,6},{6,5},{7,4},{8,11},{9,10},{10,... | collective-permute-start | bytes 98312 | tf_op jit(solution)/shard_map/ppermute | solution.py:274
  25.1 1.1 %project_late.1 = (f32[256,128]{1,0:T(8,128)}, f32[8,128]{1,0:T(8,128)S(1)}) custom-call(bf16[8,256,256]{2,1,0:T(8,128)(2,1)S(1)} %get-tuple-element.14.high_ref, bf16[8,256,256]{2,1,0:T(8,128)(2,1)S(1)} %get-tuple-element.15.low_ref, f32[256,128]{1,0:T(8,128)S(1)} %get-tuple-element.16.total_ref, f32[256,128]{1,0:T(8,128)S(1)} %collective-permute-done.4.refs_0_, ...), custom_call_target="tpu_custom_call" | custom-call | flops 160000000 | bytes 1500000 | tf_op jit(solution)/shard_map/project_late/pallas_call | solution.py:263
  26.3 0.5 %collective-permute-done.8.second_ref = f32[64,128]{1,0:T(8,128)S(1)} collective-permute-done((f32[64,128]{1,0:T(8,128)S(1)}, f32[64,128]{1,0:T(8,128)S(1)}, u32[]{:S(2)}, u32[]{:S(2)}) %collective-permute-start.8) | collective-permute-done | bytes 32800 | tf_op jit(solution)/shard_map/ppermute | solution.py:274
  26.8 2.4 %collective-permute-start.9 = (f32[64,128]{1,0:T(8,128)S(1)}, f32[64,128]{1,0:T(8,128)S(1)}, u32[]{:S(2)}, u32[]{:S(2)}) collective-permute-start(f32[64,128]{1,0:T(8,128)S(1)} %add_after.1), channel_id=1, source_target_pairs={{0,5},{1,4},{2,7},{3,6},{4,1},{5,0},{6,3},{7,2},{8,13},{9,12},{10,... | collective-permute-start | bytes 98312 | tf_op jit(solution)/shard_map/ppermute | solution.py:274
  29.1 1.6 %collective-permute-done.9 = f32[64,128]{1,0:T(8,128)S(1)} collective-permute-done((f32[64,128]{1,0:T(8,128)S(1)}, f32[64,128]{1,0:T(8,128)S(1)}, u32[]{:S(2)}, u32[]{:S(2)}) %collective-permute-start.9) | collective-permute-done | bytes 32800 | tf_op jit(solution)/shard_map/ppermute | solution.py:274
  30.8 3.2 %collective-permute-start.10 = (f32[64,128]{1,0:T(8,128)S(1)}, f32[64,128]{1,0:T(8,128)S(1)}, u32[]{:S(2)}, u32[]{:S(2)}) collective-permute-start(f32[64,128]{1,0:T(8,128)S(1)} %add.10), channel_id=1, source_target_pairs={{0,9},{1,8},{2,11},{3,10},{4,13},{5,12},{6,15},{7,14},{8,1},{9,0},... | collective-permute-start | bytes 98312 | tf_op jit(solution)/shard_map/ppermute | solution.py:274
  34.0 1.6 %collective-permute-done.10 = f32[64,128]{1,0:T(8,128)S(1)} collective-permute-done((f32[64,128]{1,0:T(8,128)S(1)}, f32[64,128]{1,0:T(8,128)S(1)}, u32[]{:S(2)}, u32[]{:S(2)}) %collective-permute-start.10) | collective-permute-done | bytes 32800 | tf_op jit(solution)/shard_map/ppermute | solution.py:274
  35.6 0.2 collective-permute-start.11
  35.8 1.0 %collective-permute-done.11.other_ref = f32[64,128]{1,0:T(8,128)S(1)} collective-permute-done((f32[64,128]{1,0:T(8,128)S(1)}, f32[64,128]{1,0:T(8,128)S(1)}, u32[]{:S(2)}, u32[]{:S(2)}) %collective-permute-start.11) | collective-permute-done | bytes 32800 | tf_op jit(solution)/shard_map/ppermute | solution.py:274
  36.8 0.6 %join.1 = f32[128,128]{1,0:T(8,128)} custom-call(s32[1]{0:T(128)} %bitcast.5.side_ref, f32[64,128]{1,0:T(8,128)S(1)} %add.11.mine_ref, f32[64,128]{1,0:T(8,128)S(1)} %collective-permute-done.11.other_ref), custom_call_target="tpu_custom_call" | custom-call | bytes 130000 | tf_op jit(solution)/shard_map/join/pallas_call | solution.py:289
  (15 shorter events, 0.1 us)
Async XLA Ops:
  0.6 15.9 %copy-start.2 = (s32[128]{0:T(128)S(1)}, s32[128]{0:T(128)}, u32[]{:S(2)}) copy-start(s32[128]{0:T(128)} %rows_ref.1) | copy-start | bytes 1540
  0.6 15.9 %copy-start.3 = (s32[128,1]{0,1:T(1,128)S(1)}, s32[128,1]{0,1:T(1,128)}, u32[]{:S(2)}) copy-start(s32[128,1]{0,1:T(1,128)} %param.11) | copy-start | bytes 1540
  0.7 15.9 %copy-start.4 = (s32[128]{0:T(128)S(1)}, s32[128]{0:T(128)}, u32[]{:S(2)}) copy-start(s32[128]{0:T(128)} %offset_ref.1) | copy-start | bytes 1540
  0.7 15.9 %copy-start = (f32[128,4096]{1,0:T(8,128)S(1)}, f32[128,4096]{1,0:T(8,128)}, u32[]{:S(2)}) copy-start(f32[128,4096]{1,0:T(8,128)} %param.9) | copy-start | bytes 6291460
  0.7 9.8 %collective-permute-start = (f32[256,128]{1,0:T(8,128)}, f32[256,128]{1,0:T(8,128)S(1)}, u32[]{:S(2)}, u32[]{:S(2)}) collective-permute-start(f32[256,128]{1,0:T(8,128)} %basis_ref.1), channel_id=1, source_target_pairs={{0,4},{1,5},{2,6},{3,7},{4,0},{5,1},{6,2},{7,3},{8,12},{9,13},{10,... | collective-permute-start | bytes 393224 | tf_op jit(solution)/shard_map/ppermute | solution.py:188
  3.8 8.9 %collective-permute-start.1 = (f32[256,128]{1,0:T(8,128)}, f32[256,128]{1,0:T(8,128)S(1)}, u32[]{:S(2)}, u32[]{:S(2)}) collective-permute-start(f32[256,128]{1,0:T(8,128)} %basis_ref.1), channel_id=1, source_target_pairs={{0,12},{1,13},{2,14},{3,15},{4,8},{5,9},{6,10},{7,11},{8,4},{9,5},... | collective-permute-start | bytes 393224 | tf_op jit(solution)/shard_map/ppermute | solution.py:188
  6.2 0.9 %copy-start.5 = (f32[256,128]{1,0:T(8,128)S(1)}, f32[256,128]{1,0:T(8,128)}, u32[]{:S(2)}) copy-start(f32[256,128]{1,0:T(8,128)} %basis_ref.1) | copy-start | bytes 393220
  7.2 12.0 %copy-start.1 = (f32[256]{0:T(256)S(1)}, f32[256]{0:T(256)}, u32[]{:S(2)}) copy-start(f32[256]{0:T(256)} %param.8) | copy-start | bytes 3076
  7.2 12.0 %collective-permute-start.2 = (f32[256,128]{1,0:T(8,128)S(1)}, f32[256,128]{1,0:T(8,128)S(1)}, u32[]{:S(2)}, u32[]{:S(2)}) collective-permute-start(f32[256,128]{1,0:T(8,128)S(1)} %prepare.1.refs_0_), channel_id=1, source_target_pairs={{0,1},{1,0},{2,3},{3,2},{4,5},{5,4},{6,7},{7,6},{8,9},{9,8},{10,11... | collective-permute-start | bytes 393224 | tf_op jit(solution)/shard_map/ppermute | solution.py:188
  7.3 11.9 %collective-permute-start.3 = (f32[256,128]{1,0:T(8,128)S(1)}, f32[256,128]{1,0:T(8,128)S(1)}, u32[]{:S(2)}, u32[]{:S(2)}) collective-permute-start(f32[256,128]{1,0:T(8,128)S(1)} %prepare.1.refs_0_), channel_id=1, source_target_pairs={{0,15},{1,2},{2,1},{3,4},{4,3},{5,6},{6,5},{7,8},{8,7},{9,10},{10,... | collective-permute-start | bytes 393224 | tf_op jit(solution)/shard_map/ppermute | solution.py:188
  9.7 10.7 %collective-permute-start.4 = (f32[256,128]{1,0:T(8,128)S(1)}, f32[256,128]{1,0:T(8,128)S(1)}, u32[]{:S(2)}, u32[]{:S(2)}) collective-permute-start(f32[256,128]{1,0:T(8,128)S(1)} %prepare.1.refs_0_), channel_id=1, source_target_pairs={{0,8},{1,9},{2,10},{3,11},{4,12},{5,13},{6,14},{7,15},{8,0},{9,1},... | collective-permute-start | bytes 393224 | tf_op jit(solution)/shard_map/ppermute | solution.py:188
  12.7 7.7 %collective-permute-start.5 = (f32[256,128]{1,0:T(8,128)S(1)}, f32[256,128]{1,0:T(8,128)S(1)}, u32[]{:S(2)}, u32[]{:S(2)}) collective-permute-start(f32[256,128]{1,0:T(8,128)S(1)} %get-tuple-element.17), channel_id=1, source_target_pairs={{0,1},{1,0},{2,3},{3,2},{4,5},{5,4},{6,7},{7,6},{8,9},{9,8},{10,11... | collective-permute-start | bytes 393224 | tf_op jit(solution)/shard_map/ppermute | solution.py:188
  12.7 7.6 %collective-permute-start.6 = (f32[256,128]{1,0:T(8,128)S(1)}, f32[256,128]{1,0:T(8,128)S(1)}, u32[]{:S(2)}, u32[]{:S(2)}) collective-permute-start(f32[256,128]{1,0:T(8,128)S(1)} %get-tuple-element.18), channel_id=1, source_target_pairs={{0,15},{1,2},{2,1},{3,4},{4,3},{5,6},{6,5},{7,8},{8,7},{9,10},{10,... | collective-permute-start | bytes 393224 | tf_op jit(solution)/shard_map/ppermute | solution.py:188
  20.7 1.3 %collective-permute-start.7 = (f32[64,128]{1,0:T(8,128)S(1)}, f32[64,128]{1,0:T(8,128)S(1)}, u32[]{:S(2)}, u32[]{:S(2)}) collective-permute-start(f32[64,128]{1,0:T(8,128)S(1)} %get-tuple-element.24), channel_id=1, source_target_pairs={{0,1},{1,0},{2,3},{3,2},{4,5},{5,4},{6,7},{7,6},{8,9},{9,8},{10,11... | collective-permute-start | bytes 98312 | tf_op jit(solution)/shard_map/ppermute | solution.py:274
  22.0 4.8 %collective-permute-start.8 = (f32[64,128]{1,0:T(8,128)S(1)}, f32[64,128]{1,0:T(8,128)S(1)}, u32[]{:S(2)}, u32[]{:S(2)}) collective-permute-start(f32[64,128]{1,0:T(8,128)S(1)} %add.9.first_ref), channel_id=1, source_target_pairs={{0,3},{1,2},{2,1},{3,0},{4,7},{5,6},{6,5},{7,4},{8,11},{9,10},{10,... | collective-permute-start | bytes 98312 | tf_op jit(solution)/shard_map/ppermute | solution.py:274
  26.8 4.0 %collective-permute-start.9 = (f32[64,128]{1,0:T(8,128)S(1)}, f32[64,128]{1,0:T(8,128)S(1)}, u32[]{:S(2)}, u32[]{:S(2)}) collective-permute-start(f32[64,128]{1,0:T(8,128)S(1)} %add_after.1), channel_id=1, source_target_pairs={{0,5},{1,4},{2,7},{3,6},{4,1},{5,0},{6,3},{7,2},{8,13},{9,12},{10,... | collective-permute-start | bytes 98312 | tf_op jit(solution)/shard_map/ppermute | solution.py:274
  30.8 4.8 %collective-permute-start.10 = (f32[64,128]{1,0:T(8,128)S(1)}, f32[64,128]{1,0:T(8,128)S(1)}, u32[]{:S(2)}, u32[]{:S(2)}) collective-permute-start(f32[64,128]{1,0:T(8,128)S(1)} %add.10), channel_id=1, source_target_pairs={{0,9},{1,8},{2,11},{3,10},{4,13},{5,12},{6,15},{7,14},{8,1},{9,0},... | collective-permute-start | bytes 98312 | tf_op jit(solution)/shard_map/ppermute | solution.py:274
  35.6 1.2 %collective-permute-start.11 = (f32[64,128]{1,0:T(8,128)S(1)}, f32[64,128]{1,0:T(8,128)S(1)}, u32[]{:S(2)}, u32[]{:S(2)}) collective-permute-start(f32[64,128]{1,0:T(8,128)S(1)} %add.11.mine_ref), channel_id=1, source_target_pairs={{0,1},{1,0},{2,3},{3,2},{4,5},{5,4},{6,7},{7,6},{8,9},{9,8},{10,11... | collective-permute-start | bytes 98312 | tf_op jit(solution)/shard_map/ppermute | solution.py:274

commit v5 on v4

--- a/solution.py
+++ b/solution.py
@@ -141,8 +141,8 @@
 
     return (
         0,
+        one_of(n - 4, even_four),
         one_of(4, even_four),
-        one_of(n - 4, even_four),
         one_of(1, even),
         one_of(n - 1, even),
         n // 2,
@@ -157,13 +157,13 @@
 
     @pl.when(straight)
     def _():
+        near_ref[...] = second_ref[...]
+        next_ref[...] = first_ref[...]
+
+    @pl.when(jnp.logical_not(straight))
+    def _():
         near_ref[...] = first_ref[...]
         next_ref[...] = second_ref[...]
-
-    @pl.when(jnp.logical_not(straight))
-    def _():
-        near_ref[...] = second_ref[...]
-        next_ref[...] = first_ref[...]
 
 
 def shards(basis, springs, tangent_blocks, tile_rows, tile_owner, tile_offset, tile_count):
@@ -193,9 +193,15 @@
     def next_chip(d):
         return d + 1 if d % 2 else d - 1
 
-    first = trade(basis, lambda d: d - 4 if d // 4 % 2 else d + 4)
-    second = trade(basis, lambda d: d + 4 if d // 4 % 2 else d - 4)
-    across = trade(held, lambda d: d + n // 2)
+    def outer(d):
+        return d - 4 if d // 4 % 2 else d + 4
+
+    def inner(d):
+        return d + 4 if d // 4 % 2 else d - 4
+
+    first = trade(basis, inner)
+    second = trade(basis, outer)
+    across = trade(first, outer) if n == 16 else trade(held, lambda d: d + n // 2)
     beside, beyond = trade(held, near), trade(held, next_chip)
     near_sent, next_sent = pl.pallas_call(
         pick,

time: 37.6 us -> 36.3 us (0.965)
  starting transfers between devices: 21.1 us -> 13.5 us
  waiting for transfers between devices: 8.09 us -> 14.4 us
    ppermute x5, starting transfers between devices: 9.04 us -> 2.62 us  [swap(): return lax.ppermute(block, 'row', [(d, d ^ apart) for d in range(n)])]
    ppermute x5, waiting for transfers between devices: 5.91 us -> 9.65 us  [swap(): return lax.ppermute(block, 'row', [(d, d ^ apart) for d in range(n)])]
    ppermute x7, waiting for transfers between devices: 2.17 us -> 4.78 us  [trade(): return lax.ppermute(block, 'row', [(d, partner(d) % n) for d in range(n)])]
    ppermute x7, starting transfers between devices: 12 us -> 10.9 us  [trade(): return lax.ppermute(block, 'row', [(d, partner(d) % n) for d in range(n)])]
  transfers between devices with their start and end apart: 12 -> 12, of which waited for: 6 -> 8; matrix products, arithmetic and copies ran while one was open for 0% -> 0% of each run, Pallas kernels for 13% -> 13%
where the time goes in v5:
time: 36.3 us; the launch traced here: 36.2 us
  waiting for transfers between devices  14.4 us (40%)
  starting transfers between devices  13.5 us (37%)
  Pallas kernels  5.74 us (16%)
  between operations  1.47 us (4%)
  local copies, waits for them, and re-layouts  0.99 us (3%)
    ppermute x7, starting transfers between devices, trade(): return lax.ppermute(block, 'row', [(d, partner(d) % n) for d in range(n)])  10.9 us
    ppermute x5, waiting for transfers between devices, swap(): return lax.ppermute(block, 'row', [(d, d ^ apart) for d in range(n)])  9.65 us
    ppermute x7, waiting for transfers between devices, trade(): return lax.ppermute(block, 'row', [(d, partner(d) % n) for d in range(n)])  4.78 us
    ppermute x5, starting transfers between devices, swap(): return lax.ppermute(block, 'row', [(d, d ^ apart) for d in range(n)])  2.62 us
    pallas_call x1, Pallas kernels, shards(): pl.pallas_call(assemble, out_shape=(jax.ShapeDtypeStruct((LINKS, ROWS, RO...  2.51 us
    pallas_call x1, Pallas kernels, shards(): pl.pallas_call(project_early, out_shape=(jax.ShapeDtypeStruct((ROWS, MODE...  1.14 us
    pallas_call x1, Pallas kernels, shards(): pl.pallas_call(project_late, out_shape=(jax.ShapeDtypeStruct((ROWS, MODES...  1.12 us
    unnamed x12, local copies, waits for them, and re-layouts  0.99 us
  transfers between devices with their start and end apart: 12, of which 8 were waited for; matrix products, arithmetic and copies ran while one was open for 0% of the time, Pallas kernels for 13%

profile of v5, /device:TPU:0, one launch (start us, length us, event | category | flops | bytes accessed | tf_op | source)
XLA Modules:
  0.0 36.2 jit_solution(12415359064857999571)
XLA Ops:
  0.7 5.1 %collective-permute-start = (f32[256,128]{1,0:T(8,128)}, f32[256,128]{1,0:T(8,128)S(1)}, u32[]{:S(2)}, u32[]{:S(2)}) collective-permute-start(f32[256,128]{1,0:T(8,128)} %basis_ref.1), channel_id=1, source_target_pairs={{0,12},{1,13},{2,14},{3,15},{4,8},{5,9},{6,10},{7,11},{8,4},{9,5},... | collective-permute-start | bytes 393224 | tf_op jit(solution)/shard_map/ppermute | solution.py:188
  5.8 0.0 collective-permute-start.1
  5.8 1.0 %copy-done.5 = f32[256,128]{1,0:T(8,128)S(1)} copy-done((f32[256,128]{1,0:T(8,128)S(1)}, f32[256,128]{1,0:T(8,128)}, u32[]{:S(2)}) %copy-start.5) | copy-done | bytes 131096
  6.8 0.0 copy-start.1
  6.8 0.1 collective-permute-start.2
  6.9 1.9 %collective-permute-start.3 = (f32[256,128]{1,0:T(8,128)S(1)}, f32[256,128]{1,0:T(8,128)S(1)}, u32[]{:S(2)}, u32[]{:S(2)}) collective-permute-start(f32[256,128]{1,0:T(8,128)S(1)} %prepare.1.refs_0_), channel_id=1, source_target_pairs={{0,15},{1,2},{2,1},{3,4},{4,3},{5,6},{6,5},{7,8},{8,7},{9,10},{10,... | collective-permute-start | bytes 393224 | tf_op jit(solution)/shard_map/ppermute | solution.py:188
  8.8 1.6 %collective-permute-done.refs_1_.first_ref = f32[256,128]{1,0:T(8,128)S(1)} collective-permute-done((f32[256,128]{1,0:T(8,128)}, f32[256,128]{1,0:T(8,128)S(1)}, u32[]{:S(2)}, u32[]{:S(2)}) %collective-permute-start) | collective-permute-done | bytes 131104 | tf_op jit(solution)/shard_map/ppermute | solution.py:188
  10.4 2.0 %collective-permute-done.1.refs_2_.second_ref = f32[256,128]{1,0:T(8,128)S(1)} collective-permute-done((f32[256,128]{1,0:T(8,128)}, f32[256,128]{1,0:T(8,128)S(1)}, u32[]{:S(2)}, u32[]{:S(2)}) %collective-permute-start.1) | collective-permute-done | bytes 131104 | tf_op jit(solution)/shard_map/ppermute | solution.py:188
  12.4 0.1 collective-permute-start.5
  12.5 1.7 %collective-permute-start.4 = (f32[256,128]{1,0:T(8,128)S(1)}, f32[256,128]{1,0:T(8,128)S(1)}, u32[]{:S(2)}, u32[]{:S(2)}) collective-permute-start(f32[256,128]{1,0:T(8,128)S(1)} %collective-permute-done.refs_1_.first_ref), channel_id=1, source_target_pairs={{0,4},{1,5},{2,6},{3,7},{4,0},{5,1},{6,2},{7,3},{8,12},{9,13},{10,... | collective-permute-start | bytes 393224 | tf_op jit(solution)/shard_map/ppermute | solution.py:188
  14.3 2.0 %collective-permute-start.6 = (f32[256,128]{1,0:T(8,128)S(1)}, f32[256,128]{1,0:T(8,128)S(1)}, u32[]{:S(2)}, u32[]{:S(2)}) collective-permute-start(f32[256,128]{1,0:T(8,128)S(1)} %get-tuple-element.18), channel_id=1, source_target_pairs={{0,15},{1,2},{2,1},{3,4},{4,3},{5,6},{6,5},{7,8},{8,7},{9,10},{10,... | collective-permute-start | bytes 393224 | tf_op jit(solution)/shard_map/ppermute | solution.py:188
  16.9 0.0 copy-done.2
  16.9 2.5 %assemble.1 = (bf16[8,256,256]{2,1,0:T(8,128)(2,1)S(1)}, bf16[8,256,256]{2,1,0:T(8,128)(2,1)S(1)}) custom-call(s32[1]{0:T(128)S(6)} %copy.9.count_ref, s32[128]{0:T(128)S(1)} %copy-done.2, s32[128]{0:T(128)S(1)} %bitcast.10, s32[128]{0:T(128)S(1)} %copy-done.4, f32[4096,128]{1,0:T(8,128)S(1)} %bitcast.8), custom_call_target="tpu_custom_call" | custom-call | flops 10000000 | bytes 8000000 | tf_op jit(solution)/shard_map/assemble/pallas_call | solution.py:218
  19.5 0.0 collective-permute-done.2.refs_3_
  19.5 0.0 collective-permute-done.3.refs_4_
  19.5 1.1 %project_early.1 = (f32[256,128]{1,0:T(8,128)S(1)}, f32[128,128]{1,0:T(8,128)S(1)}, bf16[3,128,256]{2,1,0:T(8,128)(2,1)S(1)}, bf16[3,128,256]{2,1,0:T(8,128)(2,1)S(1)}) custom-call(bf16[8,256,256]{2,1,0:T(8,128)(2,1)S(1)} %get-tuple-element.14.high_ref, bf16[8,256,256]{2,1,0:T(8,128)(2,1)S(1)} %get-tuple-element.15.low_ref, f32[1,256]{1,0:T(1,128)S(1)} %bitcast.9, ...), custom_call_target="tpu_custom_call" | custom-call | flops 300000000 | bytes 2500000 | tf_op jit(solution)/shard_map/project_early/pallas_call | solution.py:237
  20.6 0.0 collective-permute-done.4.refs_0_
  20.6 0.0 collective-permute-done.5.refs_1_
  20.7 1.2 %collective-permute-done.6.refs_2_ = f32[256,128]{1,0:T(8,128)S(1)} collective-permute-done((f32[256,128]{1,0:T(8,128)S(1)}, f32[256,128]{1,0:T(8,128)S(1)}, u32[]{:S(2)}, u32[]{:S(2)}) %collective-permute-start.6) | collective-permute-done | bytes 131104 | tf_op jit(solution)/shard_map/ppermute | solution.py:188
  21.8 0.3 reduce_late.1
  22.1 0.1 collective-permute-start.7
  22.2 1.2 %collective-permute-done.7 = f32[64,128]{1,0:T(8,128)S(1)} collective-permute-done((f32[64,128]{1,0:T(8,128)S(1)}, f32[64,128]{1,0:T(8,128)S(1)}, u32[]{:S(2)}, u32[]{:S(2)}) %collective-permute-start.7) | collective-permute-done | bytes 32800 | tf_op jit(solution)/shard_map/ppermute | solution.py:280
  23.4 0.6 %collective-permute-start.8 = (f32[64,128]{1,0:T(8,128)S(1)}, f32[64,128]{1,0:T(8,128)S(1)}, u32[]{:S(2)}, u32[]{:S(2)}) collective-permute-start(f32[64,128]{1,0:T(8,128)S(1)} %add.9.first_ref), channel_id=1, source_target_pairs={{0,3},{1,2},{2,1},{3,0},{4,7},{5,6},{6,5},{7,4},{8,11},{9,10},{10,... | collective-permute-start | bytes 98312 | tf_op jit(solution)/shard_map/ppermute | solution.py:280
  24.0 1.1 %project_late.1 = (f32[256,128]{1,0:T(8,128)}, f32[8,128]{1,0:T(8,128)S(1)}) custom-call(bf16[8,256,256]{2,1,0:T(8,128)(2,1)S(1)} %get-tuple-element.14.high_ref, bf16[8,256,256]{2,1,0:T(8,128)(2,1)S(1)} %get-tuple-element.15.low_ref, f32[256,128]{1,0:T(8,128)S(1)} %get-tuple-element.16.total_ref, f32[256,128]{1,0:T(8,128)S(1)} %collective-permute-done.4.refs_0_, ...), custom_call_target="tpu_custom_call" | custom-call | flops 160000000 | bytes 1500000 | tf_op jit(solution)/shard_map/project_late/pallas_call | solution.py:269
  25.2 1.6 %collective-permute-done.8.second_ref = f32[64,128]{1,0:T(8,128)S(1)} collective-permute-done((f32[64,128]{1,0:T(8,128)S(1)}, f32[64,128]{1,0:T(8,128)S(1)}, u32[]{:S(2)}, u32[]{:S(2)}) %collective-permute-start.8) | collective-permute-done | bytes 32800 | tf_op jit(solution)/shard_map/ppermute | solution.py:280
  26.7 1.5 %collective-permute-start.9 = (f32[64,128]{1,0:T(8,128)S(1)}, f32[64,128]{1,0:T(8,128)S(1)}, u32[]{:S(2)}, u32[]{:S(2)}) collective-permute-start(f32[64,128]{1,0:T(8,128)S(1)} %add_after.1), channel_id=1, source_target_pairs={{0,5},{1,4},{2,7},{3,6},{4,1},{5,0},{6,3},{7,2},{8,13},{9,12},{10,... | collective-permute-start | bytes 98312 | tf_op jit(solution)/shard_map/ppermute | solution.py:280
  28.3 1.8 %collective-permute-done.9 = f32[64,128]{1,0:T(8,128)S(1)} collective-permute-done((f32[64,128]{1,0:T(8,128)S(1)}, f32[64,128]{1,0:T(8,128)S(1)}, u32[]{:S(2)}, u32[]{:S(2)}) %collective-permute-start.9) | collective-permute-done | bytes 32800 | tf_op jit(solution)/shard_map/ppermute | solution.py:280
  30.1 0.2 collective-permute-start.10
  30.3 4.0 %collective-permute-done.10 = f32[64,128]{1,0:T(8,128)S(1)} collective-permute-done((f32[64,128]{1,0:T(8,128)S(1)}, f32[64,128]{1,0:T(8,128)S(1)}, u32[]{:S(2)}, u32[]{:S(2)}) %collective-permute-start.10) | collective-permute-done | bytes 32800 | tf_op jit(solution)/shard_map/ppermute | solution.py:280
  34.3 0.2 collective-permute-start.11
  34.5 1.0 %collective-permute-done.11.other_ref = f32[64,128]{1,0:T(8,128)S(1)} collective-permute-done((f32[64,128]{1,0:T(8,128)S(1)}, f32[64,128]{1,0:T(8,128)S(1)}, u32[]{:S(2)}, u32[]{:S(2)}) %collective-permute-start.11) | collective-permute-done | bytes 32800 | tf_op jit(solution)/shard_map/ppermute | solution.py:280
  35.5 0.6 %join.1 = f32[128,128]{1,0:T(8,128)} custom-call(s32[1]{0:T(128)} %bitcast.5.side_ref, f32[64,128]{1,0:T(8,128)S(1)} %add.11.mine_ref, f32[64,128]{1,0:T(8,128)S(1)} %collective-permute-done.11.other_ref), custom_call_target="tpu_custom_call" | custom-call | bytes 130000 | tf_op jit(solution)/shard_map/join/pallas_call | solution.py:295
  (15 shorter events, 0.1 us)
Async XLA Ops:
  0.6 16.3 %copy-start.2 = (s32[128]{0:T(128)S(1)}, s32[128]{0:T(128)}, u32[]{:S(2)}) copy-start(s32[128]{0:T(128)} %rows_ref.1) | copy-start | bytes 1540
  0.6 16.3 %copy-start.3 = (s32[128,1]{0,1:T(1,128)S(1)}, s32[128,1]{0,1:T(1,128)}, u32[]{:S(2)}) copy-start(s32[128,1]{0,1:T(1,128)} %param.11) | copy-start | bytes 1540
  0.7 16.3 %copy-start.4 = (s32[128]{0:T(128)S(1)}, s32[128]{0:T(128)}, u32[]{:S(2)}) copy-start(s32[128]{0:T(128)} %offset_ref.1) | copy-start | bytes 1540
  0.7 16.3 %copy-start = (f32[128,4096]{1,0:T(8,128)S(1)}, f32[128,4096]{1,0:T(8,128)}, u32[]{:S(2)}) copy-start(f32[128,4096]{1,0:T(8,128)} %param.9) | copy-start | bytes 6291460
  0.7 9.7 %collective-permute-start = (f32[256,128]{1,0:T(8,128)}, f32[256,128]{1,0:T(8,128)S(1)}, u32[]{:S(2)}, u32[]{:S(2)}) collective-permute-start(f32[256,128]{1,0:T(8,128)} %basis_ref.1), channel_id=1, source_target_pairs={{0,12},{1,13},{2,14},{3,15},{4,8},{5,9},{6,10},{7,11},{8,4},{9,5},... | collective-permute-start | bytes 393224 | tf_op jit(solution)/shard_map/ppermute | solution.py:188
  5.8 6.6 %collective-permute-start.1 = (f32[256,128]{1,0:T(8,128)}, f32[256,128]{1,0:T(8,128)S(1)}, u32[]{:S(2)}, u32[]{:S(2)}) collective-permute-start(f32[256,128]{1,0:T(8,128)} %basis_ref.1), channel_id=1, source_target_pairs={{0,4},{1,5},{2,6},{3,7},{4,0},{5,1},{6,2},{7,3},{8,12},{9,13},{10,... | collective-permute-start | bytes 393224 | tf_op jit(solution)/shard_map/ppermute | solution.py:188
  5.8 1.0 %copy-start.5 = (f32[256,128]{1,0:T(8,128)S(1)}, f32[256,128]{1,0:T(8,128)}, u32[]{:S(2)}) copy-start(f32[256,128]{1,0:T(8,128)} %basis_ref.1) | copy-start | bytes 393220
  6.8 12.7 %copy-start.1 = (f32[256]{0:T(256)S(1)}, f32[256]{0:T(256)}, u32[]{:S(2)}) copy-start(f32[256]{0:T(256)} %param.8) | copy-start | bytes 3076
  6.8 12.7 %collective-permute-start.2 = (f32[256,128]{1,0:T(8,128)S(1)}, f32[256,128]{1,0:T(8,128)S(1)}, u32[]{:S(2)}, u32[]{:S(2)}) collective-permute-start(f32[256,128]{1,0:T(8,128)S(1)} %prepare.1.refs_0_), channel_id=1, source_target_pairs={{0,1},{1,0},{2,3},{3,2},{4,5},{5,4},{6,7},{7,6},{8,9},{9,8},{10,11... | collective-permute-start | bytes 393224 | tf_op jit(solution)/shard_map/ppermute | solution.py:188
  6.9 12.6 %collective-permute-start.3 = (f32[256,128]{1,0:T(8,128)S(1)}, f32[256,128]{1,0:T(8,128)S(1)}, u32[]{:S(2)}, u32[]{:S(2)}) collective-permute-start(f32[256,128]{1,0:T(8,128)S(1)} %prepare.1.refs_0_), channel_id=1, source_target_pairs={{0,15},{1,2},{2,1},{3,4},{4,3},{5,6},{6,5},{7,8},{8,7},{9,10},{10,... | collective-permute-start | bytes 393224 | tf_op jit(solution)/shard_map/ppermute | solution.py:188
  12.4 8.2 %collective-permute-start.5 = (f32[256,128]{1,0:T(8,128)S(1)}, f32[256,128]{1,0:T(8,128)S(1)}, u32[]{:S(2)}, u32[]{:S(2)}) collective-permute-start(f32[256,128]{1,0:T(8,128)S(1)} %get-tuple-element.17), channel_id=1, source_target_pairs={{0,1},{1,0},{2,3},{3,2},{4,5},{5,4},{6,7},{7,6},{8,9},{9,8},{10,11... | collective-permute-start | bytes 393224 | tf_op jit(solution)/shard_map/ppermute | solution.py:188
  12.5 8.1 %collective-permute-start.4 = (f32[256,128]{1,0:T(8,128)S(1)}, f32[256,128]{1,0:T(8,128)S(1)}, u32[]{:S(2)}, u32[]{:S(2)}) collective-permute-start(f32[256,128]{1,0:T(8,128)S(1)} %collective-permute-done.refs_1_.first_ref), channel_id=1, source_target_pairs={{0,4},{1,5},{2,6},{3,7},{4,0},{5,1},{6,2},{7,3},{8,12},{9,13},{10,... | collective-permute-start | bytes 393224 | tf_op jit(solution)/shard_map/ppermute | solution.py:188
  14.3 7.5 %collective-permute-start.6 = (f32[256,128]{1,0:T(8,128)S(1)}, f32[256,128]{1,0:T(8,128)S(1)}, u32[]{:S(2)}, u32[]{:S(2)}) collective-permute-start(f32[256,128]{1,0:T(8,128)S(1)} %get-tuple-element.18), channel_id=1, source_target_pairs={{0,15},{1,2},{2,1},{3,4},{4,3},{5,6},{6,5},{7,8},{8,7},{9,10},{10,... | collective-permute-start | bytes 393224 | tf_op jit(solution)/shard_map/ppermute | solution.py:188
  22.1 1.3 %collective-permute-start.7 = (f32[64,128]{1,0:T(8,128)S(1)}, f32[64,128]{1,0:T(8,128)S(1)}, u32[]{:S(2)}, u32[]{:S(2)}) collective-permute-start(f32[64,128]{1,0:T(8,128)S(1)} %get-tuple-element.24), channel_id=1, source_target_pairs={{0,1},{1,0},{2,3},{3,2},{4,5},{5,4},{6,7},{7,6},{8,9},{9,8},{10,11... | collective-permute-start | bytes 98312 | tf_op jit(solution)/shard_map/ppermute | solution.py:280
  23.4 3.3 %collective-permute-start.8 = (f32[64,128]{1,0:T(8,128)S(1)}, f32[64,128]{1,0:T(8,128)S(1)}, u32[]{:S(2)}, u32[]{:S(2)}) collective-permute-start(f32[64,128]{1,0:T(8,128)S(1)} %add.9.first_ref), channel_id=1, source_target_pairs={{0,3},{1,2},{2,1},{3,0},{4,7},{5,6},{6,5},{7,4},{8,11},{9,10},{10,... | collective-permute-start | bytes 98312 | tf_op jit(solution)/shard_map/ppermute | solution.py:280
  26.7 3.3 %collective-permute-start.9 = (f32[64,128]{1,0:T(8,128)S(1)}, f32[64,128]{1,0:T(8,128)S(1)}, u32[]{:S(2)}, u32[]{:S(2)}) collective-permute-start(f32[64,128]{1,0:T(8,128)S(1)} %add_after.1), channel_id=1, source_target_pairs={{0,5},{1,4},{2,7},{3,6},{4,1},{5,0},{6,3},{7,2},{8,13},{9,12},{10,... | collective-permute-start | bytes 98312 | tf_op jit(solution)/shard_map/ppermute | solution.py:280
  30.1 4.2 %collective-permute-start.10 = (f32[64,128]{1,0:T(8,128)S(1)}, f32[64,128]{1,0:T(8,128)S(1)}, u32[]{:S(2)}, u32[]{:S(2)}) collective-permute-start(f32[64,128]{1,0:T(8,128)S(1)} %add.10), channel_id=1, source_target_pairs={{0,9},{1,8},{2,11},{3,10},{4,13},{5,12},{6,15},{7,14},{8,1},{9,0},... | collective-permute-start | bytes 98312 | tf_op jit(solution)/shard_map/ppermute | solution.py:280
  34.3 1.2 %collective-permute-start.11 = (f32[64,128]{1,0:T(8,128)S(1)}, f32[64,128]{1,0:T(8,128)S(1)}, u32[]{:S(2)}, u32[]{:S(2)}) collective-permute-start(f32[64,128]{1,0:T(8,128)S(1)} %add.11.mine_ref), channel_id=1, source_target_pairs={{0,1},{1,0},{2,3},{3,2},{4,5},{5,4},{6,7},{7,6},{8,9},{9,8},{10,11... | collective-permute-start | bytes 98312 | tf_op jit(solution)/shard_map/ppermute | solution.py:280

commit v6 on v5

--- a/solution.py
+++ b/solution.py
@@ -145,9 +145,9 @@
         one_of(4, even_four),
         one_of(1, even),
         one_of(n - 1, even),
+        one_of(n - 5, even),
         n // 2,
         one_of(5, even),
-        one_of(n - 5, even),
     )
 
 
@@ -212,7 +212,7 @@
         cost_estimate=pl.CostEstimate(flops=0, bytes_accessed=500_000, transcendentals=0),
         name="pick",
     )(first, second)
-    far_near, far_next = trade(near_sent, near), trade(next_sent, next_chip)
+    far_next, far_near = trade(next_sent, next_chip), trade(near_sent, near)
 
     blocks = tangent_blocks.reshape(CAP // 8, 8, HALF, 128).transpose(0, 2, 1, 3).reshape(CAP * HALF, 128)
     high, low = pl.pallas_call(
@@ -246,7 +246,7 @@
         out_specs=(vmem,) * 4,
         scratch_shapes=[pltpu.VMEM((ROWS, MODES), full)],
         compiler_params=params,
-        cost_estimate=pl.CostEstimate(flops=300_000_000, bytes_accessed=2_500_000, transcendentals=0),
+        cost_estimate=pl.CostEstimate(flops=20_000_000_000, bytes_accessed=2_500_000, transcendentals=0),
         name="project_early",
     )(high, low, springs.reshape(1, ROWS), held, first, second, beside, beyond)
 
@@ -264,7 +264,7 @@
         compiler_params=params,
         cost_estimate=pl.CostEstimate(flops=80_000_000, bytes_accessed=700_000, transcendentals=0),
         name="reduce_late",
-    )(side, weight_high, weight_low, early, across, far_near, far_next)
+    )(side, weight_high, weight_low, early, far_next, across, far_near)
 
     stiff_image, done = pl.pallas_call(
         project_late,
@@ -274,7 +274,7 @@
         compiler_params=params,
         cost_estimate=pl.CostEstimate(flops=160_000_000, bytes_accessed=1_500_000, transcendentals=0),
         name="project_late",
-    )(high, low, total, across, far_near, far_next)
+    )(high, low, total, far_next, across, far_near)
 
     def swap(block, apart):
         return lax.ppermute(block, "row", [(d, d ^ apart) for d in range(n)])

time: 36.3 us -> 35.3 us (0.972)
  waiting for transfers between devices: 14.4 us -> 10.4 us
  starting transfers between devices: 13.5 us -> 16.6 us
    ppermute x5, waiting for transfers between devices: 9.65 us -> 7.27 us  [swap(): return lax.ppermute(block, 'row', [(d, d ^ apart) for d in range(n)])]
    ppermute x5, starting transfers between devices: 2.62 us -> 4.99 us  [swap(): return lax.ppermute(block, 'row', [(d, d ^ apart) for d in range(n)])]
    ppermute x7, waiting for transfers between devices: 4.78 us -> 3.15 us  [trade(): return lax.ppermute(block, 'row', [(d, partner(d) % n) for d in range(n)])]
    ppermute x7, starting transfers between devices: 10.9 us -> 11.6 us  [trade(): return lax.ppermute(block, 'row', [(d, partner(d) % n) for d in range(n)])]
where the time goes in v6:
time: 35.3 us; the launch traced here: 35.1 us
  starting transfers between devices  16.6 us (47%)
  waiting for transfers between devices  10.4 us (29%)
  Pallas kernels  5.65 us (16%)
  between operations  1.43 us (4%)
  local copies, waits for them, and re-layouts  0.99 us (3%)
    ppermute x7, starting transfers between devices, trade(): return lax.ppermute(block, 'row', [(d, partner(d) % n) for d in range(n)])  11.6 us
    ppermute x5, waiting for transfers between devices, swap(): return lax.ppermute(block, 'row', [(d, d ^ apart) for d in range(n)])  7.27 us
    ppermute x5, starting transfers between devices, swap(): return lax.ppermute(block, 'row', [(d, d ^ apart) for d in range(n)])  4.99 us
    ppermute x7, waiting for transfers between devices, trade(): return lax.ppermute(block, 'row', [(d, partner(d) % n) for d in range(n)])  3.15 us
    pallas_call x1, Pallas kernels, shards(): pl.pallas_call(assemble, out_shape=(jax.ShapeDtypeStruct((LINKS, ROWS, RO...  2.42 us
    pallas_call x1, Pallas kernels, shards(): pl.pallas_call(project_late, out_shape=(jax.ShapeDtypeStruct((ROWS, MODES...  1.13 us
    pallas_call x1, Pallas kernels, shards(): pl.pallas_call(project_early, out_shape=(jax.ShapeDtypeStruct((ROWS, MODE...  1.11 us
    unnamed x12, local copies, waits for them, and re-layouts  0.99 us
  transfers between devices with their start and end apart: 12, of which 8 were waited for; matrix products, arithmetic and copies ran while one was open for 0% of the time, Pallas kernels for 13%

profile of v6, /device:TPU:0, one launch (start us, length us, event | category | flops | bytes accessed | tf_op | source)
XLA Modules:
  0.0 35.1 jit_solution(3411401787865245237)
XLA Ops:
  0.6 0.0 copy-start.1
  0.7 5.1 %collective-permute-start = (f32[256,128]{1,0:T(8,128)}, f32[256,128]{1,0:T(8,128)S(1)}, u32[]{:S(2)}, u32[]{:S(2)}) collective-permute-start(f32[256,128]{1,0:T(8,128)} %basis_ref.1), channel_id=1, source_target_pairs={{0,12},{1,13},{2,14},{3,15},{4,8},{5,9},{6,10},{7,11},{8,4},{9,5},... | collective-permute-start | bytes 393224 | tf_op jit(solution)/shard_map/ppermute | solution.py:188
  5.8 0.0 collective-permute-start.1
  5.8 1.0 %copy-done.4 = f32[256,128]{1,0:T(8,128)S(1)} copy-done((f32[256,128]{1,0:T(8,128)S(1)}, f32[256,128]{1,0:T(8,128)}, u32[]{:S(2)}) %copy-start.4) | copy-done | bytes 131096
  6.8 0.0 copy-start.5
  6.8 0.1 collective-permute-start.2
  6.9 1.9 %collective-permute-start.3 = (f32[256,128]{1,0:T(8,128)S(1)}, f32[256,128]{1,0:T(8,128)S(1)}, u32[]{:S(2)}, u32[]{:S(2)}) collective-permute-start(f32[256,128]{1,0:T(8,128)S(1)} %prepare.1.refs_0_), channel_id=1, source_target_pairs={{0,15},{1,2},{2,1},{3,4},{4,3},{5,6},{6,5},{7,8},{8,7},{9,10},{10,... | collective-permute-start | bytes 393224 | tf_op jit(solution)/shard_map/ppermute | solution.py:188
  9.5 2.4 %assemble.1 = (bf16[8,256,256]{2,1,0:T(8,128)(2,1)S(1)}, bf16[8,256,256]{2,1,0:T(8,128)(2,1)S(1)}) custom-call(s32[1]{0:T(128)S(6)} %copy.9.count_ref, s32[128]{0:T(128)S(1)} %copy-done.1, s32[128]{0:T(128)S(1)} %bitcast.9, s32[128]{0:T(128)S(1)} %copy-done.3, f32[4096,128]{1,0:T(8,128)S(1)} %bitcast.8), custom_call_target="tpu_custom_call" | custom-call | flops 10000000 | bytes 8000000 | tf_op jit(solution)/shard_map/assemble/pallas_call | solution.py:218
  11.9 0.0 collective-permute-done.refs_1_.first_ref
  11.9 0.5 %collective-permute-done.1.refs_2_.second_ref = f32[256,128]{1,0:T(8,128)S(1)} collective-permute-done((f32[256,128]{1,0:T(8,128)}, f32[256,128]{1,0:T(8,128)S(1)}, u32[]{:S(2)}, u32[]{:S(2)}) %collective-permute-start.1) | collective-permute-done | bytes 131104 | tf_op jit(solution)/shard_map/ppermute | solution.py:188
  12.4 2.3 %collective-permute-start.4 = (f32[256,128]{1,0:T(8,128)S(1)}, f32[256,128]{1,0:T(8,128)S(1)}, u32[]{:S(2)}, u32[]{:S(2)}) collective-permute-start(f32[256,128]{1,0:T(8,128)S(1)} %get-tuple-element.17), channel_id=1, source_target_pairs={{0,15},{1,2},{2,1},{3,4},{4,3},{5,6},{6,5},{7,8},{8,7},{9,10},{10,... | collective-permute-start | bytes 393224 | tf_op jit(solution)/shard_map/ppermute | solution.py:188
  14.8 0.0 collective-permute-start.6
  14.8 2.1 %collective-permute-start.5 = (f32[256,128]{1,0:T(8,128)S(1)}, f32[256,128]{1,0:T(8,128)S(1)}, u32[]{:S(2)}, u32[]{:S(2)}) collective-permute-start(f32[256,128]{1,0:T(8,128)S(1)} %collective-permute-done.refs_1_.first_ref), channel_id=1, source_target_pairs={{0,4},{1,5},{2,6},{3,7},{4,0},{5,1},{6,2},{7,3},{8,12},{9,13},{10,... | collective-permute-start | bytes 393224 | tf_op jit(solution)/shard_map/ppermute | solution.py:188
  16.9 0.0 collective-permute-done.2.refs_3_
  16.9 0.0 collective-permute-done.3.refs_4_
  16.9 1.1 %project_early.1 = (f32[256,128]{1,0:T(8,128)S(1)}, f32[128,128]{1,0:T(8,128)S(1)}, bf16[3,128,256]{2,1,0:T(8,128)(2,1)S(1)}, bf16[3,128,256]{2,1,0:T(8,128)(2,1)S(1)}) custom-call(bf16[8,256,256]{2,1,0:T(8,128)(2,1)S(1)} %get-tuple-element.14.high_ref, bf16[8,256,256]{2,1,0:T(8,128)(2,1)S(1)} %get-tuple-element.15.low_ref, f32[1,256]{1,0:T(1,128)S(1)} %bitcast.10, ...), custom_call_target="tpu_custom_call" | custom-call | flops 20000000000 | bytes 2500000 | tf_op jit(solution)/shard_map/project_early/pallas_call | solution.py:237
  18.0 2.3 %collective-permute-done.4.refs_0_ = f32[256,128]{1,0:T(8,128)S(1)} collective-permute-done((f32[256,128]{1,0:T(8,128)S(1)}, f32[256,128]{1,0:T(8,128)S(1)}, u32[]{:S(2)}, u32[]{:S(2)}) %collective-permute-start.4) | collective-permute-done | bytes 131104 | tf_op jit(solution)/shard_map/ppermute | solution.py:188
  20.3 0.4 %collective-permute-done.5.refs_1_ = f32[256,128]{1,0:T(8,128)S(1)} collective-permute-done((f32[256,128]{1,0:T(8,128)S(1)}, f32[256,128]{1,0:T(8,128)S(1)}, u32[]{:S(2)}, u32[]{:S(2)}) %collective-permute-start.5) | collective-permute-done | bytes 131104 | tf_op jit(solution)/shard_map/ppermute | solution.py:188
  20.7 0.0 collective-permute-done.6.refs_2_
  20.7 0.3 reduce_late.1
  21.0 0.1 collective-permute-start.7
  21.1 1.2 %collective-permute-done.7 = f32[64,128]{1,0:T(8,128)S(1)} collective-permute-done((f32[64,128]{1,0:T(8,128)S(1)}, f32[64,128]{1,0:T(8,128)S(1)}, u32[]{:S(2)}, u32[]{:S(2)}) %collective-permute-start.7) | collective-permute-done | bytes 32800 | tf_op jit(solution)/shard_map/ppermute | solution.py:280
  22.3 1.6 %collective-permute-start.8 = (f32[64,128]{1,0:T(8,128)S(1)}, f32[64,128]{1,0:T(8,128)S(1)}, u32[]{:S(2)}, u32[]{:S(2)}) collective-permute-start(f32[64,128]{1,0:T(8,128)S(1)} %add.9.first_ref), channel_id=1, source_target_pairs={{0,3},{1,2},{2,1},{3,0},{4,7},{5,6},{6,5},{7,4},{8,11},{9,10},{10,... | collective-permute-start | bytes 98312 | tf_op jit(solution)/shard_map/ppermute | solution.py:280
  23.9 1.1 %project_late.1 = (f32[256,128]{1,0:T(8,128)}, f32[8,128]{1,0:T(8,128)S(1)}) custom-call(bf16[8,256,256]{2,1,0:T(8,128)(2,1)S(1)} %get-tuple-element.14.high_ref, bf16[8,256,256]{2,1,0:T(8,128)(2,1)S(1)} %get-tuple-element.15.low_ref, f32[256,128]{1,0:T(8,128)S(1)} %get-tuple-element.16.total_ref, f32[256,128]{1,0:T(8,128)S(1)} %collective-permute-done.4.refs_0_, ...), custom_call_target="tpu_custom_call" | custom-call | flops 160000000 | bytes 1500000 | tf_op jit(solution)/shard_map/project_late/pallas_call | solution.py:269
  25.1 0.6 %collective-permute-done.8.second_ref = f32[64,128]{1,0:T(8,128)S(1)} collective-permute-done((f32[64,128]{1,0:T(8,128)S(1)}, f32[64,128]{1,0:T(8,128)S(1)}, u32[]{:S(2)}, u32[]{:S(2)}) %collective-permute-start.8) | collective-permute-done | bytes 32800 | tf_op jit(solution)/shard_map/ppermute | solution.py:280
  25.7 1.6 %collective-permute-start.9 = (f32[64,128]{1,0:T(8,128)S(1)}, f32[64,128]{1,0:T(8,128)S(1)}, u32[]{:S(2)}, u32[]{:S(2)}) collective-permute-start(f32[64,128]{1,0:T(8,128)S(1)} %add_after.1), channel_id=1, source_target_pairs={{0,5},{1,4},{2,7},{3,6},{4,1},{5,0},{6,3},{7,2},{8,13},{9,12},{10,... | collective-permute-start | bytes 98312 | tf_op jit(solution)/shard_map/ppermute | solution.py:280
  27.3 1.7 %collective-permute-done.9 = f32[64,128]{1,0:T(8,128)S(1)} collective-permute-done((f32[64,128]{1,0:T(8,128)S(1)}, f32[64,128]{1,0:T(8,128)S(1)}, u32[]{:S(2)}, u32[]{:S(2)}) %collective-permute-start.9) | collective-permute-done | bytes 32800 | tf_op jit(solution)/shard_map/ppermute | solution.py:280
  29.0 1.5 %collective-permute-start.10 = (f32[64,128]{1,0:T(8,128)S(1)}, f32[64,128]{1,0:T(8,128)S(1)}, u32[]{:S(2)}, u32[]{:S(2)}) collective-permute-start(f32[64,128]{1,0:T(8,128)S(1)} %add.10), channel_id=1, source_target_pairs={{0,9},{1,8},{2,11},{3,10},{4,13},{5,12},{6,15},{7,14},{8,1},{9,0},... | collective-permute-start | bytes 98312 | tf_op jit(solution)/shard_map/ppermute | solution.py:280
  30.5 2.8 %collective-permute-done.10 = f32[64,128]{1,0:T(8,128)S(1)} collective-permute-done((f32[64,128]{1,0:T(8,128)S(1)}, f32[64,128]{1,0:T(8,128)S(1)}, u32[]{:S(2)}, u32[]{:S(2)}) %collective-permute-start.10) | collective-permute-done | bytes 32800 | tf_op jit(solution)/shard_map/ppermute | solution.py:280
  33.3 0.2 collective-permute-start.11
  33.5 1.0 %collective-permute-done.11.other_ref = f32[64,128]{1,0:T(8,128)S(1)} collective-permute-done((f32[64,128]{1,0:T(8,128)S(1)}, f32[64,128]{1,0:T(8,128)S(1)}, u32[]{:S(2)}, u32[]{:S(2)}) %collective-permute-start.11) | collective-permute-done | bytes 32800 | tf_op jit(solution)/shard_map/ppermute | solution.py:280
  34.5 0.6 %join.1 = f32[128,128]{1,0:T(8,128)} custom-call(s32[1]{0:T(128)} %bitcast.5.side_ref, f32[64,128]{1,0:T(8,128)S(1)} %add.11.mine_ref, f32[64,128]{1,0:T(8,128)S(1)} %collective-permute-done.11.other_ref), custom_call_target="tpu_custom_call" | custom-call | bytes 130000 | tf_op jit(solution)/shard_map/join/pallas_call | solution.py:295
  (15 shorter events, 0.1 us)
Async XLA Ops:
  0.6 8.8 %copy-start.1 = (s32[128]{0:T(128)S(1)}, s32[128]{0:T(128)}, u32[]{:S(2)}) copy-start(s32[128]{0:T(128)} %rows_ref.1) | copy-start | bytes 1540
  0.6 8.8 %copy-start.2 = (s32[128,1]{0,1:T(1,128)S(1)}, s32[128,1]{0,1:T(1,128)}, u32[]{:S(2)}) copy-start(s32[128,1]{0,1:T(1,128)} %param.11) | copy-start | bytes 1540
  0.7 8.8 %copy-start.3 = (s32[128]{0:T(128)S(1)}, s32[128]{0:T(128)}, u32[]{:S(2)}) copy-start(s32[128]{0:T(128)} %offset_ref.1) | copy-start | bytes 1540
  0.7 8.8 %copy-start = (f32[128,4096]{1,0:T(8,128)S(1)}, f32[128,4096]{1,0:T(8,128)}, u32[]{:S(2)}) copy-start(f32[128,4096]{1,0:T(8,128)} %param.9) | copy-start | bytes 6291460
  0.7 11.2 %collective-permute-start = (f32[256,128]{1,0:T(8,128)}, f32[256,128]{1,0:T(8,128)S(1)}, u32[]{:S(2)}, u32[]{:S(2)}) collective-permute-start(f32[256,128]{1,0:T(8,128)} %basis_ref.1), channel_id=1, source_target_pairs={{0,12},{1,13},{2,14},{3,15},{4,8},{5,9},{6,10},{7,11},{8,4},{9,5},... | collective-permute-start | bytes 393224 | tf_op jit(solution)/shard_map/ppermute | solution.py:188
  5.8 6.6 %collective-permute-start.1 = (f32[256,128]{1,0:T(8,128)}, f32[256,128]{1,0:T(8,128)S(1)}, u32[]{:S(2)}, u32[]{:S(2)}) collective-permute-start(f32[256,128]{1,0:T(8,128)} %basis_ref.1), channel_id=1, source_target_pairs={{0,4},{1,5},{2,6},{3,7},{4,0},{5,1},{6,2},{7,3},{8,12},{9,13},{10,... | collective-permute-start | bytes 393224 | tf_op jit(solution)/shard_map/ppermute | solution.py:188
  5.8 1.0 %copy-start.4 = (f32[256,128]{1,0:T(8,128)S(1)}, f32[256,128]{1,0:T(8,128)}, u32[]{:S(2)}) copy-start(f32[256,128]{1,0:T(8,128)} %basis_ref.1) | copy-start | bytes 393220
  6.8 10.2 %copy-start.5 = (f32[256]{0:T(256)S(1)}, f32[256]{0:T(256)}, u32[]{:S(2)}) copy-start(f32[256]{0:T(256)} %param.8) | copy-start | bytes 3076
  6.8 10.1 %collective-permute-start.2 = (f32[256,128]{1,0:T(8,128)S(1)}, f32[256,128]{1,0:T(8,128)S(1)}, u32[]{:S(2)}, u32[]{:S(2)}) collective-permute-start(f32[256,128]{1,0:T(8,128)S(1)} %prepare.1.refs_0_), channel_id=1, source_target_pairs={{0,1},{1,0},{2,3},{3,2},{4,5},{5,4},{6,7},{7,6},{8,9},{9,8},{10,11... | collective-permute-start | bytes 393224 | tf_op jit(solution)/shard_map/ppermute | solution.py:188
  6.9 10.1 %collective-permute-start.3 = (f32[256,128]{1,0:T(8,128)S(1)}, f32[256,128]{1,0:T(8,128)S(1)}, u32[]{:S(2)}, u32[]{:S(2)}) collective-permute-start(f32[256,128]{1,0:T(8,128)S(1)} %prepare.1.refs_0_), channel_id=1, source_target_pairs={{0,15},{1,2},{2,1},{3,4},{4,3},{5,6},{6,5},{7,8},{8,7},{9,10},{10,... | collective-permute-start | bytes 393224 | tf_op jit(solution)/shard_map/ppermute | solution.py:188
  12.4 7.9 %collective-permute-start.4 = (f32[256,128]{1,0:T(8,128)S(1)}, f32[256,128]{1,0:T(8,128)S(1)}, u32[]{:S(2)}, u32[]{:S(2)}) collective-permute-start(f32[256,128]{1,0:T(8,128)S(1)} %get-tuple-element.17), channel_id=1, source_target_pairs={{0,15},{1,2},{2,1},{3,4},{4,3},{5,6},{6,5},{7,8},{8,7},{9,10},{10,... | collective-permute-start | bytes 393224 | tf_op jit(solution)/shard_map/ppermute | solution.py:188
  14.8 5.9 %collective-permute-start.6 = (f32[256,128]{1,0:T(8,128)S(1)}, f32[256,128]{1,0:T(8,128)S(1)}, u32[]{:S(2)}, u32[]{:S(2)}) collective-permute-start(f32[256,128]{1,0:T(8,128)S(1)} %get-tuple-element.18), channel_id=1, source_target_pairs={{0,1},{1,0},{2,3},{3,2},{4,5},{5,4},{6,7},{7,6},{8,9},{9,8},{10,11... | collective-permute-start | bytes 393224 | tf_op jit(solution)/shard_map/ppermute | solution.py:188
  14.8 5.9 %collective-permute-start.5 = (f32[256,128]{1,0:T(8,128)S(1)}, f32[256,128]{1,0:T(8,128)S(1)}, u32[]{:S(2)}, u32[]{:S(2)}) collective-permute-start(f32[256,128]{1,0:T(8,128)S(1)} %collective-permute-done.refs_1_.first_ref), channel_id=1, source_target_pairs={{0,4},{1,5},{2,6},{3,7},{4,0},{5,1},{6,2},{7,3},{8,12},{9,13},{10,... | collective-permute-start | bytes 393224 | tf_op jit(solution)/shard_map/ppermute | solution.py:188
  21.0 1.3 %collective-permute-start.7 = (f32[64,128]{1,0:T(8,128)S(1)}, f32[64,128]{1,0:T(8,128)S(1)}, u32[]{:S(2)}, u32[]{:S(2)}) collective-permute-start(f32[64,128]{1,0:T(8,128)S(1)} %get-tuple-element.24), channel_id=1, source_target_pairs={{0,1},{1,0},{2,3},{3,2},{4,5},{5,4},{6,7},{7,6},{8,9},{9,8},{10,11... | collective-permute-start | bytes 98312 | tf_op jit(solution)/shard_map/ppermute | solution.py:280
  22.3 3.3 %collective-permute-start.8 = (f32[64,128]{1,0:T(8,128)S(1)}, f32[64,128]{1,0:T(8,128)S(1)}, u32[]{:S(2)}, u32[]{:S(2)}) collective-permute-start(f32[64,128]{1,0:T(8,128)S(1)} %add.9.first_ref), channel_id=1, source_target_pairs={{0,3},{1,2},{2,1},{3,0},{4,7},{5,6},{6,5},{7,4},{8,11},{9,10},{10,... | collective-permute-start | bytes 98312 | tf_op jit(solution)/shard_map/ppermute | solution.py:280
  25.7 3.3 %collective-permute-start.9 = (f32[64,128]{1,0:T(8,128)S(1)}, f32[64,128]{1,0:T(8,128)S(1)}, u32[]{:S(2)}, u32[]{:S(2)}) collective-permute-start(f32[64,128]{1,0:T(8,128)S(1)} %add_after.1), channel_id=1, source_target_pairs={{0,5},{1,4},{2,7},{3,6},{4,1},{5,0},{6,3},{7,2},{8,13},{9,12},{10,... | collective-permute-start | bytes 98312 | tf_op jit(solution)/shard_map/ppermute | solution.py:280
  29.0 4.2 %collective-permute-start.10 = (f32[64,128]{1,0:T(8,128)S(1)}, f32[64,128]{1,0:T(8,128)S(1)}, u32[]{:S(2)}, u32[]{:S(2)}) collective-permute-start(f32[64,128]{1,0:T(8,128)S(1)} %add.10), channel_id=1, source_target_pairs={{0,9},{1,8},{2,11},{3,10},{4,13},{5,12},{6,15},{7,14},{8,1},{9,0},... | collective-permute-start | bytes 98312 | tf_op jit(solution)/shard_map/ppermute | solution.py:280
  33.3 1.2 %collective-permute-start.11 = (f32[64,128]{1,0:T(8,128)S(1)}, f32[64,128]{1,0:T(8,128)S(1)}, u32[]{:S(2)}, u32[]{:S(2)}) collective-permute-start(f32[64,128]{1,0:T(8,128)S(1)} %add.11.mine_ref), channel_id=1, source_target_pairs={{0,1},{1,0},{2,3},{3,2},{4,5},{5,4},{6,7},{7,6},{8,9},{9,8},{10,11... | collective-permute-start | bytes 98312 | tf_op jit(solution)/shard_map/ppermute | solution.py:280

commit v7 on v6

--- a/solution.py
+++ b/solution.py
@@ -145,13 +145,14 @@
         one_of(4, even_four),
         one_of(1, even),
         one_of(n - 1, even),
+        n // 2,
         one_of(n - 5, even),
-        n // 2,
         one_of(5, even),
     )
 
 
-def pick(first_ref, second_ref, near_ref, next_ref):
+def pick(first_ref, second_ref, outer_ref, next_ref, near_ref):
+    outer_ref[...] = first_ref[...]
     me = lax.axis_index("row")
     straight = (me % 2 == 1) == ((me // 4) % 2 == 0)
 
@@ -201,17 +202,17 @@
 
     first = trade(basis, inner)
     second = trade(basis, outer)
-    across = trade(first, outer) if n == 16 else trade(held, lambda d: d + n // 2)
     beside, beyond = trade(held, near), trade(held, next_chip)
-    near_sent, next_sent = pl.pallas_call(
+    outer_sent, next_sent, near_sent = pl.pallas_call(
         pick,
-        out_shape=(jax.ShapeDtypeStruct((ROWS, MODES), full),) * 2,
+        out_shape=(jax.ShapeDtypeStruct((ROWS, MODES), full),) * 3,
         in_specs=[vmem] * 2,
-        out_specs=(vmem,) * 2,
-        compiler_params=params,
-        cost_estimate=pl.CostEstimate(flops=0, bytes_accessed=500_000, transcendentals=0),
+        out_specs=(vmem,) * 3,
+        compiler_params=params,
+        cost_estimate=pl.CostEstimate(flops=0, bytes_accessed=700_000, transcendentals=0),
         name="pick",
     )(first, second)
+    across = trade(outer_sent, outer) if n == 16 else trade(held, lambda d: d + n // 2)
     far_next, far_near = trade(next_sent, next_chip), trade(near_sent, near)
 
     blocks = tangent_blocks.reshape(CAP // 8, 8, HALF, 128).transpose(0, 2, 1, 3).reshape(CAP * HALF, 128)
@@ -264,7 +265,7 @@
         compiler_params=params,
         cost_estimate=pl.CostEstimate(flops=80_000_000, bytes_accessed=700_000, transcendentals=0),
         name="reduce_late",
-    )(side, weight_high, weight_low, early, far_next, across, far_near)
+    )(side, weight_high, weight_low, early, across, far_next, far_near)
 
     stiff_image, done = pl.pallas_call(
         project_late,
@@ -274,7 +275,7 @@
         compiler_params=params,
         cost_estimate=pl.CostEstimate(flops=160_000_000, bytes_accessed=1_500_000, transcendentals=0),
         name="project_late",
-    )(high, low, total, far_next, across, far_near)
+    )(high, low, total, across, far_next, far_near)
 
     def swap(block, apart):
         return lax.ppermute(block, "row", [(d, d ^ apart) for d in range(n)])

time: 35.3 us -> 36.4 us (1.031)
  waiting for transfers between devices: 10.4 us -> 15.8 us
  starting transfers between devices: 16.6 us -> 12.2 us
    ppermute x5, waiting for transfers between devices: 7.27 us -> 12.3 us  [swap(): return lax.ppermute(block, 'row', [(d, d ^ apart) for d in range(n)])]
    ppermute x5, starting transfers between devices: 4.99 us -> 0.55 us  [swap(): return lax.ppermute(block, 'row', [(d, d ^ apart) for d in range(n)])]
  transfers between devices with their start and end apart: 12 -> 12, of which waited for: 8 -> 7; matrix products, arithmetic and copies ran while one was open for 0% -> 0% of each run, Pallas kernels for 13% -> 14%
where the time goes in v7:
time: 36.4 us; the launch traced here: 36.3 us
  waiting for transfers between devices  15.8 us (43%)
  starting transfers between devices  12.2 us (34%)
  Pallas kernels  5.88 us (16%)
  between operations  1.45 us (4%)
  local copies, waits for them, and re-layouts  0.99 us (3%)
    ppermute x5, waiting for transfers between devices, swap(): return lax.ppermute(block, 'row', [(d, d ^ apart) for d in range(n)])  12.3 us
    ppermute x7, starting transfers between devices, trade(): return lax.ppermute(block, 'row', [(d, partner(d) % n) for d in range(n)])  11.6 us
    ppermute x7, waiting for transfers between devices, trade(): return lax.ppermute(block, 'row', [(d, partner(d) % n) for d in range(n)])  3.49 us
    pallas_call x1, Pallas kernels, shards(): pl.pallas_call(assemble, out_shape=(jax.ShapeDtypeStruct((LINKS, ROWS, RO...  2.64 us
    pallas_call x1, Pallas kernels, shards(): pl.pallas_call(project_late, out_shape=(jax.ShapeDtypeStruct((ROWS, MODES...  1.13 us
    pallas_call x1, Pallas kernels, shards(): pl.pallas_call(project_early, out_shape=(jax.ShapeDtypeStruct((ROWS, MODE...  1.11 us
    unnamed x12, local copies, waits for them, and re-layouts  0.99 us
  transfers between devices with their start and end apart: 12, of which 7 were waited for; matrix products, arithmetic and copies ran while one was open for 0% of the time, Pallas kernels for 14%

profile of v7, /device:TPU:0, one launch (start us, length us, event | category | flops | bytes accessed | tf_op | source)
XLA Modules:
  0.0 36.3 jit_solution(18020249547456891679)
XLA Ops:
  0.7 5.1 %collective-permute-start = (f32[256,128]{1,0:T(8,128)}, f32[256,128]{1,0:T(8,128)S(1)}, u32[]{:S(2)}, u32[]{:S(2)}) collective-permute-start(f32[256,128]{1,0:T(8,128)} %basis_ref.1), channel_id=1, source_target_pairs={{0,12},{1,13},{2,14},{3,15},{4,8},{5,9},{6,10},{7,11},{8,4},{9,5},... | collective-permute-start | bytes 393224 | tf_op jit(solution)/shard_map/ppermute | solution.py:189
  5.8 0.0 collective-permute-start.1
  5.8 1.0 %copy-done.4 = f32[256,128]{1,0:T(8,128)S(1)} copy-done((f32[256,128]{1,0:T(8,128)S(1)}, f32[256,128]{1,0:T(8,128)}, u32[]{:S(2)}) %copy-start.4) | copy-done | bytes 131096
  6.8 0.0 copy-start.5
  6.8 0.1 collective-permute-start.2
  6.9 1.9 %collective-permute-start.3 = (f32[256,128]{1,0:T(8,128)S(1)}, f32[256,128]{1,0:T(8,128)S(1)}, u32[]{:S(2)}, u32[]{:S(2)}) collective-permute-start(f32[256,128]{1,0:T(8,128)S(1)} %prepare.1.refs_0_), channel_id=1, source_target_pairs={{0,15},{1,2},{2,1},{3,4},{4,3},{5,6},{6,5},{7,8},{8,7},{9,10},{10,... | collective-permute-start | bytes 393224 | tf_op jit(solution)/shard_map/ppermute | solution.py:189
  9.4 0.0 copy-done.1
  9.5 2.6 %assemble.1 = (bf16[8,256,256]{2,1,0:T(8,128)(2,1)S(1)}, bf16[8,256,256]{2,1,0:T(8,128)(2,1)S(1)}) custom-call(s32[1]{0:T(128)S(6)} %copy.9.count_ref, s32[128]{0:T(128)S(1)} %copy-done.1, s32[128]{0:T(128)S(1)} %bitcast.9, s32[128]{0:T(128)S(1)} %copy-done.3, f32[4096,128]{1,0:T(8,128)S(1)} %bitcast.8), custom_call_target="tpu_custom_call" | custom-call | flops 10000000 | bytes 8000000 | tf_op jit(solution)/shard_map/assemble/pallas_call | solution.py:219
  12.1 0.0 collective-permute-done.refs_1_.first_ref
  12.1 0.3 collective-permute-done.1.refs_2_.second_ref
  12.4 1.8 %collective-permute-start.4 = (f32[256,128]{1,0:T(8,128)S(1)}, f32[256,128]{1,0:T(8,128)S(1)}, u32[]{:S(2)}, u32[]{:S(2)}) collective-permute-start(f32[256,128]{1,0:T(8,128)S(1)} %get-tuple-element.18), channel_id=1, source_target_pairs={{0,4},{1,5},{2,6},{3,7},{4,0},{5,1},{6,2},{7,3},{8,12},{9,13},{10,... | collective-permute-start | bytes 393224 | tf_op jit(solution)/shard_map/ppermute | solution.py:189
  14.2 0.6 %collective-permute-start.5 = (f32[256,128]{1,0:T(8,128)S(1)}, f32[256,128]{1,0:T(8,128)S(1)}, u32[]{:S(2)}, u32[]{:S(2)}) collective-permute-start(f32[256,128]{1,0:T(8,128)S(1)} %get-tuple-element.19), channel_id=1, source_target_pairs={{0,15},{1,2},{2,1},{3,4},{4,3},{5,6},{6,5},{7,8},{8,7},{9,10},{10,... | collective-permute-start | bytes 393224 | tf_op jit(solution)/shard_map/ppermute | solution.py:189
  14.8 2.2 %collective-permute-start.6 = (f32[256,128]{1,0:T(8,128)S(1)}, f32[256,128]{1,0:T(8,128)S(1)}, u32[]{:S(2)}, u32[]{:S(2)}) collective-permute-start(f32[256,128]{1,0:T(8,128)S(1)} %get-tuple-element.20), channel_id=1, source_target_pairs={{0,1},{1,0},{2,3},{3,2},{4,5},{5,4},{6,7},{7,6},{8,9},{9,8},{10,11... | collective-permute-start | bytes 393224 | tf_op jit(solution)/shard_map/ppermute | solution.py:189
  16.9 0.0 collective-permute-done.2.refs_3_
  16.9 0.0 collective-permute-done.3.refs_4_
  16.9 1.1 %project_early.1 = (f32[256,128]{1,0:T(8,128)S(1)}, f32[128,128]{1,0:T(8,128)S(1)}, bf16[3,128,256]{2,1,0:T(8,128)(2,1)S(1)}, bf16[3,128,256]{2,1,0:T(8,128)(2,1)S(1)}) custom-call(bf16[8,256,256]{2,1,0:T(8,128)(2,1)S(1)} %get-tuple-element.15.high_ref, bf16[8,256,256]{2,1,0:T(8,128)(2,1)S(1)} %get-tuple-element.16.low_ref, f32[1,256]{1,0:T(1,128)S(1)} %bitcast.10, ...), custom_call_target="tpu_custom_call" | custom-call | flops 20000000000 | bytes 2500000 | tf_op jit(solution)/shard_map/project_early/pallas_call | solution.py:238
  18.1 0.0 collective-permute-done.4.refs_0_
  18.1 3.2 %collective-permute-done.5.refs_1_ = f32[256,128]{1,0:T(8,128)S(1)} collective-permute-done((f32[256,128]{1,0:T(8,128)S(1)}, f32[256,128]{1,0:T(8,128)S(1)}, u32[]{:S(2)}, u32[]{:S(2)}) %collective-permute-start.5) | collective-permute-done | bytes 131104 | tf_op jit(solution)/shard_map/ppermute | solution.py:189
  21.3 0.0 collective-permute-done.6.refs_2_
  21.3 0.3 reduce_late.1
  21.6 0.1 collective-permute-start.7
  21.7 1.2 %collective-permute-done.7 = f32[64,128]{1,0:T(8,128)S(1)} collective-permute-done((f32[64,128]{1,0:T(8,128)S(1)}, f32[64,128]{1,0:T(8,128)S(1)}, u32[]{:S(2)}, u32[]{:S(2)}) %collective-permute-start.7) | collective-permute-done | bytes 32800 | tf_op jit(solution)/shard_map/ppermute | solution.py:281
  22.9 0.4 collective-permute-start.8
  23.3 1.1 %project_late.1 = (f32[256,128]{1,0:T(8,128)}, f32[8,128]{1,0:T(8,128)S(1)}) custom-call(bf16[8,256,256]{2,1,0:T(8,128)(2,1)S(1)} %get-tuple-element.15.high_ref, bf16[8,256,256]{2,1,0:T(8,128)(2,1)S(1)} %get-tuple-element.16.low_ref, f32[256,128]{1,0:T(8,128)S(1)} %get-tuple-element.17.total_ref, f32[256,128]{1,0:T(8,128)S(1)} %collective-permute-done.4.refs_0_, ...), custom_call_target="tpu_custom_call" | custom-call | flops 160000000 | bytes 1500000 | tf_op jit(solution)/shard_map/project_late/pallas_call | solution.py:270
  24.4 1.9 %collective-permute-done.8.second_ref = f32[64,128]{1,0:T(8,128)S(1)} collective-permute-done((f32[64,128]{1,0:T(8,128)S(1)}, f32[64,128]{1,0:T(8,128)S(1)}, u32[]{:S(2)}, u32[]{:S(2)}) %collective-permute-start.8) | collective-permute-done | bytes 32800 | tf_op jit(solution)/shard_map/ppermute | solution.py:281
  26.3 0.0 collective-permute-start.9
  26.3 3.3 %collective-permute-done.9 = f32[64,128]{1,0:T(8,128)S(1)} collective-permute-done((f32[64,128]{1,0:T(8,128)S(1)}, f32[64,128]{1,0:T(8,128)S(1)}, u32[]{:S(2)}, u32[]{:S(2)}) %collective-permute-start.9) | collective-permute-done | bytes 32800 | tf_op jit(solution)/shard_map/ppermute | solution.py:281
  29.6 0.0 collective-permute-start.10
  29.6 4.8 %collective-permute-done.10 = f32[64,128]{1,0:T(8,128)S(1)} collective-permute-done((f32[64,128]{1,0:T(8,128)S(1)}, f32[64,128]{1,0:T(8,128)S(1)}, u32[]{:S(2)}, u32[]{:S(2)}) %collective-permute-start.10) | collective-permute-done | bytes 32800 | tf_op jit(solution)/shard_map/ppermute | solution.py:281
  34.4 0.1 collective-permute-start.11
  34.5 1.1 %collective-permute-done.11.other_ref = f32[64,128]{1,0:T(8,128)S(1)} collective-permute-done((f32[64,128]{1,0:T(8,128)S(1)}, f32[64,128]{1,0:T(8,128)S(1)}, u32[]{:S(2)}, u32[]{:S(2)}) %collective-permute-start.11) | collective-permute-done | bytes 32800 | tf_op jit(solution)/shard_map/ppermute | solution.py:281
  35.6 0.6 %join.1 = f32[128,128]{1,0:T(8,128)} custom-call(s32[1]{0:T(128)} %bitcast.5.side_ref, f32[64,128]{1,0:T(8,128)S(1)} %add.11.mine_ref, f32[64,128]{1,0:T(8,128)S(1)} %collective-permute-done.11.other_ref), custom_call_target="tpu_custom_call" | custom-call | bytes 130000 | tf_op jit(solution)/shard_map/join/pallas_call | solution.py:296
  (15 shorter events, 0.1 us)
Async XLA Ops:
  0.6 8.8 %copy-start.1 = (s32[128]{0:T(128)S(1)}, s32[128]{0:T(128)}, u32[]{:S(2)}) copy-start(s32[128]{0:T(128)} %rows_ref.1) | copy-start | bytes 1540
  0.6 8.8 %copy-start.2 = (s32[128,1]{0,1:T(1,128)S(1)}, s32[128,1]{0,1:T(1,128)}, u32[]{:S(2)}) copy-start(s32[128,1]{0,1:T(1,128)} %param.11) | copy-start | bytes 1540
  0.7 8.8 %copy-start.3 = (s32[128]{0:T(128)S(1)}, s32[128]{0:T(128)}, u32[]{:S(2)}) copy-start(s32[128]{0:T(128)} %offset_ref.1) | copy-start | bytes 1540
  0.7 8.8 %copy-start = (f32[128,4096]{1,0:T(8,128)S(1)}, f32[128,4096]{1,0:T(8,128)}, u32[]{:S(2)}) copy-start(f32[128,4096]{1,0:T(8,128)} %param.9) | copy-start | bytes 6291460
  0.7 11.5 %collective-permute-start = (f32[256,128]{1,0:T(8,128)}, f32[256,128]{1,0:T(8,128)S(1)}, u32[]{:S(2)}, u32[]{:S(2)}) collective-permute-start(f32[256,128]{1,0:T(8,128)} %basis_ref.1), channel_id=1, source_target_pairs={{0,12},{1,13},{2,14},{3,15},{4,8},{5,9},{6,10},{7,11},{8,4},{9,5},... | collective-permute-start | bytes 393224 | tf_op jit(solution)/shard_map/ppermute | solution.py:189
  5.8 6.6 %collective-permute-start.1 = (f32[256,128]{1,0:T(8,128)}, f32[256,128]{1,0:T(8,128)S(1)}, u32[]{:S(2)}, u32[]{:S(2)}) collective-permute-start(f32[256,128]{1,0:T(8,128)} %basis_ref.1), channel_id=1, source_target_pairs={{0,4},{1,5},{2,6},{3,7},{4,0},{5,1},{6,2},{7,3},{8,12},{9,13},{10,... | collective-permute-start | bytes 393224 | tf_op jit(solution)/shard_map/ppermute | solution.py:189
  5.8 1.0 %copy-start.4 = (f32[256,128]{1,0:T(8,128)S(1)}, f32[256,128]{1,0:T(8,128)}, u32[]{:S(2)}) copy-start(f32[256,128]{1,0:T(8,128)} %basis_ref.1) | copy-start | bytes 393220
  6.8 10.2 %copy-start.5 = (f32[256]{0:T(256)S(1)}, f32[256]{0:T(256)}, u32[]{:S(2)}) copy-start(f32[256]{0:T(256)} %param.8) | copy-start | bytes 3076
  6.8 10.2 %collective-permute-start.2 = (f32[256,128]{1,0:T(8,128)S(1)}, f32[256,128]{1,0:T(8,128)S(1)}, u32[]{:S(2)}, u32[]{:S(2)}) collective-permute-start(f32[256,128]{1,0:T(8,128)S(1)} %prepare.1.refs_0_), channel_id=1, source_target_pairs={{0,1},{1,0},{2,3},{3,2},{4,5},{5,4},{6,7},{7,6},{8,9},{9,8},{10,11... | collective-permute-start | bytes 393224 | tf_op jit(solution)/shard_map/ppermute | solution.py:189
  6.9 10.1 %collective-permute-start.3 = (f32[256,128]{1,0:T(8,128)S(1)}, f32[256,128]{1,0:T(8,128)S(1)}, u32[]{:S(2)}, u32[]{:S(2)}) collective-permute-start(f32[256,128]{1,0:T(8,128)S(1)} %prepare.1.refs_0_), channel_id=1, source_target_pairs={{0,15},{1,2},{2,1},{3,4},{4,3},{5,6},{6,5},{7,8},{8,7},{9,10},{10,... | collective-permute-start | bytes 393224 | tf_op jit(solution)/shard_map/ppermute | solution.py:189
  12.4 5.6 %collective-permute-start.4 = (f32[256,128]{1,0:T(8,128)S(1)}, f32[256,128]{1,0:T(8,128)S(1)}, u32[]{:S(2)}, u32[]{:S(2)}) collective-permute-start(f32[256,128]{1,0:T(8,128)S(1)} %get-tuple-element.18), channel_id=1, source_target_pairs={{0,4},{1,5},{2,6},{3,7},{4,0},{5,1},{6,2},{7,3},{8,12},{9,13},{10,... | collective-permute-start | bytes 393224 | tf_op jit(solution)/shard_map/ppermute | solution.py:189
  14.2 7.1 %collective-permute-start.5 = (f32[256,128]{1,0:T(8,128)S(1)}, f32[256,128]{1,0:T(8,128)S(1)}, u32[]{:S(2)}, u32[]{:S(2)}) collective-permute-start(f32[256,128]{1,0:T(8,128)S(1)} %get-tuple-element.19), channel_id=1, source_target_pairs={{0,15},{1,2},{2,1},{3,4},{4,3},{5,6},{6,5},{7,8},{8,7},{9,10},{10,... | collective-permute-start | bytes 393224 | tf_op jit(solution)/shard_map/ppermute | solution.py:189
  14.8 6.5 %collective-permute-start.6 = (f32[256,128]{1,0:T(8,128)S(1)}, f32[256,128]{1,0:T(8,128)S(1)}, u32[]{:S(2)}, u32[]{:S(2)}) collective-permute-start(f32[256,128]{1,0:T(8,128)S(1)} %get-tuple-element.20), channel_id=1, source_target_pairs={{0,1},{1,0},{2,3},{3,2},{4,5},{5,4},{6,7},{7,6},{8,9},{9,8},{10,11... | collective-permute-start | bytes 393224 | tf_op jit(solution)/shard_map/ppermute | solution.py:189
  21.6 1.3 %collective-permute-start.7 = (f32[64,128]{1,0:T(8,128)S(1)}, f32[64,128]{1,0:T(8,128)S(1)}, u32[]{:S(2)}, u32[]{:S(2)}) collective-permute-start(f32[64,128]{1,0:T(8,128)S(1)} %get-tuple-element.26), channel_id=1, source_target_pairs={{0,1},{1,0},{2,3},{3,2},{4,5},{5,4},{6,7},{7,6},{8,9},{9,8},{10,11... | collective-permute-start | bytes 98312 | tf_op jit(solution)/shard_map/ppermute | solution.py:281
  22.9 3.3 %collective-permute-start.8 = (f32[64,128]{1,0:T(8,128)S(1)}, f32[64,128]{1,0:T(8,128)S(1)}, u32[]{:S(2)}, u32[]{:S(2)}) collective-permute-start(f32[64,128]{1,0:T(8,128)S(1)} %add.9.first_ref), channel_id=1, source_target_pairs={{0,3},{1,2},{2,1},{3,0},{4,7},{5,6},{6,5},{7,4},{8,11},{9,10},{10,... | collective-permute-start | bytes 98312 | tf_op jit(solution)/shard_map/ppermute | solution.py:281
  26.3 3.3 %collective-permute-start.9 = (f32[64,128]{1,0:T(8,128)S(1)}, f32[64,128]{1,0:T(8,128)S(1)}, u32[]{:S(2)}, u32[]{:S(2)}) collective-permute-start(f32[64,128]{1,0:T(8,128)S(1)} %add_after.1), channel_id=1, source_target_pairs={{0,5},{1,4},{2,7},{3,6},{4,1},{5,0},{6,3},{7,2},{8,13},{9,12},{10,... | collective-permute-start | bytes 98312 | tf_op jit(solution)/shard_map/ppermute | solution.py:281
  29.6 4.8 %collective-permute-start.10 = (f32[64,128]{1,0:T(8,128)S(1)}, f32[64,128]{1,0:T(8,128)S(1)}, u32[]{:S(2)}, u32[]{:S(2)}) collective-permute-start(f32[64,128]{1,0:T(8,128)S(1)} %add.10), channel_id=1, source_target_pairs={{0,9},{1,8},{2,11},{3,10},{4,13},{5,12},{6,15},{7,14},{8,1},{9,0},... | collective-permute-start | bytes 98312 | tf_op jit(solution)/shard_map/ppermute | solution.py:281
  34.4 1.2 %collective-permute-start.11 = (f32[64,128]{1,0:T(8,128)S(1)}, f32[64,128]{1,0:T(8,128)S(1)}, u32[]{:S(2)}, u32[]{:S(2)}) collective-permute-start(f32[64,128]{1,0:T(8,128)S(1)} %add.11.mine_ref), channel_id=1, source_target_pairs={{0,1},{1,0},{2,3},{3,2},{4,5},{5,4},{6,7},{7,6},{8,9},{9,8},{10,11... | collective-permute-start | bytes 98312 | tf_op jit(solution)/shard_map/ppermute | solution.py:281

commit v8 on v7

--- a/solution.py
+++ b/solution.py
@@ -37,7 +37,7 @@
     held_ref[...] = basis_ref[...]
 
 
-def assemble(count_ref, rows_ref, owner_ref, offset_ref, blocks_ref, high_ref, low_ref, dense, placed, place, arrived):
+def assemble(count_ref, rows_ref, owner_ref, offset_ref, blocks_ref, held_ref, high_ref, low_ref, again_ref, dense, placed, place, arrived):
     n, me = lax.axis_size("row"), lax.axis_index("row")
     away = lax.rem(owner_ref[...].reshape(1, CAP) - me + n, n)
     link = jnp.zeros_like(away)
@@ -49,6 +49,7 @@
     copy = pltpu.make_async_copy(placed, place, arrived)
     copy.start()
     dense[...] = jnp.zeros_like(dense)
+    again_ref[...] = held_ref[...]
     copy.wait()
 
     @pl.loop(0, CAP // 8)
@@ -145,13 +146,13 @@
         one_of(4, even_four),
         one_of(1, even),
         one_of(n - 1, even),
+        one_of(n - 5, even),
         n // 2,
-        one_of(n - 5, even),
         one_of(5, even),
     )
 
 
-def pick(first_ref, second_ref, outer_ref, next_ref, near_ref):
+def pick(first_ref, second_ref, next_ref, outer_ref, near_ref):
     outer_ref[...] = first_ref[...]
     me = lax.axis_index("row")
     straight = (me % 2 == 1) == ((me // 4) % 2 == 0)
@@ -202,8 +203,7 @@
 
     first = trade(basis, inner)
     second = trade(basis, outer)
-    beside, beyond = trade(held, near), trade(held, next_chip)
-    outer_sent, next_sent, near_sent = pl.pallas_call(
+    next_sent, outer_sent, near_sent = pl.pallas_call(
         pick,
         out_shape=(jax.ShapeDtypeStruct((ROWS, MODES), full),) * 3,
         in_specs=[vmem] * 2,
@@ -216,14 +216,15 @@
     far_next, far_near = trade(next_sent, next_chip), trade(near_sent, near)
 
     blocks = tangent_blocks.reshape(CAP // 8, 8, HALF, 128).transpose(0, 2, 1, 3).reshape(CAP * HALF, 128)
-    high, low = pl.pallas_call(
+    high, low, again = pl.pallas_call(
         assemble,
         out_shape=(
             jax.ShapeDtypeStruct((LINKS, ROWS, ROWS), half),
             jax.ShapeDtypeStruct((LINKS, ROWS, ROWS), half),
+            jax.ShapeDtypeStruct((ROWS, MODES), full),
         ),
-        in_specs=[smem] + [vmem] * 4,
-        out_specs=(vmem,) * 2,
+        in_specs=[smem] + [vmem] * 5,
+        out_specs=(vmem,) * 3,
         scratch_shapes=[
             pltpu.VMEM(((CAP + 1) * HALF, 128), full),
             pltpu.VMEM((1, CAP), jnp.int32),
@@ -233,7 +234,8 @@
         compiler_params=params,
         cost_estimate=pl.CostEstimate(flops=10_000_000, bytes_accessed=8_000_000, transcendentals=0),
         name="assemble",
-    )(tile_count, tile_rows, tile_owner[:, 0], tile_offset, blocks)
+    )(tile_count, tile_rows, tile_owner[:, 0], tile_offset, blocks, held)
+    beside, beyond = trade(again, near), trade(again, next_chip)
 
     total, early, weight_high, weight_low = pl.pallas_call(
         project_early,
@@ -249,7 +251,7 @@
         compiler_params=params,
         cost_estimate=pl.CostEstimate(flops=20_000_000_000, bytes_accessed=2_500_000, transcendentals=0),
         name="project_early",
-    )(high, low, springs.reshape(1, ROWS), held, first, second, beside, beyond)
+    )(high, low, springs.reshape(1, ROWS), again, first, second, beside, beyond)
 
     side = me
     for shift in (8, 4, 2, 1):
@@ -265,7 +267,7 @@
         compiler_params=params,
         cost_estimate=pl.CostEstimate(flops=80_000_000, bytes_accessed=700_000, transcendentals=0),
         name="reduce_late",
-    )(side, weight_high, weight_low, early, across, far_next, far_near)
+    )(side, weight_high, weight_low, early, far_next, across, far_near)
 
     stiff_image, done = pl.pallas_call(
         project_late,
@@ -275,7 +277,7 @@
         compiler_params=params,
         cost_estimate=pl.CostEstimate(flops=160_000_000, bytes_accessed=1_500_000, transcendentals=0),
         name="project_late",
-    )(high, low, total, across, far_next, far_near)
+    )(high, low, total, far_next, across, far_near)
 
     def swap(block, apart):
         return lax.ppermute(block, "row", [(d, d ^ apart) for d in range(n)])

time: 36.4 us -> 35.3 us (0.970)
  waiting for transfers between devices: 15.8 us -> 13 us
  starting transfers between devices: 12.2 us -> 13.9 us
    ppermute x5, waiting for transfers between devices: 12.3 us -> 8.69 us  [swap(): return lax.ppermute(block, 'row', [(d, d ^ apart) for d in range(n)])]
    ppermute x5, starting transfers between devices: 0.55 us -> 3.58 us  [swap(): return lax.ppermute(block, 'row', [(d, d ^ apart) for d in range(n)])]
    ppermute x7, starting transfers between devices: 11.6 us -> 10.3 us  [trade(): return lax.ppermute(block, 'row', [(d, partner(d) % n) for d in range(n)])]
    ppermute x7, waiting for transfers between devices: 3.49 us -> 4.31 us  [trade(): return lax.ppermute(block, 'row', [(d, partner(d) % n) for d in range(n)])]
  transfers between devices with their start and end apart: 12 -> 12, of which waited for: 7 -> 9; matrix products, arithmetic and copies ran while one was open for 0% -> 0% of each run, Pallas kernels for 14% -> 14%
where the time goes in v8:
time: 35.3 us; the launch traced here: 35.1 us
  starting transfers between devices  13.9 us (39%)
  waiting for transfers between devices  13 us (37%)
  Pallas kernels  5.8 us (16%)
  between operations  1.42 us (4%)
  local copies, waits for them, and re-layouts  0.99 us (3%)
    ppermute x7, starting transfers between devices, trade(): return lax.ppermute(block, 'row', [(d, partner(d) % n) for d in range(n)])  10.3 us
    ppermute x5, waiting for transfers between devices, swap(): return lax.ppermute(block, 'row', [(d, d ^ apart) for d in range(n)])  8.69 us
    ppermute x7, waiting for transfers between devices, trade(): return lax.ppermute(block, 'row', [(d, partner(d) % n) for d in range(n)])  4.31 us
    ppermute x5, starting transfers between devices, swap(): return lax.ppermute(block, 'row', [(d, d ^ apart) for d in range(n)])  3.58 us
    pallas_call x1, Pallas kernels, shards(): pl.pallas_call(assemble, out_shape=(jax.ShapeDtypeStruct((LINKS, ROWS, RO...  2.57 us
    pallas_call x1, Pallas kernels, shards(): pl.pallas_call(project_late, out_shape=(jax.ShapeDtypeStruct((ROWS, MODES...  1.12 us
    pallas_call x1, Pallas kernels, shards(): pl.pallas_call(project_early, out_shape=(jax.ShapeDtypeStruct((ROWS, MODE...  1.11 us
    unnamed x12, local copies, waits for them, and re-layouts  0.99 us
  transfers between devices with their start and end apart: 12, of which 9 were waited for; matrix products, arithmetic and copies ran while one was open for 0% of the time, Pallas kernels for 14%

profile of v8, /device:TPU:0, one launch (start us, length us, event | category | flops | bytes accessed | tf_op | source)
XLA Modules:
  0.0 35.1 jit_solution(15716447662165498745)
XLA Ops:
  0.7 5.1 %collective-permute-start = (f32[256,128]{1,0:T(8,128)}, f32[256,128]{1,0:T(8,128)S(1)}, u32[]{:S(2)}, u32[]{:S(2)}) collective-permute-start(f32[256,128]{1,0:T(8,128)} %basis_ref.1), channel_id=1, source_target_pairs={{0,12},{1,13},{2,14},{3,15},{4,8},{5,9},{6,10},{7,11},{8,4},{9,5},... | collective-permute-start | bytes 393224 | tf_op jit(solution)/shard_map/ppermute | solution.py:190
  5.8 0.0 collective-permute-start.1
  5.8 1.0 %copy-done.4 = f32[256,128]{1,0:T(8,128)S(1)} copy-done((f32[256,128]{1,0:T(8,128)S(1)}, f32[256,128]{1,0:T(8,128)}, u32[]{:S(2)}) %copy-start.4) | copy-done | bytes 131096
  6.8 0.0 copy-start.5
  7.5 2.6 %assemble.1 = (bf16[8,256,256]{2,1,0:T(8,128)(2,1)S(1)}, bf16[8,256,256]{2,1,0:T(8,128)(2,1)S(1)}, f32[256,128]{1,0:T(8,128)S(1)}) custom-call(s32[1]{0:T(128)S(6)} %copy.9.count_ref, s32[128]{0:T(128)S(1)} %copy-done.1, s32[128]{0:T(128)S(1)} %bitcast.9, s32[128]{0:T(128)S(1)} %copy-done.3, f32[4096,128]{1,0:T(8,128)S(1)} %bitcast.8, ...), custom_call_target="tpu_custom_call" | custom-call | flops 10000000 | bytes 8000000 | tf_op jit(solution)/shard_map/assemble/pallas_call | solution.py:219
  10.1 0.1 collective-permute-start.2
  10.1 2.0 %collective-permute-start.3 = (f32[256,128]{1,0:T(8,128)S(1)}, f32[256,128]{1,0:T(8,128)S(1)}, u32[]{:S(2)}, u32[]{:S(2)}) collective-permute-start(f32[256,128]{1,0:T(8,128)S(1)} %get-tuple-element.18.refs_0_), channel_id=1, source_target_pairs={{0,15},{1,2},{2,1},{3,4},{4,3},{5,6},{6,5},{7,8},{8,7},{9,10},{10,... | collective-permute-start | bytes 393224 | tf_op jit(solution)/shard_map/ppermute | solution.py:190
  12.1 0.0 collective-permute-done.refs_1_.first_ref
  12.1 0.3 collective-permute-done.1.refs_2_.second_ref
  12.4 2.3 %collective-permute-start.4 = (f32[256,128]{1,0:T(8,128)S(1)}, f32[256,128]{1,0:T(8,128)S(1)}, u32[]{:S(2)}, u32[]{:S(2)}) collective-permute-start(f32[256,128]{1,0:T(8,128)S(1)} %get-tuple-element.20), channel_id=1, source_target_pairs={{0,15},{1,2},{2,1},{3,4},{4,3},{5,6},{6,5},{7,8},{8,7},{9,10},{10,... | collective-permute-start | bytes 393224 | tf_op jit(solution)/shard_map/ppermute | solution.py:190
  14.8 0.2 collective-permute-start.5
  15.0 0.6 %collective-permute-start.6 = (f32[256,128]{1,0:T(8,128)S(1)}, f32[256,128]{1,0:T(8,128)S(1)}, u32[]{:S(2)}, u32[]{:S(2)}) collective-permute-start(f32[256,128]{1,0:T(8,128)S(1)} %get-tuple-element.22), channel_id=1, source_target_pairs={{0,1},{1,0},{2,3},{3,2},{4,5},{5,4},{6,7},{7,6},{8,9},{9,8},{10,11... | collective-permute-start | bytes 393224 | tf_op jit(solution)/shard_map/ppermute | solution.py:190
  15.6 0.0 collective-permute-done.2.refs_3_
  15.6 1.9 %collective-permute-done.3.refs_4_ = f32[256,128]{1,0:T(8,128)S(1)} collective-permute-done((f32[256,128]{1,0:T(8,128)S(1)}, f32[256,128]{1,0:T(8,128)S(1)}, u32[]{:S(2)}, u32[]{:S(2)}) %collective-permute-start.3) | collective-permute-done | bytes 131104 | tf_op jit(solution)/shard_map/ppermute | solution.py:190
  17.5 0.0 copy-done.5
  17.5 1.1 %project_early.1 = (f32[256,128]{1,0:T(8,128)S(1)}, f32[128,128]{1,0:T(8,128)S(1)}, bf16[3,128,256]{2,1,0:T(8,128)(2,1)S(1)}, bf16[3,128,256]{2,1,0:T(8,128)(2,1)S(1)}) custom-call(bf16[8,256,256]{2,1,0:T(8,128)(2,1)S(1)} %get-tuple-element.16.high_ref, bf16[8,256,256]{2,1,0:T(8,128)(2,1)S(1)} %get-tuple-element.17.low_ref, f32[1,256]{1,0:T(1,128)S(1)} %bitcast.10, ...), custom_call_target="tpu_custom_call" | custom-call | flops 20000000000 | bytes 2500000 | tf_op jit(solution)/shard_map/project_early/pallas_call | solution.py:240
  18.6 1.6 %collective-permute-done.4.refs_0_ = f32[256,128]{1,0:T(8,128)S(1)} collective-permute-done((f32[256,128]{1,0:T(8,128)S(1)}, f32[256,128]{1,0:T(8,128)S(1)}, u32[]{:S(2)}, u32[]{:S(2)}) %collective-permute-start.4) | collective-permute-done | bytes 131104 | tf_op jit(solution)/shard_map/ppermute | solution.py:190
  20.2 0.5 %collective-permute-done.5.refs_1_ = f32[256,128]{1,0:T(8,128)S(1)} collective-permute-done((f32[256,128]{1,0:T(8,128)S(1)}, f32[256,128]{1,0:T(8,128)S(1)}, u32[]{:S(2)}, u32[]{:S(2)}) %collective-permute-start.5) | collective-permute-done | bytes 131104 | tf_op jit(solution)/shard_map/ppermute | solution.py:190
  20.7 0.0 collective-permute-done.6.refs_2_
  20.7 0.3 reduce_late.1
  21.0 0.1 collective-permute-start.7
  21.1 1.2 %collective-permute-done.7 = f32[64,128]{1,0:T(8,128)S(1)} collective-permute-done((f32[64,128]{1,0:T(8,128)S(1)}, f32[64,128]{1,0:T(8,128)S(1)}, u32[]{:S(2)}, u32[]{:S(2)}) %collective-permute-start.7) | collective-permute-done | bytes 32800 | tf_op jit(solution)/shard_map/ppermute | solution.py:283
  22.3 0.8 %collective-permute-start.8 = (f32[64,128]{1,0:T(8,128)S(1)}, f32[64,128]{1,0:T(8,128)S(1)}, u32[]{:S(2)}, u32[]{:S(2)}) collective-permute-start(f32[64,128]{1,0:T(8,128)S(1)} %add.9.first_ref), channel_id=1, source_target_pairs={{0,3},{1,2},{2,1},{3,0},{4,7},{5,6},{6,5},{7,4},{8,11},{9,10},{10,... | collective-permute-start | bytes 98312 | tf_op jit(solution)/shard_map/ppermute | solution.py:283
  23.1 1.1 %project_late.1 = (f32[256,128]{1,0:T(8,128)}, f32[8,128]{1,0:T(8,128)S(1)}) custom-call(bf16[8,256,256]{2,1,0:T(8,128)(2,1)S(1)} %get-tuple-element.16.high_ref, bf16[8,256,256]{2,1,0:T(8,128)(2,1)S(1)} %get-tuple-element.17.low_ref, f32[256,128]{1,0:T(8,128)S(1)} %get-tuple-element.19.total_ref, f32[256,128]{1,0:T(8,128)S(1)} %collective-permute-done.4.refs_0_, ...), custom_call_target="tpu_custom_call" | custom-call | flops 160000000 | bytes 1500000 | tf_op jit(solution)/shard_map/project_late/pallas_call | solution.py:272
  24.3 1.4 %collective-permute-done.8.second_ref = f32[64,128]{1,0:T(8,128)S(1)} collective-permute-done((f32[64,128]{1,0:T(8,128)S(1)}, f32[64,128]{1,0:T(8,128)S(1)}, u32[]{:S(2)}, u32[]{:S(2)}) %collective-permute-start.8) | collective-permute-done | bytes 32800 | tf_op jit(solution)/shard_map/ppermute | solution.py:283
  25.7 1.6 %collective-permute-start.9 = (f32[64,128]{1,0:T(8,128)S(1)}, f32[64,128]{1,0:T(8,128)S(1)}, u32[]{:S(2)}, u32[]{:S(2)}) collective-permute-start(f32[64,128]{1,0:T(8,128)S(1)} %add_after.1), channel_id=1, source_target_pairs={{0,5},{1,4},{2,7},{3,6},{4,1},{5,0},{6,3},{7,2},{8,13},{9,12},{10,... | collective-permute-start | bytes 98312 | tf_op jit(solution)/shard_map/ppermute | solution.py:283
  27.3 1.7 %collective-permute-done.9 = f32[64,128]{1,0:T(8,128)S(1)} collective-permute-done((f32[64,128]{1,0:T(8,128)S(1)}, f32[64,128]{1,0:T(8,128)S(1)}, u32[]{:S(2)}, u32[]{:S(2)}) %collective-permute-start.9) | collective-permute-done | bytes 32800 | tf_op jit(solution)/shard_map/ppermute | solution.py:283
  29.0 0.9 %collective-permute-start.10 = (f32[64,128]{1,0:T(8,128)S(1)}, f32[64,128]{1,0:T(8,128)S(1)}, u32[]{:S(2)}, u32[]{:S(2)}) collective-permute-start(f32[64,128]{1,0:T(8,128)S(1)} %add.10), channel_id=1, source_target_pairs={{0,9},{1,8},{2,11},{3,10},{4,13},{5,12},{6,15},{7,14},{8,1},{9,0},... | collective-permute-start | bytes 98312 | tf_op jit(solution)/shard_map/ppermute | solution.py:283
  29.9 3.4 %collective-permute-done.10 = f32[64,128]{1,0:T(8,128)S(1)} collective-permute-done((f32[64,128]{1,0:T(8,128)S(1)}, f32[64,128]{1,0:T(8,128)S(1)}, u32[]{:S(2)}, u32[]{:S(2)}) %collective-permute-start.10) | collective-permute-done | bytes 32800 | tf_op jit(solution)/shard_map/ppermute | solution.py:283
  33.3 0.2 collective-permute-start.11
  33.5 1.0 %collective-permute-done.11.other_ref = f32[64,128]{1,0:T(8,128)S(1)} collective-permute-done((f32[64,128]{1,0:T(8,128)S(1)}, f32[64,128]{1,0:T(8,128)S(1)}, u32[]{:S(2)}, u32[]{:S(2)}) %collective-permute-start.11) | collective-permute-done | bytes 32800 | tf_op jit(solution)/shard_map/ppermute | solution.py:283
  34.5 0.6 %join.1 = f32[128,128]{1,0:T(8,128)} custom-call(s32[1]{0:T(128)} %bitcast.5.side_ref, f32[64,128]{1,0:T(8,128)S(1)} %add.11.mine_ref, f32[64,128]{1,0:T(8,128)S(1)} %collective-permute-done.11.other_ref), custom_call_target="tpu_custom_call" | custom-call | bytes 130000 | tf_op jit(solution)/shard_map/join/pallas_call | solution.py:298
  (15 shorter events, 0.1 us)
Async XLA Ops:
  0.6 6.8 %copy-start.1 = (s32[128]{0:T(128)S(1)}, s32[128]{0:T(128)}, u32[]{:S(2)}) copy-start(s32[128]{0:T(128)} %rows_ref.1) | copy-start | bytes 1540
  0.6 6.8 %copy-start.2 = (s32[128,1]{0,1:T(1,128)S(1)}, s32[128,1]{0,1:T(1,128)}, u32[]{:S(2)}) copy-start(s32[128,1]{0,1:T(1,128)} %param.11) | copy-start | bytes 1540
  0.7 6.8 %copy-start.3 = (s32[128]{0:T(128)S(1)}, s32[128]{0:T(128)}, u32[]{:S(2)}) copy-start(s32[128]{0:T(128)} %offset_ref.1) | copy-start | bytes 1540
  0.7 6.8 %copy-start = (f32[128,4096]{1,0:T(8,128)S(1)}, f32[128,4096]{1,0:T(8,128)}, u32[]{:S(2)}) copy-start(f32[128,4096]{1,0:T(8,128)} %param.9) | copy-start | bytes 6291460
  0.7 11.5 %collective-permute-start = (f32[256,128]{1,0:T(8,128)}, f32[256,128]{1,0:T(8,128)S(1)}, u32[]{:S(2)}, u32[]{:S(2)}) collective-permute-start(f32[256,128]{1,0:T(8,128)} %basis_ref.1), channel_id=1, source_target_pairs={{0,12},{1,13},{2,14},{3,15},{4,8},{5,9},{6,10},{7,11},{8,4},{9,5},... | collective-permute-start | bytes 393224 | tf_op jit(solution)/shard_map/ppermute | solution.py:190
  5.8 6.6 %collective-permute-start.1 = (f32[256,128]{1,0:T(8,128)}, f32[256,128]{1,0:T(8,128)S(1)}, u32[]{:S(2)}, u32[]{:S(2)}) collective-permute-start(f32[256,128]{1,0:T(8,128)} %basis_ref.1), channel_id=1, source_target_pairs={{0,4},{1,5},{2,6},{3,7},{4,0},{5,1},{6,2},{7,3},{8,12},{9,13},{10,... | collective-permute-start | bytes 393224 | tf_op jit(solution)/shard_map/ppermute | solution.py:190
  5.8 1.0 %copy-start.4 = (f32[256,128]{1,0:T(8,128)S(1)}, f32[256,128]{1,0:T(8,128)}, u32[]{:S(2)}) copy-start(f32[256,128]{1,0:T(8,128)} %basis_ref.1) | copy-start | bytes 393220
  6.8 10.7 %copy-start.5 = (f32[256]{0:T(256)S(1)}, f32[256]{0:T(256)}, u32[]{:S(2)}) copy-start(f32[256]{0:T(256)} %param.8) | copy-start | bytes 3076
  10.1 5.5 %collective-permute-start.2 = (f32[256,128]{1,0:T(8,128)S(1)}, f32[256,128]{1,0:T(8,128)S(1)}, u32[]{:S(2)}, u32[]{:S(2)}) collective-permute-start(f32[256,128]{1,0:T(8,128)S(1)} %get-tuple-element.18.refs_0_), channel_id=1, source_target_pairs={{0,1},{1,0},{2,3},{3,2},{4,5},{5,4},{6,7},{7,6},{8,9},{9,8},{10,11... | collective-permute-start | bytes 393224 | tf_op jit(solution)/shard_map/ppermute | solution.py:190
  10.1 7.4 %collective-permute-start.3 = (f32[256,128]{1,0:T(8,128)S(1)}, f32[256,128]{1,0:T(8,128)S(1)}, u32[]{:S(2)}, u32[]{:S(2)}) collective-permute-start(f32[256,128]{1,0:T(8,128)S(1)} %get-tuple-element.18.refs_0_), channel_id=1, source_target_pairs={{0,15},{1,2},{2,1},{3,4},{4,3},{5,6},{6,5},{7,8},{8,7},{9,10},{10,... | collective-permute-start | bytes 393224 | tf_op jit(solution)/shard_map/ppermute | solution.py:190
  12.4 7.8 %collective-permute-start.4 = (f32[256,128]{1,0:T(8,128)S(1)}, f32[256,128]{1,0:T(8,128)S(1)}, u32[]{:S(2)}, u32[]{:S(2)}) collective-permute-start(f32[256,128]{1,0:T(8,128)S(1)} %get-tuple-element.20), channel_id=1, source_target_pairs={{0,15},{1,2},{2,1},{3,4},{4,3},{5,6},{6,5},{7,8},{8,7},{9,10},{10,... | collective-permute-start | bytes 393224 | tf_op jit(solution)/shard_map/ppermute | solution.py:190
  14.8 5.9 %collective-permute-start.5 = (f32[256,128]{1,0:T(8,128)S(1)}, f32[256,128]{1,0:T(8,128)S(1)}, u32[]{:S(2)}, u32[]{:S(2)}) collective-permute-start(f32[256,128]{1,0:T(8,128)S(1)} %get-tuple-element.21), channel_id=1, source_target_pairs={{0,4},{1,5},{2,6},{3,7},{4,0},{5,1},{6,2},{7,3},{8,12},{9,13},{10,... | collective-permute-start | bytes 393224 | tf_op jit(solution)/shard_map/ppermute | solution.py:190
  15.0 5.8 %collective-permute-start.6 = (f32[256,128]{1,0:T(8,128)S(1)}, f32[256,128]{1,0:T(8,128)S(1)}, u32[]{:S(2)}, u32[]{:S(2)}) collective-permute-start(f32[256,128]{1,0:T(8,128)S(1)} %get-tuple-element.22), channel_id=1, source_target_pairs={{0,1},{1,0},{2,3},{3,2},{4,5},{5,4},{6,7},{7,6},{8,9},{9,8},{10,11... | collective-permute-start | bytes 393224 | tf_op jit(solution)/shard_map/ppermute | solution.py:190
  21.0 1.3 %collective-permute-start.7 = (f32[64,128]{1,0:T(8,128)S(1)}, f32[64,128]{1,0:T(8,128)S(1)}, u32[]{:S(2)}, u32[]{:S(2)}) collective-permute-start(f32[64,128]{1,0:T(8,128)S(1)} %get-tuple-element.28), channel_id=1, source_target_pairs={{0,1},{1,0},{2,3},{3,2},{4,5},{5,4},{6,7},{7,6},{8,9},{9,8},{10,11... | collective-permute-start | bytes 98312 | tf_op jit(solution)/shard_map/ppermute | solution.py:283
  22.3 3.3 %collective-permute-start.8 = (f32[64,128]{1,0:T(8,128)S(1)}, f32[64,128]{1,0:T(8,128)S(1)}, u32[]{:S(2)}, u32[]{:S(2)}) collective-permute-start(f32[64,128]{1,0:T(8,128)S(1)} %add.9.first_ref), channel_id=1, source_target_pairs={{0,3},{1,2},{2,1},{3,0},{4,7},{5,6},{6,5},{7,4},{8,11},{9,10},{10,... | collective-permute-start | bytes 98312 | tf_op jit(solution)/shard_map/ppermute | solution.py:283
  25.7 3.3 %collective-permute-start.9 = (f32[64,128]{1,0:T(8,128)S(1)}, f32[64,128]{1,0:T(8,128)S(1)}, u32[]{:S(2)}, u32[]{:S(2)}) collective-permute-start(f32[64,128]{1,0:T(8,128)S(1)} %add_after.1), channel_id=1, source_target_pairs={{0,5},{1,4},{2,7},{3,6},{4,1},{5,0},{6,3},{7,2},{8,13},{9,12},{10,... | collective-permute-start | bytes 98312 | tf_op jit(solution)/shard_map/ppermute | solution.py:283
  29.0 4.2 %collective-permute-start.10 = (f32[64,128]{1,0:T(8,128)S(1)}, f32[64,128]{1,0:T(8,128)S(1)}, u32[]{:S(2)}, u32[]{:S(2)}) collective-permute-start(f32[64,128]{1,0:T(8,128)S(1)} %add.10), channel_id=1, source_target_pairs={{0,9},{1,8},{2,11},{3,10},{4,13},{5,12},{6,15},{7,14},{8,1},{9,0},... | collective-permute-start | bytes 98312 | tf_op jit(solution)/shard_map/ppermute | solution.py:283
  33.3 1.2 %collective-permute-start.11 = (f32[64,128]{1,0:T(8,128)S(1)}, f32[64,128]{1,0:T(8,128)S(1)}, u32[]{:S(2)}, u32[]{:S(2)}) collective-permute-start(f32[64,128]{1,0:T(8,128)S(1)} %add.11.mine_ref), channel_id=1, source_target_pairs={{0,1},{1,0},{2,3},{3,2},{4,5},{5,4},{6,7},{7,6},{8,9},{9,8},{10,11... | collective-permute-start | bytes 98312 | tf_op jit(solution)/shard_map/ppermute | solution.py:283

commit v9 on v6

--- a/solution.py
+++ b/solution.py
@@ -33,11 +33,11 @@
             yield pl.ds(r * B + h, HALF, stride=2), slice(r * B + h * HALF, r * B + (h + 1) * HALF)
 
 
-def prepare(basis_ref, held_ref):
-    held_ref[...] = basis_ref[...]
-
-
-def assemble(count_ref, rows_ref, owner_ref, offset_ref, blocks_ref, high_ref, low_ref, dense, placed, place, arrived):
+def prepare(token_ref):
+    token_ref[...] = jnp.zeros_like(token_ref)
+
+
+def assemble(count_ref, rows_ref, owner_ref, offset_ref, blocks_ref, basis_ref, token_ref, high_ref, low_ref, held_ref, dense, placed, place, arrived):
     n, me = lax.axis_size("row"), lax.axis_index("row")
     away = lax.rem(owner_ref[...].reshape(1, CAP) - me + n, n)
     link = jnp.zeros_like(away)
@@ -49,6 +49,7 @@
     copy = pltpu.make_async_copy(placed, place, arrived)
     copy.start()
     dense[...] = jnp.zeros_like(dense)
+    held_ref[...] = basis_ref[...]
     copy.wait()
 
     @pl.loop(0, CAP // 8)
@@ -151,7 +152,8 @@
     )
 
 
-def pick(first_ref, second_ref, near_ref, next_ref):
+def pick(first_ref, second_ref, next_ref, outer_ref, near_ref):
+    outer_ref[...] = first_ref[...]
     me = lax.axis_index("row")
     straight = (me % 2 == 1) == ((me // 4) % 2 == 0)
 
@@ -174,15 +176,15 @@
     half, full = jnp.bfloat16, jnp.float32
     params = pltpu.CompilerParams(vmem_limit_bytes=32 * 2**20)
 
-    held = pl.pallas_call(
+    token = pl.pallas_call(
         prepare,
-        out_shape=jax.ShapeDtypeStruct((ROWS, MODES), full),
-        in_specs=[vmem],
+        out_shape=jax.ShapeDtypeStruct((8, 128), full),
+        in_specs=[],
         out_specs=vmem,
         compiler_params=params,
-        cost_estimate=pl.CostEstimate(flops=10_000_000_000, bytes_accessed=300_000, transcendentals=0),
+        cost_estimate=pl.CostEstimate(flops=10_000_000_000, bytes_accessed=4_096, transcendentals=0),
         name="prepare",
-    )(basis)
+    )()
 
     def trade(block, partner):
         return lax.ppermute(block, "row", [(d, partner(d) % n) for d in range(n)])
@@ -201,28 +203,16 @@
 
     first = trade(basis, inner)
     second = trade(basis, outer)
-    across = trade(first, outer) if n == 16 else trade(held, lambda d: d + n // 2)
-    beside, beyond = trade(held, near), trade(held, next_chip)
-    near_sent, next_sent = pl.pallas_call(
-        pick,
-        out_shape=(jax.ShapeDtypeStruct((ROWS, MODES), full),) * 2,
-        in_specs=[vmem] * 2,
-        out_specs=(vmem,) * 2,
-        compiler_params=params,
-        cost_estimate=pl.CostEstimate(flops=0, bytes_accessed=500_000, transcendentals=0),
-        name="pick",
-    )(first, second)
-    far_next, far_near = trade(next_sent, next_chip), trade(near_sent, near)
-
     blocks = tangent_blocks.reshape(CAP // 8, 8, HALF, 128).transpose(0, 2, 1, 3).reshape(CAP * HALF, 128)
-    high, low = pl.pallas_call(
+    high, low, held = pl.pallas_call(
         assemble,
         out_shape=(
             jax.ShapeDtypeStruct((LINKS, ROWS, ROWS), half),
             jax.ShapeDtypeStruct((LINKS, ROWS, ROWS), half),
+            jax.ShapeDtypeStruct((ROWS, MODES), full),
         ),
-        in_specs=[smem] + [vmem] * 4,
-        out_specs=(vmem,) * 2,
+        in_specs=[smem] + [vmem] * 6,
+        out_specs=(vmem,) * 3,
         scratch_shapes=[
             pltpu.VMEM(((CAP + 1) * HALF, 128), full),
             pltpu.VMEM((1, CAP), jnp.int32),
@@ -232,7 +222,20 @@
         compiler_params=params,
         cost_estimate=pl.CostEstimate(flops=10_000_000, bytes_accessed=8_000_000, transcendentals=0),
         name="assemble",
-    )(tile_count, tile_rows, tile_owner[:, 0], tile_offset, blocks)
+    )(tile_count, tile_rows, tile_owner[:, 0], tile_offset, blocks, basis, token)
+    beside, beyond = trade(held, near), trade(held, next_chip)
+
+    next_sent, outer_sent, near_sent = pl.pallas_call(
+        pick,
+        out_shape=(jax.ShapeDtypeStruct((ROWS, MODES), full),) * 3,
+        in_specs=[vmem] * 2,
+        out_specs=(vmem,) * 3,
+        compiler_params=params,
+        cost_estimate=pl.CostEstimate(flops=0, bytes_accessed=700_000, transcendentals=0),
+        name="pick",
+    )(first, second)
+    across = trade(outer_sent, outer) if n == 16 else trade(held, lambda d: d + n // 2)
+    far_next, far_near = trade(next_sent, next_chip), trade(near_sent, near)
 
     total, early, weight_high, weight_low = pl.pallas_call(
         project_early,

time: 35.3 us -> 35.5 us (level)
  waiting for transfers between devices: 10.4 us -> 15.1 us
  starting transfers between devices: 16.6 us -> 13 us
  local copies, waits for them, and re-layouts: 0.99 us -> 0.02 us
    ppermute x5, waiting for transfers between devices: 7.27 us -> 10.1 us  [swap(): return lax.ppermute(block, 'row', [(d, d ^ apart) for d in range(n)])]
    ppermute x5, starting transfers between devices: 4.99 us -> 2.73 us  [swap(): return lax.ppermute(block, 'row', [(d, d ^ apart) for d in range(n)])]
    ppermute x7, waiting for transfers between devices: 3.15 us -> 5.04 us  [trade(): return lax.ppermute(block, 'row', [(d, partner(d) % n) for d in range(n)])]
    ppermute x7, starting transfers between devices: 11.6 us -> 10.3 us  [trade(): return lax.ppermute(block, 'row', [(d, partner(d) % n) for d in range(n)])]
    unnamed x12, local copies, waits for them, and re-layouts: 0.99 us -> 0.02 us
  transfers between devices with their start and end apart: 12 -> 12, of which waited for: 8 -> 9; matrix products, arithmetic and copies ran while one was open for 0% -> 0% of each run, Pallas kernels for 13% -> 14%
where the time goes in v9:
time: 35.5 us; the launch traced here: 35.4 us
  waiting for transfers between devices  15.1 us (43%)
  starting transfers between devices  13 us (37%)
  Pallas kernels  5.78 us (16%)
  between operations  1.44 us (4%)
    ppermute x7, starting transfers between devices, trade(): return lax.ppermute(block, 'row', [(d, partner(d) % n) for d in range(n)])  10.3 us
    ppermute x5, waiting for transfers between devices, swap(): return lax.ppermute(block, 'row', [(d, d ^ apart) for d in range(n)])  10.1 us
    ppermute x7, waiting for transfers between devices, trade(): return lax.ppermute(block, 'row', [(d, partner(d) % n) for d in range(n)])  5.04 us
    ppermute x5, starting transfers between devices, swap(): return lax.ppermute(block, 'row', [(d, d ^ apart) for d in range(n)])  2.73 us
    pallas_call x1, Pallas kernels, shards(): pl.pallas_call(assemble, out_shape=(jax.ShapeDtypeStruct((LINKS, ROWS, RO...  2.55 us
    pallas_call x1, Pallas kernels, shards(): pl.pallas_call(project_late, out_shape=(jax.ShapeDtypeStruct((ROWS, MODES...  1.12 us
    pallas_call x1, Pallas kernels, shards(): pl.pallas_call(project_early, out_shape=(jax.ShapeDtypeStruct((ROWS, MODE...  1.11 us
  transfers between devices with their start and end apart: 12, of which 9 were waited for; matrix products, arithmetic and copies ran while one was open for 0% of the time, Pallas kernels for 14%

profile of v9, /device:TPU:0, one launch (start us, length us, event | category | flops | bytes accessed | tf_op | source)
XLA Modules:
  0.0 35.4 jit_solution(359422605480480409)
XLA Ops:
  0.7 5.1 %collective-permute-start = (f32[256,128]{1,0:T(8,128)}, f32[256,128]{1,0:T(8,128)S(1)}, u32[]{:S(2)}, u32[]{:S(2)}) collective-permute-start(f32[256,128]{1,0:T(8,128)} %basis_ref.1), channel_id=1, source_target_pairs={{0,12},{1,13},{2,14},{3,15},{4,8},{5,9},{6,10},{7,11},{8,4},{9,5},... | collective-permute-start | bytes 393224 | tf_op jit(solution)/shard_map/ppermute | solution.py:190
  5.8 0.0 collective-permute-start.1
  6.5 0.0 copy-done.1
  6.5 0.0 copy-done.2
  6.5 0.0 copy-done.3
  6.5 2.6 %assemble.1 = (bf16[8,256,256]{2,1,0:T(8,128)(2,1)S(1)}, bf16[8,256,256]{2,1,0:T(8,128)(2,1)S(1)}, f32[256,128]{1,0:T(8,128)S(1)}) custom-call(s32[1]{0:T(128)S(6)} %copy.9.count_ref, s32[128]{0:T(128)S(1)} %copy-done.2, s32[128]{0:T(128)S(1)} %bitcast.9, s32[128]{0:T(128)S(1)} %copy-done.4, f32[4096,128]{1,0:T(8,128)S(1)} %bitcast.8, ...), custom_call_target="tpu_custom_call" | custom-call | flops 10000000 | bytes 8000000 | tf_op jit(solution)/shard_map/assemble/pallas_call | solution.py:207
  9.1 0.1 collective-permute-start.2
  9.2 2.0 %collective-permute-start.3 = (f32[256,128]{1,0:T(8,128)S(1)}, f32[256,128]{1,0:T(8,128)S(1)}, u32[]{:S(2)}, u32[]{:S(2)}) collective-permute-start(f32[256,128]{1,0:T(8,128)S(1)} %get-tuple-element.18.refs_0_), channel_id=1, source_target_pairs={{0,15},{1,2},{2,1},{3,4},{4,3},{5,6},{6,5},{7,8},{8,7},{9,10},{10,... | collective-permute-start | bytes 393224 | tf_op jit(solution)/shard_map/ppermute | solution.py:190
  11.1 0.0 collective-permute-done.refs_1_.first_ref
  11.1 1.3 %collective-permute-done.1.refs_2_.second_ref = f32[256,128]{1,0:T(8,128)S(1)} collective-permute-done((f32[256,128]{1,0:T(8,128)}, f32[256,128]{1,0:T(8,128)S(1)}, u32[]{:S(2)}, u32[]{:S(2)}) %collective-permute-start.1) | collective-permute-done | bytes 131104 | tf_op jit(solution)/shard_map/ppermute | solution.py:190
  12.5 1.3 %collective-permute-start.4 = (f32[256,128]{1,0:T(8,128)S(1)}, f32[256,128]{1,0:T(8,128)S(1)}, u32[]{:S(2)}, u32[]{:S(2)}) collective-permute-start(f32[256,128]{1,0:T(8,128)S(1)} %get-tuple-element.20), channel_id=1, source_target_pairs={{0,15},{1,2},{2,1},{3,4},{4,3},{5,6},{6,5},{7,8},{8,7},{9,10},{10,... | collective-permute-start | bytes 393224 | tf_op jit(solution)/shard_map/ppermute | solution.py:190
  13.8 0.9 %collective-permute-start.5 = (f32[256,128]{1,0:T(8,128)S(1)}, f32[256,128]{1,0:T(8,128)S(1)}, u32[]{:S(2)}, u32[]{:S(2)}) collective-permute-start(f32[256,128]{1,0:T(8,128)S(1)} %get-tuple-element.21), channel_id=1, source_target_pairs={{0,4},{1,5},{2,6},{3,7},{4,0},{5,1},{6,2},{7,3},{8,12},{9,13},{10,... | collective-permute-start | bytes 393224 | tf_op jit(solution)/shard_map/ppermute | solution.py:190
  14.7 0.9 %collective-permute-start.6 = (f32[256,128]{1,0:T(8,128)S(1)}, f32[256,128]{1,0:T(8,128)S(1)}, u32[]{:S(2)}, u32[]{:S(2)}) collective-permute-start(f32[256,128]{1,0:T(8,128)S(1)} %get-tuple-element.22), channel_id=1, source_target_pairs={{0,1},{1,0},{2,3},{3,2},{4,5},{5,4},{6,7},{7,6},{8,9},{9,8},{10,11... | collective-permute-start | bytes 393224 | tf_op jit(solution)/shard_map/ppermute | solution.py:190
  15.6 0.0 collective-permute-done.2.refs_3_
  15.6 0.8 %collective-permute-done.3.refs_4_ = f32[256,128]{1,0:T(8,128)S(1)} collective-permute-done((f32[256,128]{1,0:T(8,128)S(1)}, f32[256,128]{1,0:T(8,128)S(1)}, u32[]{:S(2)}, u32[]{:S(2)}) %collective-permute-start.3) | collective-permute-done | bytes 131104 | tf_op jit(solution)/shard_map/ppermute | solution.py:190
  16.4 1.1 %project_early.1 = (f32[256,128]{1,0:T(8,128)S(1)}, f32[128,128]{1,0:T(8,128)S(1)}, bf16[3,128,256]{2,1,0:T(8,128)(2,1)S(1)}, bf16[3,128,256]{2,1,0:T(8,128)(2,1)S(1)}) custom-call(bf16[8,256,256]{2,1,0:T(8,128)(2,1)S(1)} %get-tuple-element.16.high_ref, bf16[8,256,256]{2,1,0:T(8,128)(2,1)S(1)} %get-tuple-element.17.low_ref, f32[1,256]{1,0:T(1,128)S(1)} %bitcast.10, ...), custom_call_target="tpu_custom_call" | custom-call | flops 20000000000 | bytes 2500000 | tf_op jit(solution)/shard_map/project_early/pallas_call | solution.py:240
  17.5 2.6 %collective-permute-done.4.refs_0_ = f32[256,128]{1,0:T(8,128)S(1)} collective-permute-done((f32[256,128]{1,0:T(8,128)S(1)}, f32[256,128]{1,0:T(8,128)S(1)}, u32[]{:S(2)}, u32[]{:S(2)}) %collective-permute-start.4) | collective-permute-done | bytes 131104 | tf_op jit(solution)/shard_map/ppermute | solution.py:190
  20.1 0.4 %collective-permute-done.5.refs_1_ = f32[256,128]{1,0:T(8,128)S(1)} collective-permute-done((f32[256,128]{1,0:T(8,128)S(1)}, f32[256,128]{1,0:T(8,128)S(1)}, u32[]{:S(2)}, u32[]{:S(2)}) %collective-permute-start.5) | collective-permute-done | bytes 131104 | tf_op jit(solution)/shard_map/ppermute | solution.py:190
  20.4 0.0 collective-permute-done.6.refs_2_
  20.5 0.3 reduce_late.1
  20.8 0.1 collective-permute-start.7
  20.9 1.2 %collective-permute-done.7 = f32[64,128]{1,0:T(8,128)S(1)} collective-permute-done((f32[64,128]{1,0:T(8,128)S(1)}, f32[64,128]{1,0:T(8,128)S(1)}, u32[]{:S(2)}, u32[]{:S(2)}) %collective-permute-start.7) | collective-permute-done | bytes 32800 | tf_op jit(solution)/shard_map/ppermute | solution.py:283
  22.1 0.9 %collective-permute-start.8 = (f32[64,128]{1,0:T(8,128)S(1)}, f32[64,128]{1,0:T(8,128)S(1)}, u32[]{:S(2)}, u32[]{:S(2)}) collective-permute-start(f32[64,128]{1,0:T(8,128)S(1)} %add.9.first_ref), channel_id=1, source_target_pairs={{0,3},{1,2},{2,1},{3,0},{4,7},{5,6},{6,5},{7,4},{8,11},{9,10},{10,... | collective-permute-start | bytes 98312 | tf_op jit(solution)/shard_map/ppermute | solution.py:283
  22.9 1.1 %project_late.1 = (f32[256,128]{1,0:T(8,128)}, f32[8,128]{1,0:T(8,128)S(1)}) custom-call(bf16[8,256,256]{2,1,0:T(8,128)(2,1)S(1)} %get-tuple-element.16.high_ref, bf16[8,256,256]{2,1,0:T(8,128)(2,1)S(1)} %get-tuple-element.17.low_ref, f32[256,128]{1,0:T(8,128)S(1)} %get-tuple-element.19.total_ref, f32[256,128]{1,0:T(8,128)S(1)} %collective-permute-done.4.refs_0_, ...), custom_call_target="tpu_custom_call" | custom-call | flops 160000000 | bytes 1500000 | tf_op jit(solution)/shard_map/project_late/pallas_call | solution.py:272
  24.1 1.3 %collective-permute-done.8.second_ref = f32[64,128]{1,0:T(8,128)S(1)} collective-permute-done((f32[64,128]{1,0:T(8,128)S(1)}, f32[64,128]{1,0:T(8,128)S(1)}, u32[]{:S(2)}, u32[]{:S(2)}) %collective-permute-start.8) | collective-permute-done | bytes 32800 | tf_op jit(solution)/shard_map/ppermute | solution.py:283
  25.4 0.9 %collective-permute-start.9 = (f32[64,128]{1,0:T(8,128)S(1)}, f32[64,128]{1,0:T(8,128)S(1)}, u32[]{:S(2)}, u32[]{:S(2)}) collective-permute-start(f32[64,128]{1,0:T(8,128)S(1)} %add_after.1), channel_id=1, source_target_pairs={{0,5},{1,4},{2,7},{3,6},{4,1},{5,0},{6,3},{7,2},{8,13},{9,12},{10,... | collective-permute-start | bytes 98312 | tf_op jit(solution)/shard_map/ppermute | solution.py:283
  26.3 2.5 %collective-permute-done.9 = f32[64,128]{1,0:T(8,128)S(1)} collective-permute-done((f32[64,128]{1,0:T(8,128)S(1)}, f32[64,128]{1,0:T(8,128)S(1)}, u32[]{:S(2)}, u32[]{:S(2)}) %collective-permute-start.9) | collective-permute-done | bytes 32800 | tf_op jit(solution)/shard_map/ppermute | solution.py:283
  28.8 0.0 collective-permute-start.10
  28.8 4.2 %collective-permute-done.10 = f32[64,128]{1,0:T(8,128)S(1)} collective-permute-done((f32[64,128]{1,0:T(8,128)S(1)}, f32[64,128]{1,0:T(8,128)S(1)}, u32[]{:S(2)}, u32[]{:S(2)}) %collective-permute-start.10) | collective-permute-done | bytes 32800 | tf_op jit(solution)/shard_map/ppermute | solution.py:283
  33.0 0.9 %collective-permute-start.11 = (f32[64,128]{1,0:T(8,128)S(1)}, f32[64,128]{1,0:T(8,128)S(1)}, u32[]{:S(2)}, u32[]{:S(2)}) collective-permute-start(f32[64,128]{1,0:T(8,128)S(1)} %add.11.mine_ref), channel_id=1, source_target_pairs={{0,1},{1,0},{2,3},{3,2},{4,5},{5,4},{6,7},{7,6},{8,9},{9,8},{10,11... | collective-permute-start | bytes 98312 | tf_op jit(solution)/shard_map/ppermute | solution.py:283
  33.9 0.9 %collective-permute-done.11.other_ref = f32[64,128]{1,0:T(8,128)S(1)} collective-permute-done((f32[64,128]{1,0:T(8,128)S(1)}, f32[64,128]{1,0:T(8,128)S(1)}, u32[]{:S(2)}, u32[]{:S(2)}) %collective-permute-start.11) | collective-permute-done | bytes 32800 | tf_op jit(solution)/shard_map/ppermute | solution.py:283
  34.7 0.6 %join.1 = f32[128,128]{1,0:T(8,128)} custom-call(s32[1]{0:T(128)} %bitcast.5.side_ref, f32[64,128]{1,0:T(8,128)S(1)} %add.11.mine_ref, f32[64,128]{1,0:T(8,128)S(1)} %collective-permute-done.11.other_ref), custom_call_target="tpu_custom_call" | custom-call | bytes 130000 | tf_op jit(solution)/shard_map/join/pallas_call | solution.py:298
  (15 shorter events, 0.1 us)
Async XLA Ops:
  0.6 5.8 %copy-start.1 = (f32[256,128]{1,0:T(8,128)S(1)}, f32[256,128]{1,0:T(8,128)}, u32[]{:S(2)}) copy-start(f32[256,128]{1,0:T(8,128)} %basis_ref.1) | copy-start | bytes 393220
  0.6 5.8 %copy-start.2 = (s32[128]{0:T(128)S(1)}, s32[128]{0:T(128)}, u32[]{:S(2)}) copy-start(s32[128]{0:T(128)} %rows_ref.1) | copy-start | bytes 1540
  0.7 5.8 %copy-start.3 = (s32[128,1]{0,1:T(1,128)S(1)}, s32[128,1]{0,1:T(1,128)}, u32[]{:S(2)}) copy-start(s32[128,1]{0,1:T(1,128)} %param.11) | copy-start | bytes 1540
  0.7 5.8 %copy-start.4 = (s32[128]{0:T(128)S(1)}, s32[128]{0:T(128)}, u32[]{:S(2)}) copy-start(s32[128]{0:T(128)} %offset_ref.1) | copy-start | bytes 1540
  0.7 5.8 %copy-start = (f32[128,4096]{1,0:T(8,128)S(1)}, f32[128,4096]{1,0:T(8,128)}, u32[]{:S(2)}) copy-start(f32[128,4096]{1,0:T(8,128)} %param.9) | copy-start | bytes 6291460
  0.7 10.5 %collective-permute-start = (f32[256,128]{1,0:T(8,128)}, f32[256,128]{1,0:T(8,128)S(1)}, u32[]{:S(2)}, u32[]{:S(2)}) collective-permute-start(f32[256,128]{1,0:T(8,128)} %basis_ref.1), channel_id=1, source_target_pairs={{0,12},{1,13},{2,14},{3,15},{4,8},{5,9},{6,10},{7,11},{8,4},{9,5},... | collective-permute-start | bytes 393224 | tf_op jit(solution)/shard_map/ppermute | solution.py:190
  5.8 6.6 %collective-permute-start.1 = (f32[256,128]{1,0:T(8,128)}, f32[256,128]{1,0:T(8,128)S(1)}, u32[]{:S(2)}, u32[]{:S(2)}) collective-permute-start(f32[256,128]{1,0:T(8,128)} %basis_ref.1), channel_id=1, source_target_pairs={{0,4},{1,5},{2,6},{3,7},{4,0},{5,1},{6,2},{7,3},{8,12},{9,13},{10,... | collective-permute-start | bytes 393224 | tf_op jit(solution)/shard_map/ppermute | solution.py:190
  5.8 10.6 %copy-start.5 = (f32[256]{0:T(256)S(1)}, f32[256]{0:T(256)}, u32[]{:S(2)}) copy-start(f32[256]{0:T(256)} %param.8) | copy-start | bytes 3076
  9.1 6.5 %collective-permute-start.2 = (f32[256,128]{1,0:T(8,128)S(1)}, f32[256,128]{1,0:T(8,128)S(1)}, u32[]{:S(2)}, u32[]{:S(2)}) collective-permute-start(f32[256,128]{1,0:T(8,128)S(1)} %get-tuple-element.18.refs_0_), channel_id=1, source_target_pairs={{0,1},{1,0},{2,3},{3,2},{4,5},{5,4},{6,7},{7,6},{8,9},{9,8},{10,11... | collective-permute-start | bytes 393224 | tf_op jit(solution)/shard_map/ppermute | solution.py:190
  9.2 7.2 %collective-permute-start.3 = (f32[256,128]{1,0:T(8,128)S(1)}, f32[256,128]{1,0:T(8,128)S(1)}, u32[]{:S(2)}, u32[]{:S(2)}) collective-permute-start(f32[256,128]{1,0:T(8,128)S(1)} %get-tuple-element.18.refs_0_), channel_id=1, source_target_pairs={{0,15},{1,2},{2,1},{3,4},{4,3},{5,6},{6,5},{7,8},{8,7},{9,10},{10,... | collective-permute-start | bytes 393224 | tf_op jit(solution)/shard_map/ppermute | solution.py:190
  12.5 7.6 %collective-permute-start.4 = (f32[256,128]{1,0:T(8,128)S(1)}, f32[256,128]{1,0:T(8,128)S(1)}, u32[]{:S(2)}, u32[]{:S(2)}) collective-permute-start(f32[256,128]{1,0:T(8,128)S(1)} %get-tuple-element.20), channel_id=1, source_target_pairs={{0,15},{1,2},{2,1},{3,4},{4,3},{5,6},{6,5},{7,8},{8,7},{9,10},{10,... | collective-permute-start | bytes 393224 | tf_op jit(solution)/shard_map/ppermute | solution.py:190
  13.8 6.7 %collective-permute-start.5 = (f32[256,128]{1,0:T(8,128)S(1)}, f32[256,128]{1,0:T(8,128)S(1)}, u32[]{:S(2)}, u32[]{:S(2)}) collective-permute-start(f32[256,128]{1,0:T(8,128)S(1)} %get-tuple-element.21), channel_id=1, source_target_pairs={{0,4},{1,5},{2,6},{3,7},{4,0},{5,1},{6,2},{7,3},{8,12},{9,13},{10,... | collective-permute-start | bytes 393224 | tf_op jit(solution)/shard_map/ppermute | solution.py:190
  14.7 5.8 %collective-permute-start.6 = (f32[256,128]{1,0:T(8,128)S(1)}, f32[256,128]{1,0:T(8,128)S(1)}, u32[]{:S(2)}, u32[]{:S(2)}) collective-permute-start(f32[256,128]{1,0:T(8,128)S(1)} %get-tuple-element.22), channel_id=1, source_target_pairs={{0,1},{1,0},{2,3},{3,2},{4,5},{5,4},{6,7},{7,6},{8,9},{9,8},{10,11... | collective-permute-start | bytes 393224 | tf_op jit(solution)/shard_map/ppermute | solution.py:190
  20.8 1.3 %collective-permute-start.7 = (f32[64,128]{1,0:T(8,128)S(1)}, f32[64,128]{1,0:T(8,128)S(1)}, u32[]{:S(2)}, u32[]{:S(2)}) collective-permute-start(f32[64,128]{1,0:T(8,128)S(1)} %get-tuple-element.28), channel_id=1, source_target_pairs={{0,1},{1,0},{2,3},{3,2},{4,5},{5,4},{6,7},{7,6},{8,9},{9,8},{10,11... | collective-permute-start | bytes 98312 | tf_op jit(solution)/shard_map/ppermute | solution.py:283
  22.1 3.3 %collective-permute-start.8 = (f32[64,128]{1,0:T(8,128)S(1)}, f32[64,128]{1,0:T(8,128)S(1)}, u32[]{:S(2)}, u32[]{:S(2)}) collective-permute-start(f32[64,128]{1,0:T(8,128)S(1)} %add.9.first_ref), channel_id=1, source_target_pairs={{0,3},{1,2},{2,1},{3,0},{4,7},{5,6},{6,5},{7,4},{8,11},{9,10},{10,... | collective-permute-start | bytes 98312 | tf_op jit(solution)/shard_map/ppermute | solution.py:283
  25.4 3.3 %collective-permute-start.9 = (f32[64,128]{1,0:T(8,128)S(1)}, f32[64,128]{1,0:T(8,128)S(1)}, u32[]{:S(2)}, u32[]{:S(2)}) collective-permute-start(f32[64,128]{1,0:T(8,128)S(1)} %add_after.1), channel_id=1, source_target_pairs={{0,5},{1,4},{2,7},{3,6},{4,1},{5,0},{6,3},{7,2},{8,13},{9,12},{10,... | collective-permute-start | bytes 98312 | tf_op jit(solution)/shard_map/ppermute | solution.py:283
  28.8 4.2 %collective-permute-start.10 = (f32[64,128]{1,0:T(8,128)S(1)}, f32[64,128]{1,0:T(8,128)S(1)}, u32[]{:S(2)}, u32[]{:S(2)}) collective-permute-start(f32[64,128]{1,0:T(8,128)S(1)} %add.10), channel_id=1, source_target_pairs={{0,9},{1,8},{2,11},{3,10},{4,13},{5,12},{6,15},{7,14},{8,1},{9,0},... | collective-permute-start | bytes 98312 | tf_op jit(solution)/shard_map/ppermute | solution.py:283
  33.0 1.7 %collective-permute-start.11 = (f32[64,128]{1,0:T(8,128)S(1)}, f32[64,128]{1,0:T(8,128)S(1)}, u32[]{:S(2)}, u32[]{:S(2)}) collective-permute-start(f32[64,128]{1,0:T(8,128)S(1)} %add.11.mine_ref), channel_id=1, source_target_pairs={{0,1},{1,0},{2,3},{3,2},{4,5},{5,4},{6,7},{7,6},{8,9},{9,8},{10,11... | collective-permute-start | bytes 98312 | tf_op jit(solution)/shard_map/ppermute | solution.py:283

commit v10 on v9

--- a/solution.py
+++ b/solution.py
@@ -152,20 +152,15 @@
     )
 
 
-def pick(first_ref, second_ref, next_ref, outer_ref, near_ref):
+def pick(short, first_ref, second_ref, next_ref, outer_ref, near_ref):
     outer_ref[...] = first_ref[...]
     me = lax.axis_index("row")
     straight = (me % 2 == 1) == ((me // 4) % 2 == 0)
 
-    @pl.when(straight)
-    def _():
-        near_ref[...] = second_ref[...]
-        next_ref[...] = first_ref[...]
-
-    @pl.when(jnp.logical_not(straight))
-    def _():
-        near_ref[...] = first_ref[...]
-        next_ref[...] = second_ref[...]
+    near_ref[...] = jnp.where(straight, second_ref[...], first_ref[...])
+    if short:
+        straight = jnp.logical_or(straight, jnp.logical_or(me % 4 == 0, me % 4 == 3))
+    next_ref[...] = jnp.where(straight, first_ref[...], second_ref[...])
 
 
 def shards(basis, springs, tangent_blocks, tile_rows, tile_owner, tile_offset, tile_count):
@@ -226,7 +221,7 @@
     beside, beyond = trade(held, near), trade(held, next_chip)
 
     next_sent, outer_sent, near_sent = pl.pallas_call(
-        pick,
+        functools.partial(pick, n == 16),
         out_shape=(jax.ShapeDtypeStruct((ROWS, MODES), full),) * 3,
         in_specs=[vmem] * 2,
         out_specs=(vmem,) * 3,
@@ -234,8 +229,13 @@
         cost_estimate=pl.CostEstimate(flops=0, bytes_accessed=700_000, transcendentals=0),
         name="pick",
     )(first, second)
-    across = trade(outer_sent, outer) if n == 16 else trade(held, lambda d: d + n // 2)
-    far_next, far_near = trade(next_sent, next_chip), trade(near_sent, near)
+    if n == 16:
+        across = trade(outer_sent, outer)
+        far_next = trade(next_sent, lambda d: {0: 7, 7: 0, 8: 15, 15: 8}.get(d, next_chip(d)))
+    else:
+        across = trade(held, lambda d: d + n // 2)
+        far_next = trade(next_sent, next_chip)
+    far_near = trade(near_sent, near)
 
     total, early, weight_high, weight_low = pl.pallas_call(
         project_early,

time: 35.5 us -> 35.5 us (level)
  waiting for transfers between devices: 15.1 us -> 15.8 us
  starting transfers between devices: 13 us -> 12.4 us
    ppermute x5, waiting for transfers between devices: 10.1 us -> 10.7 us  [swap(): return lax.ppermute(block, 'row', [(d, d ^ apart) for d in range(n)])]
    ppermute x5, starting transfers between devices: 2.73 us -> 2.14 us  [swap(): return lax.ppermute(block, 'row', [(d, d ^ apart) for d in range(n)])]
  transfers between devices with their start and end apart: 12 -> 12, of which waited for: 9 -> 9; matrix products, arithmetic and copies ran while one was open for 0% -> 0% of each run, Pallas kernels for 14% -> 13%
where the time goes in v10:
time: 35.5 us; the launch traced here: 35.4 us
  waiting for transfers between devices  15.8 us (45%)
  starting transfers between devices  12.4 us (35%)
  Pallas kernels  5.7 us (16%)
  between operations  1.44 us (4%)
    ppermute x5, waiting for transfers between devices, swap(): return lax.ppermute(block, 'row', [(d, d ^ apart) for d in range(n)])  10.7 us
    ppermute x7, starting transfers between devices, trade(): return lax.ppermute(block, 'row', [(d, partner(d) % n) for d in range(n)])  10.3 us
    ppermute x7, waiting for transfers between devices, trade(): return lax.ppermute(block, 'row', [(d, partner(d) % n) for d in range(n)])  5.13 us
    pallas_call x1, Pallas kernels, shards(): pl.pallas_call(assemble, out_shape=(jax.ShapeDtypeStruct((LINKS, ROWS, RO...  2.47 us
    ppermute x5, starting transfers between devices, swap(): return lax.ppermute(block, 'row', [(d, d ^ apart) for d in range(n)])  2.14 us
    pallas_call x1, Pallas kernels, shards(): pl.pallas_call(project_late, out_shape=(jax.ShapeDtypeStruct((ROWS, MODES...  1.12 us
    pallas_call x1, Pallas kernels, shards(): pl.pallas_call(project_early, out_shape=(jax.ShapeDtypeStruct((ROWS, MODE...  1.11 us
  transfers between devices with their start and end apart: 12, of which 9 were waited for; matrix products, arithmetic and copies ran while one was open for 0% of the time, Pallas kernels for 13%

profile of v10, /device:TPU:0, one launch (start us, length us, event | category | flops | bytes accessed | tf_op | source)
XLA Modules:
  0.0 35.4 jit_solution(14317267620184309071)
XLA Ops:
  0.6 0.0 copy-start.1
  0.6 0.0 copy-start.2
  0.7 0.0 copy-start.3
  0.7 5.1 %collective-permute-start = (f32[256,128]{1,0:T(8,128)}, f32[256,128]{1,0:T(8,128)S(1)}, u32[]{:S(2)}, u32[]{:S(2)}) collective-permute-start(f32[256,128]{1,0:T(8,128)} %basis_ref.1), channel_id=1, source_target_pairs={{0,12},{1,13},{2,14},{3,15},{4,8},{5,9},{6,10},{7,11},{8,4},{9,5},... | collective-permute-start | bytes 393224 | tf_op jit(solution)/shard_map/ppermute | solution.py:185
  5.8 0.0 collective-permute-start.1
  6.5 2.5 %assemble.1 = (bf16[8,256,256]{2,1,0:T(8,128)(2,1)S(1)}, bf16[8,256,256]{2,1,0:T(8,128)(2,1)S(1)}, f32[256,128]{1,0:T(8,128)S(1)}) custom-call(s32[1]{0:T(128)S(6)} %copy.9.count_ref, s32[128]{0:T(128)S(1)} %copy-done.2, s32[128]{0:T(128)S(1)} %bitcast.9, s32[128]{0:T(128)S(1)} %copy-done.4, f32[4096,128]{1,0:T(8,128)S(1)} %bitcast.8, ...), custom_call_target="tpu_custom_call" | custom-call | flops 10000000 | bytes 8000000 | tf_op jit(solution)/shard_map/assemble/pallas_call | solution.py:202
  9.0 0.1 collective-permute-start.2
  9.1 2.0 %collective-permute-start.3 = (f32[256,128]{1,0:T(8,128)S(1)}, f32[256,128]{1,0:T(8,128)S(1)}, u32[]{:S(2)}, u32[]{:S(2)}) collective-permute-start(f32[256,128]{1,0:T(8,128)S(1)} %get-tuple-element.18.refs_0_), channel_id=1, source_target_pairs={{0,15},{1,2},{2,1},{3,4},{4,3},{5,6},{6,5},{7,8},{8,7},{9,10},{10,... | collective-permute-start | bytes 393224 | tf_op jit(solution)/shard_map/ppermute | solution.py:185
  11.0 0.0 collective-permute-done.refs_1_.first_ref
  11.0 1.4 %collective-permute-done.1.refs_2_.second_ref = f32[256,128]{1,0:T(8,128)S(1)} collective-permute-done((f32[256,128]{1,0:T(8,128)}, f32[256,128]{1,0:T(8,128)S(1)}, u32[]{:S(2)}, u32[]{:S(2)}) %collective-permute-start.1) | collective-permute-done | bytes 131104 | tf_op jit(solution)/shard_map/ppermute | solution.py:185
  12.5 1.3 %collective-permute-start.4 = (f32[256,128]{1,0:T(8,128)S(1)}, f32[256,128]{1,0:T(8,128)S(1)}, u32[]{:S(2)}, u32[]{:S(2)}) collective-permute-start(f32[256,128]{1,0:T(8,128)S(1)} %get-tuple-element.20), channel_id=1, source_target_pairs={{0,7},{1,2},{2,1},{3,4},{4,3},{5,6},{6,5},{7,0},{8,15},{9,10},{10,... | collective-permute-start | bytes 393224 | tf_op jit(solution)/shard_map/ppermute | solution.py:185
  13.8 0.9 %collective-permute-start.5 = (f32[256,128]{1,0:T(8,128)S(1)}, f32[256,128]{1,0:T(8,128)S(1)}, u32[]{:S(2)}, u32[]{:S(2)}) collective-permute-start(f32[256,128]{1,0:T(8,128)S(1)} %get-tuple-element.21), channel_id=1, source_target_pairs={{0,4},{1,5},{2,6},{3,7},{4,0},{5,1},{6,2},{7,3},{8,12},{9,13},{10,... | collective-permute-start | bytes 393224 | tf_op jit(solution)/shard_map/ppermute | solution.py:185
  14.7 0.9 %collective-permute-start.6 = (f32[256,128]{1,0:T(8,128)S(1)}, f32[256,128]{1,0:T(8,128)S(1)}, u32[]{:S(2)}, u32[]{:S(2)}) collective-permute-start(f32[256,128]{1,0:T(8,128)S(1)} %get-tuple-element.22), channel_id=1, source_target_pairs={{0,1},{1,0},{2,3},{3,2},{4,5},{5,4},{6,7},{7,6},{8,9},{9,8},{10,11... | collective-permute-start | bytes 393224 | tf_op jit(solution)/shard_map/ppermute | solution.py:185
  15.6 0.0 collective-permute-done.2.refs_3_
  15.6 0.7 %collective-permute-done.3.refs_4_ = f32[256,128]{1,0:T(8,128)S(1)} collective-permute-done((f32[256,128]{1,0:T(8,128)S(1)}, f32[256,128]{1,0:T(8,128)S(1)}, u32[]{:S(2)}, u32[]{:S(2)}) %collective-permute-start.3) | collective-permute-done | bytes 131104 | tf_op jit(solution)/shard_map/ppermute | solution.py:185
  16.3 1.1 %project_early.1 = (f32[256,128]{1,0:T(8,128)S(1)}, f32[128,128]{1,0:T(8,128)S(1)}, bf16[3,128,256]{2,1,0:T(8,128)(2,1)S(1)}, bf16[3,128,256]{2,1,0:T(8,128)(2,1)S(1)}) custom-call(bf16[8,256,256]{2,1,0:T(8,128)(2,1)S(1)} %get-tuple-element.16.high_ref, bf16[8,256,256]{2,1,0:T(8,128)(2,1)S(1)} %get-tuple-element.17.low_ref, f32[1,256]{1,0:T(1,128)S(1)} %bitcast.10, ...), custom_call_target="tpu_custom_call" | custom-call | flops 20000000000 | bytes 2500000 | tf_op jit(solution)/shard_map/project_early/pallas_call | solution.py:240
  17.4 1.1 %collective-permute-done.4.refs_0_ = f32[256,128]{1,0:T(8,128)S(1)} collective-permute-done((f32[256,128]{1,0:T(8,128)S(1)}, f32[256,128]{1,0:T(8,128)S(1)}, u32[]{:S(2)}, u32[]{:S(2)}) %collective-permute-start.4) | collective-permute-done | bytes 131104 | tf_op jit(solution)/shard_map/ppermute | solution.py:185
  18.6 1.9 %collective-permute-done.5.refs_1_ = f32[256,128]{1,0:T(8,128)S(1)} collective-permute-done((f32[256,128]{1,0:T(8,128)S(1)}, f32[256,128]{1,0:T(8,128)S(1)}, u32[]{:S(2)}, u32[]{:S(2)}) %collective-permute-start.5) | collective-permute-done | bytes 131104 | tf_op jit(solution)/shard_map/ppermute | solution.py:185
  20.4 0.0 collective-permute-done.6.refs_2_
  20.5 0.3 reduce_late.1
  20.8 0.1 collective-permute-start.7
  20.9 1.2 %collective-permute-done.7 = f32[64,128]{1,0:T(8,128)S(1)} collective-permute-done((f32[64,128]{1,0:T(8,128)S(1)}, f32[64,128]{1,0:T(8,128)S(1)}, u32[]{:S(2)}, u32[]{:S(2)}) %collective-permute-start.7) | collective-permute-done | bytes 32800 | tf_op jit(solution)/shard_map/ppermute | solution.py:283
  22.1 0.2 collective-permute-start.8
  22.2 1.1 %project_late.1 = (f32[256,128]{1,0:T(8,128)}, f32[8,128]{1,0:T(8,128)S(1)}) custom-call(bf16[8,256,256]{2,1,0:T(8,128)(2,1)S(1)} %get-tuple-element.16.high_ref, bf16[8,256,256]{2,1,0:T(8,128)(2,1)S(1)} %get-tuple-element.17.low_ref, f32[256,128]{1,0:T(8,128)S(1)} %get-tuple-element.19.total_ref, f32[256,128]{1,0:T(8,128)S(1)} %collective-permute-done.4.refs_0_, ...), custom_call_target="tpu_custom_call" | custom-call | flops 160000000 | bytes 1500000 | tf_op jit(solution)/shard_map/project_late/pallas_call | solution.py:272
  23.3 2.1 %collective-permute-done.8.second_ref = f32[64,128]{1,0:T(8,128)S(1)} collective-permute-done((f32[64,128]{1,0:T(8,128)S(1)}, f32[64,128]{1,0:T(8,128)S(1)}, u32[]{:S(2)}, u32[]{:S(2)}) %collective-permute-start.8) | collective-permute-done | bytes 32800 | tf_op jit(solution)/shard_map/ppermute | solution.py:283
  25.4 0.9 %collective-permute-start.9 = (f32[64,128]{1,0:T(8,128)S(1)}, f32[64,128]{1,0:T(8,128)S(1)}, u32[]{:S(2)}, u32[]{:S(2)}) collective-permute-start(f32[64,128]{1,0:T(8,128)S(1)} %add_after.1), channel_id=1, source_target_pairs={{0,5},{1,4},{2,7},{3,6},{4,1},{5,0},{6,3},{7,2},{8,13},{9,12},{10,... | collective-permute-start | bytes 98312 | tf_op jit(solution)/shard_map/ppermute | solution.py:283
  26.3 2.4 %collective-permute-done.9 = f32[64,128]{1,0:T(8,128)S(1)} collective-permute-done((f32[64,128]{1,0:T(8,128)S(1)}, f32[64,128]{1,0:T(8,128)S(1)}, u32[]{:S(2)}, u32[]{:S(2)}) %collective-permute-start.9) | collective-permute-done | bytes 32800 | tf_op jit(solution)/shard_map/ppermute | solution.py:283
  28.8 0.1 collective-permute-start.10
  28.9 4.1 %collective-permute-done.10 = f32[64,128]{1,0:T(8,128)S(1)} collective-permute-done((f32[64,128]{1,0:T(8,128)S(1)}, f32[64,128]{1,0:T(8,128)S(1)}, u32[]{:S(2)}, u32[]{:S(2)}) %collective-permute-start.10) | collective-permute-done | bytes 32800 | tf_op jit(solution)/shard_map/ppermute | solution.py:283
  33.0 0.9 %collective-permute-start.11 = (f32[64,128]{1,0:T(8,128)S(1)}, f32[64,128]{1,0:T(8,128)S(1)}, u32[]{:S(2)}, u32[]{:S(2)}) collective-permute-start(f32[64,128]{1,0:T(8,128)S(1)} %add.11.mine_ref), channel_id=1, source_target_pairs={{0,1},{1,0},{2,3},{3,2},{4,5},{5,4},{6,7},{7,6},{8,9},{9,8},{10,11... | collective-permute-start | bytes 98312 | tf_op jit(solution)/shard_map/ppermute | solution.py:283
  33.9 0.9 %collective-permute-done.11.other_ref = f32[64,128]{1,0:T(8,128)S(1)} collective-permute-done((f32[64,128]{1,0:T(8,128)S(1)}, f32[64,128]{1,0:T(8,128)S(1)}, u32[]{:S(2)}, u32[]{:S(2)}) %collective-permute-start.11) | collective-permute-done | bytes 32800 | tf_op jit(solution)/shard_map/ppermute | solution.py:283
  34.7 0.6 %join.1 = f32[128,128]{1,0:T(8,128)} custom-call(s32[1]{0:T(128)} %bitcast.5.side_ref, f32[64,128]{1,0:T(8,128)S(1)} %add.11.mine_ref, f32[64,128]{1,0:T(8,128)S(1)} %collective-permute-done.11.other_ref), custom_call_target="tpu_custom_call" | custom-call | bytes 130000 | tf_op jit(solution)/shard_map/join/pallas_call | solution.py:298
  (15 shorter events, 0.1 us)
Async XLA Ops:
  0.6 5.8 %copy-start.1 = (f32[256,128]{1,0:T(8,128)S(1)}, f32[256,128]{1,0:T(8,128)}, u32[]{:S(2)}) copy-start(f32[256,128]{1,0:T(8,128)} %basis_ref.1) | copy-start | bytes 393220
  0.6 5.8 %copy-start.2 = (s32[128]{0:T(128)S(1)}, s32[128]{0:T(128)}, u32[]{:S(2)}) copy-start(s32[128]{0:T(128)} %rows_ref.1) | copy-start | bytes 1540
  0.7 5.8 %copy-start.3 = (s32[128,1]{0,1:T(1,128)S(1)}, s32[128,1]{0,1:T(1,128)}, u32[]{:S(2)}) copy-start(s32[128,1]{0,1:T(1,128)} %param.11) | copy-start | bytes 1540
  0.7 5.8 %copy-start.4 = (s32[128]{0:T(128)S(1)}, s32[128]{0:T(128)}, u32[]{:S(2)}) copy-start(s32[128]{0:T(128)} %offset_ref.1) | copy-start | bytes 1540
  0.7 5.8 %copy-start = (f32[128,4096]{1,0:T(8,128)S(1)}, f32[128,4096]{1,0:T(8,128)}, u32[]{:S(2)}) copy-start(f32[128,4096]{1,0:T(8,128)} %param.9) | copy-start | bytes 6291460
  0.7 10.4 %collective-permute-start = (f32[256,128]{1,0:T(8,128)}, f32[256,128]{1,0:T(8,128)S(1)}, u32[]{:S(2)}, u32[]{:S(2)}) collective-permute-start(f32[256,128]{1,0:T(8,128)} %basis_ref.1), channel_id=1, source_target_pairs={{0,12},{1,13},{2,14},{3,15},{4,8},{5,9},{6,10},{7,11},{8,4},{9,5},... | collective-permute-start | bytes 393224 | tf_op jit(solution)/shard_map/ppermute | solution.py:185
  5.8 6.6 %collective-permute-start.1 = (f32[256,128]{1,0:T(8,128)}, f32[256,128]{1,0:T(8,128)S(1)}, u32[]{:S(2)}, u32[]{:S(2)}) collective-permute-start(f32[256,128]{1,0:T(8,128)} %basis_ref.1), channel_id=1, source_target_pairs={{0,4},{1,5},{2,6},{3,7},{4,0},{5,1},{6,2},{7,3},{8,12},{9,13},{10,... | collective-permute-start | bytes 393224 | tf_op jit(solution)/shard_map/ppermute | solution.py:185
  5.8 10.5 %copy-start.5 = (f32[256]{0:T(256)S(1)}, f32[256]{0:T(256)}, u32[]{:S(2)}) copy-start(f32[256]{0:T(256)} %param.8) | copy-start | bytes 3076
  9.0 6.6 %collective-permute-start.2 = (f32[256,128]{1,0:T(8,128)S(1)}, f32[256,128]{1,0:T(8,128)S(1)}, u32[]{:S(2)}, u32[]{:S(2)}) collective-permute-start(f32[256,128]{1,0:T(8,128)S(1)} %get-tuple-element.18.refs_0_), channel_id=1, source_target_pairs={{0,1},{1,0},{2,3},{3,2},{4,5},{5,4},{6,7},{7,6},{8,9},{9,8},{10,11... | collective-permute-start | bytes 393224 | tf_op jit(solution)/shard_map/ppermute | solution.py:185
  9.1 7.2 %collective-permute-start.3 = (f32[256,128]{1,0:T(8,128)S(1)}, f32[256,128]{1,0:T(8,128)S(1)}, u32[]{:S(2)}, u32[]{:S(2)}) collective-permute-start(f32[256,128]{1,0:T(8,128)S(1)} %get-tuple-element.18.refs_0_), channel_id=1, source_target_pairs={{0,15},{1,2},{2,1},{3,4},{4,3},{5,6},{6,5},{7,8},{8,7},{9,10},{10,... | collective-permute-start | bytes 393224 | tf_op jit(solution)/shard_map/ppermute | solution.py:185
  12.5 6.1 %collective-permute-start.4 = (f32[256,128]{1,0:T(8,128)S(1)}, f32[256,128]{1,0:T(8,128)S(1)}, u32[]{:S(2)}, u32[]{:S(2)}) collective-permute-start(f32[256,128]{1,0:T(8,128)S(1)} %get-tuple-element.20), channel_id=1, source_target_pairs={{0,7},{1,2},{2,1},{3,4},{4,3},{5,6},{6,5},{7,0},{8,15},{9,10},{10,... | collective-permute-start | bytes 393224 | tf_op jit(solution)/shard_map/ppermute | solution.py:185
  13.8 6.7 %collective-permute-start.5 = (f32[256,128]{1,0:T(8,128)S(1)}, f32[256,128]{1,0:T(8,128)S(1)}, u32[]{:S(2)}, u32[]{:S(2)}) collective-permute-start(f32[256,128]{1,0:T(8,128)S(1)} %get-tuple-element.21), channel_id=1, source_target_pairs={{0,4},{1,5},{2,6},{3,7},{4,0},{5,1},{6,2},{7,3},{8,12},{9,13},{10,... | collective-permute-start | bytes 393224 | tf_op jit(solution)/shard_map/ppermute | solution.py:185
  14.7 5.8 %collective-permute-start.6 = (f32[256,128]{1,0:T(8,128)S(1)}, f32[256,128]{1,0:T(8,128)S(1)}, u32[]{:S(2)}, u32[]{:S(2)}) collective-permute-start(f32[256,128]{1,0:T(8,128)S(1)} %get-tuple-element.22), channel_id=1, source_target_pairs={{0,1},{1,0},{2,3},{3,2},{4,5},{5,4},{6,7},{7,6},{8,9},{9,8},{10,11... | collective-permute-start | bytes 393224 | tf_op jit(solution)/shard_map/ppermute | solution.py:185
  20.8 1.3 %collective-permute-start.7 = (f32[64,128]{1,0:T(8,128)S(1)}, f32[64,128]{1,0:T(8,128)S(1)}, u32[]{:S(2)}, u32[]{:S(2)}) collective-permute-start(f32[64,128]{1,0:T(8,128)S(1)} %get-tuple-element.28), channel_id=1, source_target_pairs={{0,1},{1,0},{2,3},{3,2},{4,5},{5,4},{6,7},{7,6},{8,9},{9,8},{10,11... | collective-permute-start | bytes 98312 | tf_op jit(solution)/shard_map/ppermute | solution.py:283
  22.1 3.3 %collective-permute-start.8 = (f32[64,128]{1,0:T(8,128)S(1)}, f32[64,128]{1,0:T(8,128)S(1)}, u32[]{:S(2)}, u32[]{:S(2)}) collective-permute-start(f32[64,128]{1,0:T(8,128)S(1)} %add.9.first_ref), channel_id=1, source_target_pairs={{0,3},{1,2},{2,1},{3,0},{4,7},{5,6},{6,5},{7,4},{8,11},{9,10},{10,... | collective-permute-start | bytes 98312 | tf_op jit(solution)/shard_map/ppermute | solution.py:283
  25.4 3.3 %collective-permute-start.9 = (f32[64,128]{1,0:T(8,128)S(1)}, f32[64,128]{1,0:T(8,128)S(1)}, u32[]{:S(2)}, u32[]{:S(2)}) collective-permute-start(f32[64,128]{1,0:T(8,128)S(1)} %add_after.1), channel_id=1, source_target_pairs={{0,5},{1,4},{2,7},{3,6},{4,1},{5,0},{6,3},{7,2},{8,13},{9,12},{10,... | collective-permute-start | bytes 98312 | tf_op jit(solution)/shard_map/ppermute | solution.py:283
  28.8 4.2 %collective-permute-start.10 = (f32[64,128]{1,0:T(8,128)S(1)}, f32[64,128]{1,0:T(8,128)S(1)}, u32[]{:S(2)}, u32[]{:S(2)}) collective-permute-start(f32[64,128]{1,0:T(8,128)S(1)} %add.10), channel_id=1, source_target_pairs={{0,9},{1,8},{2,11},{3,10},{4,13},{5,12},{6,15},{7,14},{8,1},{9,0},... | collective-permute-start | bytes 98312 | tf_op jit(solution)/shard_map/ppermute | solution.py:283
  33.0 1.7 %collective-permute-start.11 = (f32[64,128]{1,0:T(8,128)S(1)}, f32[64,128]{1,0:T(8,128)S(1)}, u32[]{:S(2)}, u32[]{:S(2)}) collective-permute-start(f32[64,128]{1,0:T(8,128)S(1)} %add.11.mine_ref), channel_id=1, source_target_pairs={{0,1},{1,0},{2,3},{3,2},{4,5},{5,4},{6,7},{7,6},{8,9},{9,8},{10,11... | collective-permute-start | bytes 98312 | tf_op jit(solution)/shard_map/ppermute | solution.py:283

commit v11 on v10

--- a/solution.py
+++ b/solution.py
@@ -146,13 +146,13 @@
         one_of(4, even_four),
         one_of(1, even),
         one_of(n - 1, even),
+        n // 2,
         one_of(n - 5, even),
-        n // 2,
         one_of(5, even),
     )
 
 
-def pick(short, first_ref, second_ref, next_ref, outer_ref, near_ref):
+def pick(short, first_ref, second_ref, outer_ref, next_ref, near_ref):
     outer_ref[...] = first_ref[...]
     me = lax.axis_index("row")
     straight = (me % 2 == 1) == ((me // 4) % 2 == 0)
@@ -220,7 +220,7 @@
     )(tile_count, tile_rows, tile_owner[:, 0], tile_offset, blocks, basis, token)
     beside, beyond = trade(held, near), trade(held, next_chip)
 
-    next_sent, outer_sent, near_sent = pl.pallas_call(
+    outer_sent, next_sent, near_sent = pl.pallas_call(
         functools.partial(pick, n == 16),
         out_shape=(jax.ShapeDtypeStruct((ROWS, MODES), full),) * 3,
         in_specs=[vmem] * 2,
@@ -267,7 +267,7 @@
         compiler_params=params,
         cost_estimate=pl.CostEstimate(flops=80_000_000, bytes_accessed=700_000, transcendentals=0),
         name="reduce_late",
-    )(side, weight_high, weight_low, early, far_next, across, far_near)
+    )(side, weight_high, weight_low, early, across, far_next, far_near)
 
     stiff_image, done = pl.pallas_call(
         project_late,
@@ -277,7 +277,7 @@
         compiler_params=params,
         cost_estimate=pl.CostEstimate(flops=160_000_000, bytes_accessed=1_500_000, transcendentals=0),
         name="project_late",
-    )(high, low, total, far_next, across, far_near)
+    )(high, low, total, across, far_next, far_near)
 
     def swap(block, apart):
         return lax.ppermute(block, "row", [(d, d ^ apart) for d in range(n)])

time: 35.5 us -> 36 us (1.014)
  waiting for transfers between devices: 15.8 us -> 16.7 us
  starting transfers between devices: 12.4 us -> 11.8 us
    ppermute x5, waiting for transfers between devices: 10.7 us -> 11.8 us  [swap(): return lax.ppermute(block, 'row', [(d, d ^ apart) for d in range(n)])]
    ppermute x5, starting transfers between devices: 2.14 us -> 1.28 us  [swap(): return lax.ppermute(block, 'row', [(d, d ^ apart) for d in range(n)])]
  transfers between devices with their start and end apart: 12 -> 12, of which waited for: 9 -> 9; matrix products, arithmetic and copies ran while one was open for 0% -> 0% of each run, Pallas kernels for 13% -> 14%
where the time goes in v11:
time: 36 us; the launch traced here: 35.8 us
  waiting for transfers between devices  16.7 us (46%)
  starting transfers between devices  11.8 us (33%)
  Pallas kernels  5.88 us (16%)
  between operations  1.44 us (4%)
    ppermute x5, waiting for transfers between devices, swap(): return lax.ppermute(block, 'row', [(d, d ^ apart) for d in range(n)])  11.8 us
    ppermute x7, starting transfers between devices, trade(): return lax.ppermute(block, 'row', [(d, partner(d) % n) for d in range(n)])  10.5 us
    ppermute x7, waiting for transfers between devices, trade(): return lax.ppermute(block, 'row', [(d, partner(d) % n) for d in range(n)])  4.9 us
    pallas_call x1, Pallas kernels, shards(): pl.pallas_call(assemble, out_shape=(jax.ShapeDtypeStruct((LINKS, ROWS, RO...  2.65 us
    ppermute x5, starting transfers between devices, swap(): return lax.ppermute(block, 'row', [(d, d ^ apart) for d in range(n)])  1.28 us
    pallas_call x1, Pallas kernels, shards(): pl.pallas_call(project_late, out_shape=(jax.ShapeDtypeStruct((ROWS, MODES...  1.12 us
    pallas_call x1, Pallas kernels, shards(): pl.pallas_call(project_early, out_shape=(jax.ShapeDtypeStruct((ROWS, MODE...  1.11 us
  transfers between devices with their start and end apart: 12, of which 9 were waited for; matrix products, arithmetic and copies ran while one was open for 0% of the time, Pallas kernels for 14%

profile of v11, /device:TPU:0, one launch (start us, length us, event | category | flops | bytes accessed | tf_op | source)
XLA Modules:
  0.0 35.8 jit_solution(15908426881544058700)
XLA Ops:
  0.6 0.0 copy-start.1
  0.6 0.0 copy-start.2
  0.7 0.0 copy-start.3
  0.7 5.1 %collective-permute-start = (f32[256,128]{1,0:T(8,128)}, f32[256,128]{1,0:T(8,128)S(1)}, u32[]{:S(2)}, u32[]{:S(2)}) collective-permute-start(f32[256,128]{1,0:T(8,128)} %basis_ref.1), channel_id=1, source_target_pairs={{0,12},{1,13},{2,14},{3,15},{4,8},{5,9},{6,10},{7,11},{8,4},{9,5},... | collective-permute-start | bytes 393224 | tf_op jit(solution)/shard_map/ppermute | solution.py:185
  5.8 0.0 collective-permute-start.1
  6.5 2.7 %assemble.1 = (bf16[8,256,256]{2,1,0:T(8,128)(2,1)S(1)}, bf16[8,256,256]{2,1,0:T(8,128)(2,1)S(1)}, f32[256,128]{1,0:T(8,128)S(1)}) custom-call(s32[1]{0:T(128)S(6)} %copy.9.count_ref, s32[128]{0:T(128)S(1)} %copy-done.2, s32[128]{0:T(128)S(1)} %bitcast.9, s32[128]{0:T(128)S(1)} %copy-done.4, f32[4096,128]{1,0:T(8,128)S(1)} %bitcast.8, ...), custom_call_target="tpu_custom_call" | custom-call | flops 10000000 | bytes 8000000 | tf_op jit(solution)/shard_map/assemble/pallas_call | solution.py:202
  9.2 0.1 collective-permute-start.2
  9.3 1.9 %collective-permute-start.3 = (f32[256,128]{1,0:T(8,128)S(1)}, f32[256,128]{1,0:T(8,128)S(1)}, u32[]{:S(2)}, u32[]{:S(2)}) collective-permute-start(f32[256,128]{1,0:T(8,128)S(1)} %get-tuple-element.18.refs_0_), channel_id=1, source_target_pairs={{0,15},{1,2},{2,1},{3,4},{4,3},{5,6},{6,5},{7,8},{8,7},{9,10},{10,... | collective-permute-start | bytes 393224 | tf_op jit(solution)/shard_map/ppermute | solution.py:185
  11.2 0.0 collective-permute-done.refs_1_.first_ref
  11.2 1.2 %collective-permute-done.1.refs_2_.second_ref = f32[256,128]{1,0:T(8,128)S(1)} collective-permute-done((f32[256,128]{1,0:T(8,128)}, f32[256,128]{1,0:T(8,128)S(1)}, u32[]{:S(2)}, u32[]{:S(2)}) %collective-permute-start.1) | collective-permute-done | bytes 131104 | tf_op jit(solution)/shard_map/ppermute | solution.py:185
  12.5 1.8 %collective-permute-start.4 = (f32[256,128]{1,0:T(8,128)S(1)}, f32[256,128]{1,0:T(8,128)S(1)}, u32[]{:S(2)}, u32[]{:S(2)}) collective-permute-start(f32[256,128]{1,0:T(8,128)S(1)} %get-tuple-element.20), channel_id=1, source_target_pairs={{0,4},{1,5},{2,6},{3,7},{4,0},{5,1},{6,2},{7,3},{8,12},{9,13},{10,... | collective-permute-start | bytes 393224 | tf_op jit(solution)/shard_map/ppermute | solution.py:185
  14.2 0.2 collective-permute-start.5
  14.4 1.4 %collective-permute-start.6 = (f32[256,128]{1,0:T(8,128)S(1)}, f32[256,128]{1,0:T(8,128)S(1)}, u32[]{:S(2)}, u32[]{:S(2)}) collective-permute-start(f32[256,128]{1,0:T(8,128)S(1)} %get-tuple-element.22), channel_id=1, source_target_pairs={{0,1},{1,0},{2,3},{3,2},{4,5},{5,4},{6,7},{7,6},{8,9},{9,8},{10,11... | collective-permute-start | bytes 393224 | tf_op jit(solution)/shard_map/ppermute | solution.py:185
  15.8 0.0 collective-permute-done.2.refs_3_
  15.8 0.7 %collective-permute-done.3.refs_4_ = f32[256,128]{1,0:T(8,128)S(1)} collective-permute-done((f32[256,128]{1,0:T(8,128)S(1)}, f32[256,128]{1,0:T(8,128)S(1)}, u32[]{:S(2)}, u32[]{:S(2)}) %collective-permute-start.3) | collective-permute-done | bytes 131104 | tf_op jit(solution)/shard_map/ppermute | solution.py:185
  16.5 1.1 %project_early.1 = (f32[256,128]{1,0:T(8,128)S(1)}, f32[128,128]{1,0:T(8,128)S(1)}, bf16[3,128,256]{2,1,0:T(8,128)(2,1)S(1)}, bf16[3,128,256]{2,1,0:T(8,128)(2,1)S(1)}) custom-call(bf16[8,256,256]{2,1,0:T(8,128)(2,1)S(1)} %get-tuple-element.16.high_ref, bf16[8,256,256]{2,1,0:T(8,128)(2,1)S(1)} %get-tuple-element.17.low_ref, f32[1,256]{1,0:T(1,128)S(1)} %bitcast.10, ...), custom_call_target="tpu_custom_call" | custom-call | flops 20000000000 | bytes 2500000 | tf_op jit(solution)/shard_map/project_early/pallas_call | solution.py:240
  17.6 0.5 %collective-permute-done.4.refs_0_ = f32[256,128]{1,0:T(8,128)S(1)} collective-permute-done((f32[256,128]{1,0:T(8,128)S(1)}, f32[256,128]{1,0:T(8,128)S(1)}, u32[]{:S(2)}, u32[]{:S(2)}) %collective-permute-start.4) | collective-permute-done | bytes 131104 | tf_op jit(solution)/shard_map/ppermute | solution.py:185
  18.1 2.5 %collective-permute-done.5.refs_1_ = f32[256,128]{1,0:T(8,128)S(1)} collective-permute-done((f32[256,128]{1,0:T(8,128)S(1)}, f32[256,128]{1,0:T(8,128)S(1)}, u32[]{:S(2)}, u32[]{:S(2)}) %collective-permute-start.5) | collective-permute-done | bytes 131104 | tf_op jit(solution)/shard_map/ppermute | solution.py:185
  20.6 0.0 collective-permute-done.6.refs_2_
  20.6 0.3 reduce_late.1
  21.0 0.1 collective-permute-start.7
  21.0 1.2 %collective-permute-done.7 = f32[64,128]{1,0:T(8,128)S(1)} collective-permute-done((f32[64,128]{1,0:T(8,128)S(1)}, f32[64,128]{1,0:T(8,128)S(1)}, u32[]{:S(2)}, u32[]{:S(2)}) %collective-permute-start.7) | collective-permute-done | bytes 32800 | tf_op jit(solution)/shard_map/ppermute | solution.py:283
  22.2 0.7 %collective-permute-start.8 = (f32[64,128]{1,0:T(8,128)S(1)}, f32[64,128]{1,0:T(8,128)S(1)}, u32[]{:S(2)}, u32[]{:S(2)}) collective-permute-start(f32[64,128]{1,0:T(8,128)S(1)} %add.9.first_ref), channel_id=1, source_target_pairs={{0,3},{1,2},{2,1},{3,0},{4,7},{5,6},{6,5},{7,4},{8,11},{9,10},{10,... | collective-permute-start | bytes 98312 | tf_op jit(solution)/shard_map/ppermute | solution.py:283
  22.9 1.1 %project_late.1 = (f32[256,128]{1,0:T(8,128)}, f32[8,128]{1,0:T(8,128)S(1)}) custom-call(bf16[8,256,256]{2,1,0:T(8,128)(2,1)S(1)} %get-tuple-element.16.high_ref, bf16[8,256,256]{2,1,0:T(8,128)(2,1)S(1)} %get-tuple-element.17.low_ref, f32[256,128]{1,0:T(8,128)S(1)} %get-tuple-element.19.total_ref, f32[256,128]{1,0:T(8,128)S(1)} %collective-permute-done.4.refs_0_, ...), custom_call_target="tpu_custom_call" | custom-call | flops 160000000 | bytes 1500000 | tf_op jit(solution)/shard_map/project_late/pallas_call | solution.py:272
  24.0 1.6 %collective-permute-done.8.second_ref = f32[64,128]{1,0:T(8,128)S(1)} collective-permute-done((f32[64,128]{1,0:T(8,128)S(1)}, f32[64,128]{1,0:T(8,128)S(1)}, u32[]{:S(2)}, u32[]{:S(2)}) %collective-permute-start.8) | collective-permute-done | bytes 32800 | tf_op jit(solution)/shard_map/ppermute | solution.py:283
  25.6 0.1 collective-permute-start.9
  25.7 3.2 %collective-permute-done.9 = f32[64,128]{1,0:T(8,128)S(1)} collective-permute-done((f32[64,128]{1,0:T(8,128)S(1)}, f32[64,128]{1,0:T(8,128)S(1)}, u32[]{:S(2)}, u32[]{:S(2)}) %collective-permute-start.9) | collective-permute-done | bytes 32800 | tf_op jit(solution)/shard_map/ppermute | solution.py:283
  28.9 0.3 collective-permute-start.10
  29.3 4.7 %collective-permute-done.10 = f32[64,128]{1,0:T(8,128)S(1)} collective-permute-done((f32[64,128]{1,0:T(8,128)S(1)}, f32[64,128]{1,0:T(8,128)S(1)}, u32[]{:S(2)}, u32[]{:S(2)}) %collective-permute-start.10) | collective-permute-done | bytes 32800 | tf_op jit(solution)/shard_map/ppermute | solution.py:283
  34.0 0.1 collective-permute-start.11
  34.1 1.1 %collective-permute-done.11.other_ref = f32[64,128]{1,0:T(8,128)S(1)} collective-permute-done((f32[64,128]{1,0:T(8,128)S(1)}, f32[64,128]{1,0:T(8,128)S(1)}, u32[]{:S(2)}, u32[]{:S(2)}) %collective-permute-start.11) | collective-permute-done | bytes 32800 | tf_op jit(solution)/shard_map/ppermute | solution.py:283
  35.2 0.6 %join.1 = f32[128,128]{1,0:T(8,128)} custom-call(s32[1]{0:T(128)} %bitcast.5.side_ref, f32[64,128]{1,0:T(8,128)S(1)} %add.11.mine_ref, f32[64,128]{1,0:T(8,128)S(1)} %collective-permute-done.11.other_ref), custom_call_target="tpu_custom_call" | custom-call | bytes 130000 | tf_op jit(solution)/shard_map/join/pallas_call | solution.py:298
  (15 shorter events, 0.1 us)
Async XLA Ops:
  0.6 5.8 %copy-start.1 = (f32[256,128]{1,0:T(8,128)S(1)}, f32[256,128]{1,0:T(8,128)}, u32[]{:S(2)}) copy-start(f32[256,128]{1,0:T(8,128)} %basis_ref.1) | copy-start | bytes 393220
  0.6 5.8 %copy-start.2 = (s32[128]{0:T(128)S(1)}, s32[128]{0:T(128)}, u32[]{:S(2)}) copy-start(s32[128]{0:T(128)} %rows_ref.1) | copy-start | bytes 1540
  0.7 5.8 %copy-start.3 = (s32[128,1]{0,1:T(1,128)S(1)}, s32[128,1]{0,1:T(1,128)}, u32[]{:S(2)}) copy-start(s32[128,1]{0,1:T(1,128)} %param.11) | copy-start | bytes 1540
  0.7 5.8 %copy-start.4 = (s32[128]{0:T(128)S(1)}, s32[128]{0:T(128)}, u32[]{:S(2)}) copy-start(s32[128]{0:T(128)} %offset_ref.1) | copy-start | bytes 1540
  0.7 5.8 %copy-start = (f32[128,4096]{1,0:T(8,128)S(1)}, f32[128,4096]{1,0:T(8,128)}, u32[]{:S(2)}) copy-start(f32[128,4096]{1,0:T(8,128)} %param.9) | copy-start | bytes 6291460
  0.7 10.5 %collective-permute-start = (f32[256,128]{1,0:T(8,128)}, f32[256,128]{1,0:T(8,128)S(1)}, u32[]{:S(2)}, u32[]{:S(2)}) collective-permute-start(f32[256,128]{1,0:T(8,128)} %basis_ref.1), channel_id=1, source_target_pairs={{0,12},{1,13},{2,14},{3,15},{4,8},{5,9},{6,10},{7,11},{8,4},{9,5},... | collective-permute-start | bytes 393224 | tf_op jit(solution)/shard_map/ppermute | solution.py:185
  5.8 6.6 %collective-permute-start.1 = (f32[256,128]{1,0:T(8,128)}, f32[256,128]{1,0:T(8,128)S(1)}, u32[]{:S(2)}, u32[]{:S(2)}) collective-permute-start(f32[256,128]{1,0:T(8,128)} %basis_ref.1), channel_id=1, source_target_pairs={{0,4},{1,5},{2,6},{3,7},{4,0},{5,1},{6,2},{7,3},{8,12},{9,13},{10,... | collective-permute-start | bytes 393224 | tf_op jit(solution)/shard_map/ppermute | solution.py:185
  5.8 10.7 %copy-start.5 = (f32[256]{0:T(256)S(1)}, f32[256]{0:T(256)}, u32[]{:S(2)}) copy-start(f32[256]{0:T(256)} %param.8) | copy-start | bytes 3076
  9.2 6.7 %collective-permute-start.2 = (f32[256,128]{1,0:T(8,128)S(1)}, f32[256,128]{1,0:T(8,128)S(1)}, u32[]{:S(2)}, u32[]{:S(2)}) collective-permute-start(f32[256,128]{1,0:T(8,128)S(1)} %get-tuple-element.18.refs_0_), channel_id=1, source_target_pairs={{0,1},{1,0},{2,3},{3,2},{4,5},{5,4},{6,7},{7,6},{8,9},{9,8},{10,11... | collective-permute-start | bytes 393224 | tf_op jit(solution)/shard_map/ppermute | solution.py:185
  9.3 7.2 %collective-permute-start.3 = (f32[256,128]{1,0:T(8,128)S(1)}, f32[256,128]{1,0:T(8,128)S(1)}, u32[]{:S(2)}, u32[]{:S(2)}) collective-permute-start(f32[256,128]{1,0:T(8,128)S(1)} %get-tuple-element.18.refs_0_), channel_id=1, source_target_pairs={{0,15},{1,2},{2,1},{3,4},{4,3},{5,6},{6,5},{7,8},{8,7},{9,10},{10,... | collective-permute-start | bytes 393224 | tf_op jit(solution)/shard_map/ppermute | solution.py:185
  12.5 5.6 %collective-permute-start.4 = (f32[256,128]{1,0:T(8,128)S(1)}, f32[256,128]{1,0:T(8,128)S(1)}, u32[]{:S(2)}, u32[]{:S(2)}) collective-permute-start(f32[256,128]{1,0:T(8,128)S(1)} %get-tuple-element.20), channel_id=1, source_target_pairs={{0,4},{1,5},{2,6},{3,7},{4,0},{5,1},{6,2},{7,3},{8,12},{9,13},{10,... | collective-permute-start | bytes 393224 | tf_op jit(solution)/shard_map/ppermute | solution.py:185
  14.2 6.4 %collective-permute-start.5 = (f32[256,128]{1,0:T(8,128)S(1)}, f32[256,128]{1,0:T(8,128)S(1)}, u32[]{:S(2)}, u32[]{:S(2)}) collective-permute-start(f32[256,128]{1,0:T(8,128)S(1)} %get-tuple-element.21), channel_id=1, source_target_pairs={{0,7},{1,2},{2,1},{3,4},{4,3},{5,6},{6,5},{7,0},{8,15},{9,10},{10,... | collective-permute-start | bytes 393224 | tf_op jit(solution)/shard_map/ppermute | solution.py:185
  14.4 6.2 %collective-permute-start.6 = (f32[256,128]{1,0:T(8,128)S(1)}, f32[256,128]{1,0:T(8,128)S(1)}, u32[]{:S(2)}, u32[]{:S(2)}) collective-permute-start(f32[256,128]{1,0:T(8,128)S(1)} %get-tuple-element.22), channel_id=1, source_target_pairs={{0,1},{1,0},{2,3},{3,2},{4,5},{5,4},{6,7},{7,6},{8,9},{9,8},{10,11... | collective-permute-start | bytes 393224 | tf_op jit(solution)/shard_map/ppermute | solution.py:185
  21.0 1.3 %collective-permute-start.7 = (f32[64,128]{1,0:T(8,128)S(1)}, f32[64,128]{1,0:T(8,128)S(1)}, u32[]{:S(2)}, u32[]{:S(2)}) collective-permute-start(f32[64,128]{1,0:T(8,128)S(1)} %get-tuple-element.28), channel_id=1, source_target_pairs={{0,1},{1,0},{2,3},{3,2},{4,5},{5,4},{6,7},{7,6},{8,9},{9,8},{10,11... | collective-permute-start | bytes 98312 | tf_op jit(solution)/shard_map/ppermute | solution.py:283
  22.2 3.3 %collective-permute-start.8 = (f32[64,128]{1,0:T(8,128)S(1)}, f32[64,128]{1,0:T(8,128)S(1)}, u32[]{:S(2)}, u32[]{:S(2)}) collective-permute-start(f32[64,128]{1,0:T(8,128)S(1)} %add.9.first_ref), channel_id=1, source_target_pairs={{0,3},{1,2},{2,1},{3,0},{4,7},{5,6},{6,5},{7,4},{8,11},{9,10},{10,... | collective-permute-start | bytes 98312 | tf_op jit(solution)/shard_map/ppermute | solution.py:283
  25.6 3.3 %collective-permute-start.9 = (f32[64,128]{1,0:T(8,128)S(1)}, f32[64,128]{1,0:T(8,128)S(1)}, u32[]{:S(2)}, u32[]{:S(2)}) collective-permute-start(f32[64,128]{1,0:T(8,128)S(1)} %add_after.1), channel_id=1, source_target_pairs={{0,5},{1,4},{2,7},{3,6},{4,1},{5,0},{6,3},{7,2},{8,13},{9,12},{10,... | collective-permute-start | bytes 98312 | tf_op jit(solution)/shard_map/ppermute | solution.py:283
  28.9 5.0 %collective-permute-start.10 = (f32[64,128]{1,0:T(8,128)S(1)}, f32[64,128]{1,0:T(8,128)S(1)}, u32[]{:S(2)}, u32[]{:S(2)}) collective-permute-start(f32[64,128]{1,0:T(8,128)S(1)} %add.10), channel_id=1, source_target_pairs={{0,9},{1,8},{2,11},{3,10},{4,13},{5,12},{6,15},{7,14},{8,1},{9,0},... | collective-permute-start | bytes 98312 | tf_op jit(solution)/shard_map/ppermute | solution.py:283
  34.0 1.2 %collective-permute-start.11 = (f32[64,128]{1,0:T(8,128)S(1)}, f32[64,128]{1,0:T(8,128)S(1)}, u32[]{:S(2)}, u32[]{:S(2)}) collective-permute-start(f32[64,128]{1,0:T(8,128)S(1)} %add.11.mine_ref), channel_id=1, source_target_pairs={{0,1},{1,0},{2,3},{3,2},{4,5},{5,4},{6,7},{7,6},{8,9},{9,8},{10,11... | collective-permute-start | bytes 98312 | tf_op jit(solution)/shard_map/ppermute | solution.py:283

commit v12 on v11

--- a/solution.py
+++ b/solution.py
@@ -152,8 +152,11 @@
     )
 
 
-def pick(short, first_ref, second_ref, outer_ref, next_ref, near_ref):
+def hand_on(first_ref, outer_ref):
     outer_ref[...] = first_ref[...]
+
+
+def pick(short, first_ref, second_ref, next_ref, near_ref):
     me = lax.axis_index("row")
     straight = (me % 2 == 1) == ((me // 4) % 2 == 0)
 
@@ -220,17 +223,26 @@
     )(tile_count, tile_rows, tile_owner[:, 0], tile_offset, blocks, basis, token)
     beside, beyond = trade(held, near), trade(held, next_chip)
 
-    outer_sent, next_sent, near_sent = pl.pallas_call(
+    ready = pl.pallas_call(
+        hand_on,
+        out_shape=jax.ShapeDtypeStruct((ROWS, MODES), full),
+        in_specs=[vmem],
+        out_specs=vmem,
+        compiler_params=params,
+        cost_estimate=pl.CostEstimate(flops=5_000_000_000, bytes_accessed=300_000, transcendentals=0),
+        name="hand_on",
+    )(first)
+    next_sent, near_sent = pl.pallas_call(
         functools.partial(pick, n == 16),
-        out_shape=(jax.ShapeDtypeStruct((ROWS, MODES), full),) * 3,
+        out_shape=(jax.ShapeDtypeStruct((ROWS, MODES), full),) * 2,
         in_specs=[vmem] * 2,
-        out_specs=(vmem,) * 3,
+        out_specs=(vmem,) * 2,
         compiler_params=params,
         cost_estimate=pl.CostEstimate(flops=0, bytes_accessed=700_000, transcendentals=0),
         name="pick",
     )(first, second)
     if n == 16:
-        across = trade(outer_sent, outer)
+        across = trade(ready, outer)
         far_next = trade(next_sent, lambda d: {0: 7, 7: 0, 8: 15, 15: 8}.get(d, next_chip(d)))
     else:
         across = trade(held, lambda d: d + n // 2)

time: 36 us -> 35.8 us (level)
  starting transfers between devices: 11.8 us -> 10.7 us
  waiting for transfers between devices: 16.7 us -> 17.7 us
    ppermute x5, starting transfers between devices: 1.28 us -> 0.61 us  [swap(): return lax.ppermute(block, 'row', [(d, d ^ apart) for d in range(n)])]
    ppermute x5, waiting for transfers between devices: 11.8 us -> 12.4 us  [swap(): return lax.ppermute(block, 'row', [(d, d ^ apart) for d in range(n)])]
    ppermute x7, starting transfers between devices: 10.5 us -> 10.1 us  [trade(): return lax.ppermute(block, 'row', [(d, partner(d) % n) for d in range(n)])]
    ppermute x7, waiting for transfers between devices: 4.9 us -> 5.3 us  [trade(): return lax.ppermute(block, 'row', [(d, partner(d) % n) for d in range(n)])]
  transfers between devices with their start and end apart: 12 -> 12, of which waited for: 9 -> 9; matrix products, arithmetic and copies ran while one was open for 0% -> 0% of each run, Pallas kernels for 14% -> 13%
where the time goes in v12:
time: 35.8 us; the launch traced here: 35.6 us
  waiting for transfers between devices  17.7 us (49%)
  starting transfers between devices  10.7 us (30%)
  Pallas kernels  5.71 us (16%)
  between operations  1.43 us (4%)
    ppermute x5, waiting for transfers between devices, swap(): return lax.ppermute(block, 'row', [(d, d ^ apart) for d in range(n)])  12.4 us
    ppermute x7, starting transfers between devices, trade(): return lax.ppermute(block, 'row', [(d, partner(d) % n) for d in range(n)])  10.1 us
    ppermute x7, waiting for transfers between devices, trade(): return lax.ppermute(block, 'row', [(d, partner(d) % n) for d in range(n)])  5.3 us
    pallas_call x1, Pallas kernels, shards(): pl.pallas_call(assemble, out_shape=(jax.ShapeDtypeStruct((LINKS, ROWS, RO...  2.47 us
    pallas_call x1, Pallas kernels, shards(): pl.pallas_call(project_late, out_shape=(jax.ShapeDtypeStruct((ROWS, MODES...  1.12 us
    pallas_call x1, Pallas kernels, shards(): pl.pallas_call(project_early, out_shape=(jax.ShapeDtypeStruct((ROWS, MODE...  1.11 us
  transfers between devices with their start and end apart: 12, of which 9 were waited for; matrix products, arithmetic and copies ran while one was open for 0% of the time, Pallas kernels for 13%

profile of v12, /device:TPU:0, one launch (start us, length us, event | category | flops | bytes accessed | tf_op | source)
XLA Modules:
  0.0 35.6 jit_solution(10617036718227603212)
XLA Ops:
  0.6 0.0 copy-start.1
  0.6 0.0 copy-start.2
  0.7 0.0 copy-start.3
  0.7 5.1 %collective-permute-start = (f32[256,128]{1,0:T(8,128)}, f32[256,128]{1,0:T(8,128)S(1)}, u32[]{:S(2)}, u32[]{:S(2)}) collective-permute-start(f32[256,128]{1,0:T(8,128)} %basis_ref.1), channel_id=1, source_target_pairs={{0,12},{1,13},{2,14},{3,15},{4,8},{5,9},{6,10},{7,11},{8,4},{9,5},... | collective-permute-start | bytes 393224 | tf_op jit(solution)/shard_map/ppermute | solution.py:188
  5.8 0.0 collective-permute-start.1
  6.5 2.5 %assemble.1 = (bf16[8,256,256]{2,1,0:T(8,128)(2,1)S(1)}, bf16[8,256,256]{2,1,0:T(8,128)(2,1)S(1)}, f32[256,128]{1,0:T(8,128)S(1)}) custom-call(s32[1]{0:T(128)S(6)} %copy.9.count_ref, s32[128]{0:T(128)S(1)} %copy-done.2, s32[128]{0:T(128)S(1)} %bitcast.9, s32[128]{0:T(128)S(1)} %copy-done.4, f32[4096,128]{1,0:T(8,128)S(1)} %bitcast.8, ...), custom_call_target="tpu_custom_call" | custom-call | flops 10000000 | bytes 8000000 | tf_op jit(solution)/shard_map/assemble/pallas_call | solution.py:205
  9.0 0.1 collective-permute-start.2
  9.1 2.0 %collective-permute-start.3 = (f32[256,128]{1,0:T(8,128)S(1)}, f32[256,128]{1,0:T(8,128)S(1)}, u32[]{:S(2)}, u32[]{:S(2)}) collective-permute-start(f32[256,128]{1,0:T(8,128)S(1)} %get-tuple-element.17.refs_0_), channel_id=1, source_target_pairs={{0,15},{1,2},{2,1},{3,4},{4,3},{5,6},{6,5},{7,8},{8,7},{9,10},{10,... | collective-permute-start | bytes 393224 | tf_op jit(solution)/shard_map/ppermute | solution.py:188
  11.1 0.0 collective-permute-done.refs_1_.first_ref
  11.1 1.2 %collective-permute-start.4 = (f32[256,128]{1,0:T(8,128)S(1)}, f32[256,128]{1,0:T(8,128)S(1)}, u32[]{:S(2)}, u32[]{:S(2)}) collective-permute-start(f32[256,128]{1,0:T(8,128)S(1)} %hand_on.1), channel_id=1, source_target_pairs={{0,4},{1,5},{2,6},{3,7},{4,0},{5,1},{6,2},{7,3},{8,12},{9,13},{10,... | collective-permute-start | bytes 393224 | tf_op jit(solution)/shard_map/ppermute | solution.py:188
  12.3 0.1 collective-permute-done.1.refs_2_.second_ref
  12.5 1.3 %collective-permute-start.5 = (f32[256,128]{1,0:T(8,128)S(1)}, f32[256,128]{1,0:T(8,128)S(1)}, u32[]{:S(2)}, u32[]{:S(2)}) collective-permute-start(f32[256,128]{1,0:T(8,128)S(1)} %get-tuple-element.19), channel_id=1, source_target_pairs={{0,7},{1,2},{2,1},{3,4},{4,3},{5,6},{6,5},{7,0},{8,15},{9,10},{10,... | collective-permute-start | bytes 393224 | tf_op jit(solution)/shard_map/ppermute | solution.py:188
  13.8 0.4 %collective-permute-start.6 = (f32[256,128]{1,0:T(8,128)S(1)}, f32[256,128]{1,0:T(8,128)S(1)}, u32[]{:S(2)}, u32[]{:S(2)}) collective-permute-start(f32[256,128]{1,0:T(8,128)S(1)} %get-tuple-element.20), channel_id=1, source_target_pairs={{0,1},{1,0},{2,3},{3,2},{4,5},{5,4},{6,7},{7,6},{8,9},{9,8},{10,11... | collective-permute-start | bytes 393224 | tf_op jit(solution)/shard_map/ppermute | solution.py:188
  14.2 0.0 collective-permute-done.2.refs_3_
  14.2 2.2 %collective-permute-done.3.refs_4_ = f32[256,128]{1,0:T(8,128)S(1)} collective-permute-done((f32[256,128]{1,0:T(8,128)S(1)}, f32[256,128]{1,0:T(8,128)S(1)}, u32[]{:S(2)}, u32[]{:S(2)}) %collective-permute-start.3) | collective-permute-done | bytes 131104 | tf_op jit(solution)/shard_map/ppermute | solution.py:188
  16.4 1.1 %project_early.1 = (f32[256,128]{1,0:T(8,128)S(1)}, f32[128,128]{1,0:T(8,128)S(1)}, bf16[3,128,256]{2,1,0:T(8,128)(2,1)S(1)}, bf16[3,128,256]{2,1,0:T(8,128)(2,1)S(1)}) custom-call(bf16[8,256,256]{2,1,0:T(8,128)(2,1)S(1)} %get-tuple-element.15.high_ref, bf16[8,256,256]{2,1,0:T(8,128)(2,1)S(1)} %get-tuple-element.16.low_ref, f32[1,256]{1,0:T(1,128)S(1)} %bitcast.10, ...), custom_call_target="tpu_custom_call" | custom-call | flops 20000000000 | bytes 2500000 | tf_op jit(solution)/shard_map/project_early/pallas_call | solution.py:252
  17.5 0.4 %collective-permute-done.4.refs_0_ = f32[256,128]{1,0:T(8,128)S(1)} collective-permute-done((f32[256,128]{1,0:T(8,128)S(1)}, f32[256,128]{1,0:T(8,128)S(1)}, u32[]{:S(2)}, u32[]{:S(2)}) %collective-permute-start.4) | collective-permute-done | bytes 131104 | tf_op jit(solution)/shard_map/ppermute | solution.py:188
  17.9 2.5 %collective-permute-done.5.refs_1_ = f32[256,128]{1,0:T(8,128)S(1)} collective-permute-done((f32[256,128]{1,0:T(8,128)S(1)}, f32[256,128]{1,0:T(8,128)S(1)}, u32[]{:S(2)}, u32[]{:S(2)}) %collective-permute-start.5) | collective-permute-done | bytes 131104 | tf_op jit(solution)/shard_map/ppermute | solution.py:188
  20.4 0.0 collective-permute-done.6.refs_2_
  20.4 0.3 reduce_late.1
  20.8 0.1 collective-permute-start.7
  20.8 1.2 %collective-permute-done.7 = f32[64,128]{1,0:T(8,128)S(1)} collective-permute-done((f32[64,128]{1,0:T(8,128)S(1)}, f32[64,128]{1,0:T(8,128)S(1)}, u32[]{:S(2)}, u32[]{:S(2)}) %collective-permute-start.7) | collective-permute-done | bytes 32800 | tf_op jit(solution)/shard_map/ppermute | solution.py:295
  22.0 0.0 collective-permute-start.8
  22.0 1.1 %project_late.1 = (f32[256,128]{1,0:T(8,128)}, f32[8,128]{1,0:T(8,128)S(1)}) custom-call(bf16[8,256,256]{2,1,0:T(8,128)(2,1)S(1)} %get-tuple-element.15.high_ref, bf16[8,256,256]{2,1,0:T(8,128)(2,1)S(1)} %get-tuple-element.16.low_ref, f32[256,128]{1,0:T(8,128)S(1)} %get-tuple-element.18.total_ref, f32[256,128]{1,0:T(8,128)S(1)} %collective-permute-done.4.refs_0_, ...), custom_call_target="tpu_custom_call" | custom-call | flops 160000000 | bytes 1500000 | tf_op jit(solution)/shard_map/project_late/pallas_call | solution.py:284
  23.2 2.2 %collective-permute-done.8.second_ref = f32[64,128]{1,0:T(8,128)S(1)} collective-permute-done((f32[64,128]{1,0:T(8,128)S(1)}, f32[64,128]{1,0:T(8,128)S(1)}, u32[]{:S(2)}, u32[]{:S(2)}) %collective-permute-start.8) | collective-permute-done | bytes 32800 | tf_op jit(solution)/shard_map/ppermute | solution.py:295
  25.4 0.1 collective-permute-start.9
  25.5 3.3 %collective-permute-done.9 = f32[64,128]{1,0:T(8,128)S(1)} collective-permute-done((f32[64,128]{1,0:T(8,128)S(1)}, f32[64,128]{1,0:T(8,128)S(1)}, u32[]{:S(2)}, u32[]{:S(2)}) %collective-permute-start.9) | collective-permute-done | bytes 32800 | tf_op jit(solution)/shard_map/ppermute | solution.py:295
  28.7 0.3 collective-permute-start.10
  29.1 4.7 %collective-permute-done.10 = f32[64,128]{1,0:T(8,128)S(1)} collective-permute-done((f32[64,128]{1,0:T(8,128)S(1)}, f32[64,128]{1,0:T(8,128)S(1)}, u32[]{:S(2)}, u32[]{:S(2)}) %collective-permute-start.10) | collective-permute-done | bytes 32800 | tf_op jit(solution)/shard_map/ppermute | solution.py:295
  33.7 0.1 collective-permute-start.11
  33.9 1.1 %collective-permute-done.11.other_ref = f32[64,128]{1,0:T(8,128)S(1)} collective-permute-done((f32[64,128]{1,0:T(8,128)S(1)}, f32[64,128]{1,0:T(8,128)S(1)}, u32[]{:S(2)}, u32[]{:S(2)}) %collective-permute-start.11) | collective-permute-done | bytes 32800 | tf_op jit(solution)/shard_map/ppermute | solution.py:295
  35.0 0.6 %join.1 = f32[128,128]{1,0:T(8,128)} custom-call(s32[1]{0:T(128)} %bitcast.5.side_ref, f32[64,128]{1,0:T(8,128)S(1)} %add.11.mine_ref, f32[64,128]{1,0:T(8,128)S(1)} %collective-permute-done.11.other_ref), custom_call_target="tpu_custom_call" | custom-call | bytes 130000 | tf_op jit(solution)/shard_map/join/pallas_call | solution.py:310
  (16 shorter events, 0.1 us)
Async XLA Ops:
  0.6 5.8 %copy-start.1 = (f32[256,128]{1,0:T(8,128)S(1)}, f32[256,128]{1,0:T(8,128)}, u32[]{:S(2)}) copy-start(f32[256,128]{1,0:T(8,128)} %basis_ref.1) | copy-start | bytes 393220
  0.6 5.8 %copy-start.2 = (s32[128]{0:T(128)S(1)}, s32[128]{0:T(128)}, u32[]{:S(2)}) copy-start(s32[128]{0:T(128)} %rows_ref.1) | copy-start | bytes 1540
  0.7 5.8 %copy-start.3 = (s32[128,1]{0,1:T(1,128)S(1)}, s32[128,1]{0,1:T(1,128)}, u32[]{:S(2)}) copy-start(s32[128,1]{0,1:T(1,128)} %param.11) | copy-start | bytes 1540
  0.7 5.8 %copy-start.4 = (s32[128]{0:T(128)S(1)}, s32[128]{0:T(128)}, u32[]{:S(2)}) copy-start(s32[128]{0:T(128)} %offset_ref.1) | copy-start | bytes 1540
  0.7 5.8 %copy-start = (f32[128,4096]{1,0:T(8,128)S(1)}, f32[128,4096]{1,0:T(8,128)}, u32[]{:S(2)}) copy-start(f32[128,4096]{1,0:T(8,128)} %param.9) | copy-start | bytes 6291460
  0.7 10.4 %collective-permute-start = (f32[256,128]{1,0:T(8,128)}, f32[256,128]{1,0:T(8,128)S(1)}, u32[]{:S(2)}, u32[]{:S(2)}) collective-permute-start(f32[256,128]{1,0:T(8,128)} %basis_ref.1), channel_id=1, source_target_pairs={{0,12},{1,13},{2,14},{3,15},{4,8},{5,9},{6,10},{7,11},{8,4},{9,5},... | collective-permute-start | bytes 393224 | tf_op jit(solution)/shard_map/ppermute | solution.py:188
  5.8 6.6 %collective-permute-start.1 = (f32[256,128]{1,0:T(8,128)}, f32[256,128]{1,0:T(8,128)S(1)}, u32[]{:S(2)}, u32[]{:S(2)}) collective-permute-start(f32[256,128]{1,0:T(8,128)} %basis_ref.1), channel_id=1, source_target_pairs={{0,4},{1,5},{2,6},{3,7},{4,0},{5,1},{6,2},{7,3},{8,12},{9,13},{10,... | collective-permute-start | bytes 393224 | tf_op jit(solution)/shard_map/ppermute | solution.py:188
  9.0 5.2 %collective-permute-start.2 = (f32[256,128]{1,0:T(8,128)S(1)}, f32[256,128]{1,0:T(8,128)S(1)}, u32[]{:S(2)}, u32[]{:S(2)}) collective-permute-start(f32[256,128]{1,0:T(8,128)S(1)} %get-tuple-element.17.refs_0_), channel_id=1, source_target_pairs={{0,1},{1,0},{2,3},{3,2},{4,5},{5,4},{6,7},{7,6},{8,9},{9,8},{10,11... | collective-permute-start | bytes 393224 | tf_op jit(solution)/shard_map/ppermute | solution.py:188
  9.1 7.3 %collective-permute-start.3 = (f32[256,128]{1,0:T(8,128)S(1)}, f32[256,128]{1,0:T(8,128)S(1)}, u32[]{:S(2)}, u32[]{:S(2)}) collective-permute-start(f32[256,128]{1,0:T(8,128)S(1)} %get-tuple-element.17.refs_0_), channel_id=1, source_target_pairs={{0,15},{1,2},{2,1},{3,4},{4,3},{5,6},{6,5},{7,8},{8,7},{9,10},{10,... | collective-permute-start | bytes 393224 | tf_op jit(solution)/shard_map/ppermute | solution.py:188
  11.1 5.3 %copy-start.5 = (f32[256]{0:T(256)S(1)}, f32[256]{0:T(256)}, u32[]{:S(2)}) copy-start(f32[256]{0:T(256)} %param.8) | copy-start | bytes 3076
  11.1 6.8 %collective-permute-start.4 = (f32[256,128]{1,0:T(8,128)S(1)}, f32[256,128]{1,0:T(8,128)S(1)}, u32[]{:S(2)}, u32[]{:S(2)}) collective-permute-start(f32[256,128]{1,0:T(8,128)S(1)} %hand_on.1), channel_id=1, source_target_pairs={{0,4},{1,5},{2,6},{3,7},{4,0},{5,1},{6,2},{7,3},{8,12},{9,13},{10,... | collective-permute-start | bytes 393224 | tf_op jit(solution)/shard_map/ppermute | solution.py:188
  12.5 8.0 %collective-permute-start.5 = (f32[256,128]{1,0:T(8,128)S(1)}, f32[256,128]{1,0:T(8,128)S(1)}, u32[]{:S(2)}, u32[]{:S(2)}) collective-permute-start(f32[256,128]{1,0:T(8,128)S(1)} %get-tuple-element.19), channel_id=1, source_target_pairs={{0,7},{1,2},{2,1},{3,4},{4,3},{5,6},{6,5},{7,0},{8,15},{9,10},{10,... | collective-permute-start | bytes 393224 | tf_op jit(solution)/shard_map/ppermute | solution.py:188
  13.8 6.7 %collective-permute-start.6 = (f32[256,128]{1,0:T(8,128)S(1)}, f32[256,128]{1,0:T(8,128)S(1)}, u32[]{:S(2)}, u32[]{:S(2)}) collective-permute-start(f32[256,128]{1,0:T(8,128)S(1)} %get-tuple-element.20), channel_id=1, source_target_pairs={{0,1},{1,0},{2,3},{3,2},{4,5},{5,4},{6,7},{7,6},{8,9},{9,8},{10,11... | collective-permute-start | bytes 393224 | tf_op jit(solution)/shard_map/ppermute | solution.py:188
  20.8 1.3 %collective-permute-start.7 = (f32[64,128]{1,0:T(8,128)S(1)}, f32[64,128]{1,0:T(8,128)S(1)}, u32[]{:S(2)}, u32[]{:S(2)}) collective-permute-start(f32[64,128]{1,0:T(8,128)S(1)} %get-tuple-element.26), channel_id=1, source_target_pairs={{0,1},{1,0},{2,3},{3,2},{4,5},{5,4},{6,7},{7,6},{8,9},{9,8},{10,11... | collective-permute-start | bytes 98312 | tf_op jit(solution)/shard_map/ppermute | solution.py:295
  22.0 3.3 %collective-permute-start.8 = (f32[64,128]{1,0:T(8,128)S(1)}, f32[64,128]{1,0:T(8,128)S(1)}, u32[]{:S(2)}, u32[]{:S(2)}) collective-permute-start(f32[64,128]{1,0:T(8,128)S(1)} %add.9.first_ref), channel_id=1, source_target_pairs={{0,3},{1,2},{2,1},{3,0},{4,7},{5,6},{6,5},{7,4},{8,11},{9,10},{10,... | collective-permute-start | bytes 98312 | tf_op jit(solution)/shard_map/ppermute | solution.py:295
  25.4 3.3 %collective-permute-start.9 = (f32[64,128]{1,0:T(8,128)S(1)}, f32[64,128]{1,0:T(8,128)S(1)}, u32[]{:S(2)}, u32[]{:S(2)}) collective-permute-start(f32[64,128]{1,0:T(8,128)S(1)} %add_after.1), channel_id=1, source_target_pairs={{0,5},{1,4},{2,7},{3,6},{4,1},{5,0},{6,3},{7,2},{8,13},{9,12},{10,... | collective-permute-start | bytes 98312 | tf_op jit(solution)/shard_map/ppermute | solution.py:295
  28.7 5.0 %collective-permute-start.10 = (f32[64,128]{1,0:T(8,128)S(1)}, f32[64,128]{1,0:T(8,128)S(1)}, u32[]{:S(2)}, u32[]{:S(2)}) collective-permute-start(f32[64,128]{1,0:T(8,128)S(1)} %add.10), channel_id=1, source_target_pairs={{0,9},{1,8},{2,11},{3,10},{4,13},{5,12},{6,15},{7,14},{8,1},{9,0},... | collective-permute-start | bytes 98312 | tf_op jit(solution)/shard_map/ppermute | solution.py:295
  33.7 1.2 %collective-permute-start.11 = (f32[64,128]{1,0:T(8,128)S(1)}, f32[64,128]{1,0:T(8,128)S(1)}, u32[]{:S(2)}, u32[]{:S(2)}) collective-permute-start(f32[64,128]{1,0:T(8,128)S(1)} %add.11.mine_ref), channel_id=1, source_target_pairs={{0,1},{1,0},{2,3},{3,2},{4,5},{5,4},{6,7},{7,6},{8,9},{9,8},{10,11... | collective-permute-start | bytes 98312 | tf_op jit(solution)/shard_map/ppermute | solution.py:295

commit v13 on v10

--- a/solution.py
+++ b/solution.py
@@ -37,7 +37,7 @@
     token_ref[...] = jnp.zeros_like(token_ref)
 
 
-def assemble(count_ref, rows_ref, owner_ref, offset_ref, blocks_ref, basis_ref, token_ref, high_ref, low_ref, held_ref, dense, placed, place, arrived):
+def assemble(count_ref, rows_ref, owner_ref, offset_ref, blocks_ref, token_ref, high_ref, low_ref, dense, placed, place, arrived):
     n, me = lax.axis_size("row"), lax.axis_index("row")
     away = lax.rem(owner_ref[...].reshape(1, CAP) - me + n, n)
     link = jnp.zeros_like(away)
@@ -49,7 +49,6 @@
     copy = pltpu.make_async_copy(placed, place, arrived)
     copy.start()
     dense[...] = jnp.zeros_like(dense)
-    held_ref[...] = basis_ref[...]
     copy.wait()
 
     @pl.loop(0, CAP // 8)
@@ -198,16 +197,16 @@
 
     first = trade(basis, inner)
     second = trade(basis, outer)
+    beside, beyond = trade(basis, near), trade(basis, next_chip)
     blocks = tangent_blocks.reshape(CAP // 8, 8, HALF, 128).transpose(0, 2, 1, 3).reshape(CAP * HALF, 128)
-    high, low, held = pl.pallas_call(
+    high, low = pl.pallas_call(
         assemble,
         out_shape=(
             jax.ShapeDtypeStruct((LINKS, ROWS, ROWS), half),
             jax.ShapeDtypeStruct((LINKS, ROWS, ROWS), half),
-            jax.ShapeDtypeStruct((ROWS, MODES), full),
         ),
-        in_specs=[smem] + [vmem] * 6,
-        out_specs=(vmem,) * 3,
+        in_specs=[smem] + [vmem] * 5,
+        out_specs=(vmem,) * 2,
         scratch_shapes=[
             pltpu.VMEM(((CAP + 1) * HALF, 128), full),
             pltpu.VMEM((1, CAP), jnp.int32),
@@ -217,8 +216,7 @@
         compiler_params=params,
         cost_estimate=pl.CostEstimate(flops=10_000_000, bytes_accessed=8_000_000, transcendentals=0),
         name="assemble",
-    )(tile_count, tile_rows, tile_owner[:, 0], tile_offset, blocks, basis, token)
-    beside, beyond = trade(held, near), trade(held, next_chip)
+    )(tile_count, tile_rows, tile_owner[:, 0], tile_offset, blocks, token)
 
     next_sent, outer_sent, near_sent = pl.pallas_call(
         functools.partial(pick, n == 16),
@@ -233,7 +231,7 @@
         across = trade(outer_sent, outer)
         far_next = trade(next_sent, lambda d: {0: 7, 7: 0, 8: 15, 15: 8}.get(d, next_chip(d)))
     else:
-        across = trade(held, lambda d: d + n // 2)
+        across = trade(basis, lambda d: d + n // 2)
         far_next = trade(next_sent, next_chip)
     far_near = trade(near_sent, near)
 
@@ -251,7 +249,7 @@
         compiler_params=params,
         cost_estimate=pl.CostEstimate(flops=20_000_000_000, bytes_accessed=2_500_000, transcendentals=0),
         name="project_early",
-    )(high, low, springs.reshape(1, ROWS), held, first, second, beside, beyond)
+    )(high, low, springs.reshape(1, ROWS), basis, first, second, beside, beyond)
 
     side = me
     for shift in (8, 4, 2, 1):

time: 35.5 us -> 36.2 us (1.020)
  waiting for transfers between devices: 15.8 us -> 17.2 us
  starting transfers between devices: 12.4 us -> 11.5 us
    ppermute x5, waiting for transfers between devices: 10.7 us -> 12.6 us  [swap(): return lax.ppermute(block, 'row', [(d, d ^ apart) for d in range(n)])]
    ppermute x5, starting transfers between devices: 2.14 us -> 0.2 us  [swap(): return lax.ppermute(block, 'row', [(d, d ^ apart) for d in range(n)])]
    ppermute x7, starting transfers between devices: 10.3 us -> 11.3 us  [trade(): return lax.ppermute(block, 'row', [(d, partner(d) % n) for d in range(n)])]
    ppermute x7, waiting for transfers between devices: 5.13 us -> 4.57 us  [trade(): return lax.ppermute(block, 'row', [(d, partner(d) % n) for d in range(n)])]
  transfers between devices with their start and end apart: 12 -> 12, of which waited for: 9 -> 8; matrix products, arithmetic and copies ran while one was open for 0% -> 0% of each run, Pallas kernels for 13% -> 13%
where the time goes in v13:
time: 36.2 us; the launch traced here: 36 us
  waiting for transfers between devices  17.2 us (48%)
  starting transfers between devices  11.5 us (32%)
  Pallas kernels  5.81 us (16%)
  between operations  1.47 us (4%)
    ppermute x5, waiting for transfers between devices, swap(): return lax.ppermute(block, 'row', [(d, d ^ apart) for d in range(n)])  12.6 us
    ppermute x7, starting transfers between devices, trade(): return lax.ppermute(block, 'row', [(d, partner(d) % n) for d in range(n)])  11.3 us
    ppermute x7, waiting for transfers between devices, trade(): return lax.ppermute(block, 'row', [(d, partner(d) % n) for d in range(n)])  4.57 us
    pallas_call x1, Pallas kernels, shards(): pl.pallas_call(assemble, out_shape=(jax.ShapeDtypeStruct((LINKS, ROWS, RO...  2.58 us
    pallas_call x1, Pallas kernels, shards(): pl.pallas_call(project_late, out_shape=(jax.ShapeDtypeStruct((ROWS, MODES...  1.12 us
    pallas_call x1, Pallas kernels, shards(): pl.pallas_call(project_early, out_shape=(jax.ShapeDtypeStruct((ROWS, MODE...  1.12 us
  transfers between devices with their start and end apart: 12, of which 8 were waited for; matrix products, arithmetic and copies ran while one was open for 0% of the time, Pallas kernels for 13%

profile of v13, /device:TPU:0, one launch (start us, length us, event | category | flops | bytes accessed | tf_op | source)
XLA Modules:
  0.0 36.0 jit_solution(11690878034461744971)
XLA Ops:
  0.7 5.1 %collective-permute-start = (f32[256,128]{1,0:T(8,128)}, f32[256,128]{1,0:T(8,128)S(1)}, u32[]{:S(2)}, u32[]{:S(2)}) collective-permute-start(f32[256,128]{1,0:T(8,128)} %refs_0_.1), channel_id=1, source_target_pairs={{0,12},{1,13},{2,14},{3,15},{4,8},{5,9},{6,10},{7,11},{8,4},{9,5},... | collective-permute-start | bytes 393224 | tf_op jit(solution)/shard_map/ppermute | solution.py:184
  5.8 0.0 collective-permute-start.1
  5.8 0.0 collective-permute-start.2
  5.8 2.0 %collective-permute-start.3 = (f32[256,128]{1,0:T(8,128)}, f32[256,128]{1,0:T(8,128)S(1)}, u32[]{:S(2)}, u32[]{:S(2)}) collective-permute-start(f32[256,128]{1,0:T(8,128)} %refs_0_.1), channel_id=1, source_target_pairs={{0,15},{1,2},{2,1},{3,4},{4,3},{5,6},{6,5},{7,8},{8,7},{9,10},{10,... | collective-permute-start | bytes 393224 | tf_op jit(solution)/shard_map/ppermute | solution.py:184
  8.5 0.0 copy-done.1
  8.5 0.0 copy-done.2
  8.5 0.0 copy-done.3
  8.5 2.6 %assemble.1 = (bf16[8,256,256]{2,1,0:T(8,128)(2,1)S(1)}, bf16[8,256,256]{2,1,0:T(8,128)(2,1)S(1)}) custom-call(s32[1]{0:T(128)S(6)} %copy.9.count_ref, s32[128]{0:T(128)S(1)} %copy-done.1, s32[128]{0:T(128)S(1)} %bitcast.9, s32[128]{0:T(128)S(1)} %copy-done.3, f32[4096,128]{1,0:T(8,128)S(1)} %bitcast.8, f32[8,128]{1,0:T(8,128)S(1)} %prepare.1.token_ref), custom_call_target="tpu_custom_call" | custom-call | flops 10000000 | bytes 8000000 | tf_op jit(solution)/shard_map/assemble/pallas_call | solution.py:202
  11.1 0.0 collective-permute-done.refs_1_.first_ref
  11.1 1.3 %collective-permute-done.1.refs_2_.second_ref = f32[256,128]{1,0:T(8,128)S(1)} collective-permute-done((f32[256,128]{1,0:T(8,128)}, f32[256,128]{1,0:T(8,128)S(1)}, u32[]{:S(2)}, u32[]{:S(2)}) %collective-permute-start.1) | collective-permute-done | bytes 131104 | tf_op jit(solution)/shard_map/ppermute | solution.py:184
  12.5 1.3 %collective-permute-start.4 = (f32[256,128]{1,0:T(8,128)S(1)}, f32[256,128]{1,0:T(8,128)S(1)}, u32[]{:S(2)}, u32[]{:S(2)}) collective-permute-start(f32[256,128]{1,0:T(8,128)S(1)} %get-tuple-element.18), channel_id=1, source_target_pairs={{0,7},{1,2},{2,1},{3,4},{4,3},{5,6},{6,5},{7,0},{8,15},{9,10},{10,... | collective-permute-start | bytes 393224 | tf_op jit(solution)/shard_map/ppermute | solution.py:184
  13.8 1.5 %collective-permute-start.5 = (f32[256,128]{1,0:T(8,128)S(1)}, f32[256,128]{1,0:T(8,128)S(1)}, u32[]{:S(2)}, u32[]{:S(2)}) collective-permute-start(f32[256,128]{1,0:T(8,128)S(1)} %get-tuple-element.19), channel_id=1, source_target_pairs={{0,4},{1,5},{2,6},{3,7},{4,0},{5,1},{6,2},{7,3},{8,12},{9,13},{10,... | collective-permute-start | bytes 393224 | tf_op jit(solution)/shard_map/ppermute | solution.py:184
  15.3 1.4 %collective-permute-start.6 = (f32[256,128]{1,0:T(8,128)S(1)}, f32[256,128]{1,0:T(8,128)S(1)}, u32[]{:S(2)}, u32[]{:S(2)}) collective-permute-start(f32[256,128]{1,0:T(8,128)S(1)} %get-tuple-element.20), channel_id=1, source_target_pairs={{0,1},{1,0},{2,3},{3,2},{4,5},{5,4},{6,7},{7,6},{8,9},{9,8},{10,11... | collective-permute-start | bytes 393224 | tf_op jit(solution)/shard_map/ppermute | solution.py:184
  16.7 0.0 collective-permute-done.2.refs_3_
  16.7 0.0 collective-permute-done.3.refs_4_
  16.7 1.1 %project_early.1 = (f32[256,128]{1,0:T(8,128)S(1)}, f32[128,128]{1,0:T(8,128)S(1)}, bf16[3,128,256]{2,1,0:T(8,128)(2,1)S(1)}, bf16[3,128,256]{2,1,0:T(8,128)(2,1)S(1)}) custom-call(bf16[8,256,256]{2,1,0:T(8,128)(2,1)S(1)} %get-tuple-element.15.high_ref, bf16[8,256,256]{2,1,0:T(8,128)(2,1)S(1)} %get-tuple-element.16.low_ref, f32[1,256]{1,0:T(1,128)S(1)} %bitcast.10, ...), custom_call_target="tpu_custom_call" | custom-call | flops 20000000000 | bytes 2500000 | tf_op jit(solution)/shard_map/project_early/pallas_call | solution.py:238
  17.8 0.1 collective-permute-done.4.refs_0_
  17.9 3.1 %collective-permute-done.5.refs_1_ = f32[256,128]{1,0:T(8,128)S(1)} collective-permute-done((f32[256,128]{1,0:T(8,128)S(1)}, f32[256,128]{1,0:T(8,128)S(1)}, u32[]{:S(2)}, u32[]{:S(2)}) %collective-permute-start.5) | collective-permute-done | bytes 131104 | tf_op jit(solution)/shard_map/ppermute | solution.py:184
  21.0 0.0 collective-permute-done.6.refs_2_
  21.0 0.3 reduce_late.1
  21.4 0.1 collective-permute-start.7
  21.5 1.2 %collective-permute-done.7 = f32[64,128]{1,0:T(8,128)S(1)} collective-permute-done((f32[64,128]{1,0:T(8,128)S(1)}, f32[64,128]{1,0:T(8,128)S(1)}, u32[]{:S(2)}, u32[]{:S(2)}) %collective-permute-start.7) | collective-permute-done | bytes 32800 | tf_op jit(solution)/shard_map/ppermute | solution.py:281
  22.7 0.0 collective-permute-start.8
  22.7 1.1 %project_late.1 = (f32[256,128]{1,0:T(8,128)}, f32[8,128]{1,0:T(8,128)S(1)}) custom-call(bf16[8,256,256]{2,1,0:T(8,128)(2,1)S(1)} %get-tuple-element.15.high_ref, bf16[8,256,256]{2,1,0:T(8,128)(2,1)S(1)} %get-tuple-element.16.low_ref, f32[256,128]{1,0:T(8,128)S(1)} %get-tuple-element.17.total_ref, f32[256,128]{1,0:T(8,128)S(1)} %collective-permute-done.4.refs_0_, ...), custom_call_target="tpu_custom_call" | custom-call | flops 160000000 | bytes 1500000 | tf_op jit(solution)/shard_map/project_late/pallas_call | solution.py:270
  23.8 2.2 %collective-permute-done.8.second_ref = f32[64,128]{1,0:T(8,128)S(1)} collective-permute-done((f32[64,128]{1,0:T(8,128)S(1)}, f32[64,128]{1,0:T(8,128)S(1)}, u32[]{:S(2)}, u32[]{:S(2)}) %collective-permute-start.8) | collective-permute-done | bytes 32800 | tf_op jit(solution)/shard_map/ppermute | solution.py:281
  26.0 0.0 collective-permute-start.9
  26.0 3.3 %collective-permute-done.9 = f32[64,128]{1,0:T(8,128)S(1)} collective-permute-done((f32[64,128]{1,0:T(8,128)S(1)}, f32[64,128]{1,0:T(8,128)S(1)}, u32[]{:S(2)}, u32[]{:S(2)}) %collective-permute-start.9) | collective-permute-done | bytes 32800 | tf_op jit(solution)/shard_map/ppermute | solution.py:281
  29.4 0.0 collective-permute-start.10
  29.4 4.8 %collective-permute-done.10 = f32[64,128]{1,0:T(8,128)S(1)} collective-permute-done((f32[64,128]{1,0:T(8,128)S(1)}, f32[64,128]{1,0:T(8,128)S(1)}, u32[]{:S(2)}, u32[]{:S(2)}) %collective-permute-start.10) | collective-permute-done | bytes 32800 | tf_op jit(solution)/shard_map/ppermute | solution.py:281
  34.2 0.1 collective-permute-start.11
  34.3 1.1 %collective-permute-done.11.other_ref = f32[64,128]{1,0:T(8,128)S(1)} collective-permute-done((f32[64,128]{1,0:T(8,128)S(1)}, f32[64,128]{1,0:T(8,128)S(1)}, u32[]{:S(2)}, u32[]{:S(2)}) %collective-permute-start.11) | collective-permute-done | bytes 32800 | tf_op jit(solution)/shard_map/ppermute | solution.py:281
  35.4 0.6 %join.1 = f32[128,128]{1,0:T(8,128)} custom-call(s32[1]{0:T(128)} %bitcast.5.side_ref, f32[64,128]{1,0:T(8,128)S(1)} %add.11.mine_ref, f32[64,128]{1,0:T(8,128)S(1)} %collective-permute-done.11.other_ref), custom_call_target="tpu_custom_call" | custom-call | bytes 130000 | tf_op jit(solution)/shard_map/join/pallas_call | solution.py:296
  (15 shorter events, 0.1 us)
Async XLA Ops:
  0.6 7.8 %copy-start.1 = (s32[128]{0:T(128)S(1)}, s32[128]{0:T(128)}, u32[]{:S(2)}) copy-start(s32[128]{0:T(128)} %rows_ref.1) | copy-start | bytes 1540
  0.6 7.8 %copy-start.2 = (s32[128,1]{0,1:T(1,128)S(1)}, s32[128,1]{0,1:T(1,128)}, u32[]{:S(2)}) copy-start(s32[128,1]{0,1:T(1,128)} %param.11) | copy-start | bytes 1540
  0.7 7.8 %copy-start.3 = (s32[128]{0:T(128)S(1)}, s32[128]{0:T(128)}, u32[]{:S(2)}) copy-start(s32[128]{0:T(128)} %offset_ref.1) | copy-start | bytes 1540
  0.7 7.8 %copy-start = (f32[128,4096]{1,0:T(8,128)S(1)}, f32[128,4096]{1,0:T(8,128)}, u32[]{:S(2)}) copy-start(f32[128,4096]{1,0:T(8,128)} %param.9) | copy-start | bytes 6291460
  0.7 10.4 %collective-permute-start = (f32[256,128]{1,0:T(8,128)}, f32[256,128]{1,0:T(8,128)S(1)}, u32[]{:S(2)}, u32[]{:S(2)}) collective-permute-start(f32[256,128]{1,0:T(8,128)} %refs_0_.1), channel_id=1, source_target_pairs={{0,12},{1,13},{2,14},{3,15},{4,8},{5,9},{6,10},{7,11},{8,4},{9,5},... | collective-permute-start | bytes 393224 | tf_op jit(solution)/shard_map/ppermute | solution.py:184
  5.8 6.6 %collective-permute-start.1 = (f32[256,128]{1,0:T(8,128)}, f32[256,128]{1,0:T(8,128)S(1)}, u32[]{:S(2)}, u32[]{:S(2)}) collective-permute-start(f32[256,128]{1,0:T(8,128)} %refs_0_.1), channel_id=1, source_target_pairs={{0,4},{1,5},{2,6},{3,7},{4,0},{5,1},{6,2},{7,3},{8,12},{9,13},{10,... | collective-permute-start | bytes 393224 | tf_op jit(solution)/shard_map/ppermute | solution.py:184
  5.8 10.9 %collective-permute-start.2 = (f32[256,128]{1,0:T(8,128)}, f32[256,128]{1,0:T(8,128)S(1)}, u32[]{:S(2)}, u32[]{:S(2)}) collective-permute-start(f32[256,128]{1,0:T(8,128)} %refs_0_.1), channel_id=1, source_target_pairs={{0,1},{1,0},{2,3},{3,2},{4,5},{5,4},{6,7},{7,6},{8,9},{9,8},{10,11... | collective-permute-start | bytes 393224 | tf_op jit(solution)/shard_map/ppermute | solution.py:184
  5.8 10.9 %collective-permute-start.3 = (f32[256,128]{1,0:T(8,128)}, f32[256,128]{1,0:T(8,128)S(1)}, u32[]{:S(2)}, u32[]{:S(2)}) collective-permute-start(f32[256,128]{1,0:T(8,128)} %refs_0_.1), channel_id=1, source_target_pairs={{0,15},{1,2},{2,1},{3,4},{4,3},{5,6},{6,5},{7,8},{8,7},{9,10},{10,... | collective-permute-start | bytes 393224 | tf_op jit(solution)/shard_map/ppermute | solution.py:184
  7.8 8.9 %copy-start.4 = (f32[256,128]{1,0:T(8,128)S(1)}, f32[256,128]{1,0:T(8,128)}, u32[]{:S(2)}) copy-start(f32[256,128]{1,0:T(8,128)} %refs_0_.1) | copy-start | bytes 393220
  7.8 8.9 %copy-start.5 = (f32[256]{0:T(256)S(1)}, f32[256]{0:T(256)}, u32[]{:S(2)}) copy-start(f32[256]{0:T(256)} %param.8) | copy-start | bytes 3076
  12.5 5.5 %collective-permute-start.4 = (f32[256,128]{1,0:T(8,128)S(1)}, f32[256,128]{1,0:T(8,128)S(1)}, u32[]{:S(2)}, u32[]{:S(2)}) collective-permute-start(f32[256,128]{1,0:T(8,128)S(1)} %get-tuple-element.18), channel_id=1, source_target_pairs={{0,7},{1,2},{2,1},{3,4},{4,3},{5,6},{6,5},{7,0},{8,15},{9,10},{10,... | collective-permute-start | bytes 393224 | tf_op jit(solution)/shard_map/ppermute | solution.py:184
  13.8 7.3 %collective-permute-start.5 = (f32[256,128]{1,0:T(8,128)S(1)}, f32[256,128]{1,0:T(8,128)S(1)}, u32[]{:S(2)}, u32[]{:S(2)}) collective-permute-start(f32[256,128]{1,0:T(8,128)S(1)} %get-tuple-element.19), channel_id=1, source_target_pairs={{0,4},{1,5},{2,6},{3,7},{4,0},{5,1},{6,2},{7,3},{8,12},{9,13},{10,... | collective-permute-start | bytes 393224 | tf_op jit(solution)/shard_map/ppermute | solution.py:184
  15.3 5.8 %collective-permute-start.6 = (f32[256,128]{1,0:T(8,128)S(1)}, f32[256,128]{1,0:T(8,128)S(1)}, u32[]{:S(2)}, u32[]{:S(2)}) collective-permute-start(f32[256,128]{1,0:T(8,128)S(1)} %get-tuple-element.20), channel_id=1, source_target_pairs={{0,1},{1,0},{2,3},{3,2},{4,5},{5,4},{6,7},{7,6},{8,9},{9,8},{10,11... | collective-permute-start | bytes 393224 | tf_op jit(solution)/shard_map/ppermute | solution.py:184
  21.4 1.3 %collective-permute-start.7 = (f32[64,128]{1,0:T(8,128)S(1)}, f32[64,128]{1,0:T(8,128)S(1)}, u32[]{:S(2)}, u32[]{:S(2)}) collective-permute-start(f32[64,128]{1,0:T(8,128)S(1)} %get-tuple-element.26), channel_id=1, source_target_pairs={{0,1},{1,0},{2,3},{3,2},{4,5},{5,4},{6,7},{7,6},{8,9},{9,8},{10,11... | collective-permute-start | bytes 98312 | tf_op jit(solution)/shard_map/ppermute | solution.py:281
  22.7 3.3 %collective-permute-start.8 = (f32[64,128]{1,0:T(8,128)S(1)}, f32[64,128]{1,0:T(8,128)S(1)}, u32[]{:S(2)}, u32[]{:S(2)}) collective-permute-start(f32[64,128]{1,0:T(8,128)S(1)} %add.9.first_ref), channel_id=1, source_target_pairs={{0,3},{1,2},{2,1},{3,0},{4,7},{5,6},{6,5},{7,4},{8,11},{9,10},{10,... | collective-permute-start | bytes 98312 | tf_op jit(solution)/shard_map/ppermute | solution.py:281
  26.0 3.3 %collective-permute-start.9 = (f32[64,128]{1,0:T(8,128)S(1)}, f32[64,128]{1,0:T(8,128)S(1)}, u32[]{:S(2)}, u32[]{:S(2)}) collective-permute-start(f32[64,128]{1,0:T(8,128)S(1)} %add_after.1), channel_id=1, source_target_pairs={{0,5},{1,4},{2,7},{3,6},{4,1},{5,0},{6,3},{7,2},{8,13},{9,12},{10,... | collective-permute-start | bytes 98312 | tf_op jit(solution)/shard_map/ppermute | solution.py:281
  29.4 4.8 %collective-permute-start.10 = (f32[64,128]{1,0:T(8,128)S(1)}, f32[64,128]{1,0:T(8,128)S(1)}, u32[]{:S(2)}, u32[]{:S(2)}) collective-permute-start(f32[64,128]{1,0:T(8,128)S(1)} %add.10), channel_id=1, source_target_pairs={{0,9},{1,8},{2,11},{3,10},{4,13},{5,12},{6,15},{7,14},{8,1},{9,0},... | collective-permute-start | bytes 98312 | tf_op jit(solution)/shard_map/ppermute | solution.py:281
  34.2 1.2 %collective-permute-start.11 = (f32[64,128]{1,0:T(8,128)S(1)}, f32[64,128]{1,0:T(8,128)S(1)}, u32[]{:S(2)}, u32[]{:S(2)}) collective-permute-start(f32[64,128]{1,0:T(8,128)S(1)} %add.11.mine_ref), channel_id=1, source_target_pairs={{0,1},{1,0},{2,3},{3,2},{4,5},{5,4},{6,7},{7,6},{8,9},{9,8},{10,11... | collective-permute-start | bytes 98312 | tf_op jit(solution)/shard_map/ppermute | solution.py:281
